TPU v7x, 32 devices: a whole 2x2x4 slice. The times are simulated.
32 devices in a mesh: dp: 4 (over x, core), ep: 2 (over y), cp: 4 (over z).
Axes of the slice: x: 2, y: 2, z: 4, core: 2. Of those that a mesh axis runs over, the one named last changes fastest.
Arguments:
- tokens: bfloat16 [1024, 16, 1024], P('cp', ('dp', 'ep')), may hold values from -6 to 6
- lengths: int32 [16], P(('dp', 'ep')), may hold values from 256 to 1024, as said below
- expert_ids: int32 [1024, 16, 2], P('cp', ('dp', 'ep')), may hold values from 0 to 3, as said below
- places: int32 [1024, 16, 2], P('cp', ('dp', 'ep')), may hold values from -1 to 319, as said below
- buckets: int32 [1024], replicated, may hold values from 0 to 31, as said below
- w_attn: bfloat16 [1024, 4096], replicated
- bias_table: float32 [16, 32], replicated, may hold values from -4 to 4
- norm1_gain: float32 [1024], replicated, may hold values from 0.5 to 1.5
- norm2_gain: float32 [1024], replicated, may hold values from 0.5 to 1.5
- w_router: bfloat16 [1024, 4], replicated, may hold values from -0.125 to 0.125
- w_gate: bfloat16 [4, 1024, 2816], P('ep'), may hold values from -0.1875 to 0.1875
- w_up: bfloat16 [4, 1024, 2816], P('ep'), may hold values from -0.1875 to 0.1875
- w_down: bfloat16 [4, 1024, 2816], P('ep'), may hold values from -1.25 to 1.25
- cotangent: bfloat16 [1024, 16, 1024], P('cp', ('dp', 'ep')), may hold values from -6 to 6
Outputs:
- mixed: bfloat16 [1024, 16, 1024], P('cp', ('dp', 'ep'))
- tokens_grad: bfloat16 [1024, 16, 1024], P('cp', ('dp', 'ep'))
- w_attn_grad: float32 [1024, 4096], P(None, ('dp', 'ep', 'cp'))
- bias_table_grad: float32 [16, 32], replicated
- norm1_gain_grad: float32 [1024], replicated
- norm2_gain_grad: float32 [1024], replicated
- w_router_grad: float32 [1024, 4], replicated
- w_gate_grad: float32 [4, 1024, 2816], P('ep', None, ('dp', 'cp'))
- w_up_grad: float32 [4, 1024, 2816], P('ep', None, ('dp', 'cp'))
- w_down_grad: float32 [4, 1024, 2816], P('ep', None, ('dp', 'cp'))
Inputs may be any that keep to these rules, and one draw needn't show every extreme that they name: `lengths`: in each group of 2 slots held by one index of dp+ep, one slot has length 1024. `expert_ids`: the 2 experts of a token differ. -1 for padding positions and for choices beyond an expert's places; within the rows of one device the routed choices of one expert have distinct places. `buckets`: Non-decreasing in the distance, 0 at distance 0.
All inputs are finite; a program needn't handle non-finite values.
Results may differ from a plain program's by a relative error of at most 0.02.
Values may be sent and summed in bfloat16 or wider, within the bound.
A program may use at most 320 MiB of HBM per device.

v0:
```python
import jax
import jax.numpy as jnp
from jax import lax
from jax.sharding import PartitionSpec as P

epsilon = 1e-06
masked_value = -1000000000.0


def gelu_tanh(values):
    return jax.nn.gelu(values, approximate=True)


def root_scale(values):
    return lax.rsqrt(jnp.mean(values * values, axis=-1, keepdims=True) + epsilon)


def norm_back(grad_in, values, scale_rows, gain_vector):
    scaled = grad_in * gain_vector
    inner_mean = jnp.mean(scaled * values, axis=-1, keepdims=True)
    return scale_rows * (scaled - values * scale_rows * scale_rows * inner_mean)


def block_logits(
    queries, key_rows, key_start, query_pos, lengths, table_step, rise_points, head_scale
):
    key_count = key_rows.shape[0]
    key_pos = key_start + jnp.arange(key_count, dtype=jnp.int32)
    scores = (
        jnp.einsum("qshd,kshd->shqk", queries, key_rows, preferred_element_type=jnp.float32)
        * head_scale
    )
    distance = query_pos[:, None] - key_pos[None, :]
    steps = (distance[:, :, None] >= rise_points[None, None, :]).astype(jnp.float32)
    pair_bias = jnp.einsum("hb,qkb->hqk", table_step, steps, precision=lax.Precision.HIGHEST)
    allowed = (distance >= 0)[None, :, :] & (key_pos[None, None, :] < lengths[:, None, None])
    logits = jnp.where(allowed[:, None], scores + pair_bias[None], masked_value)
    return (logits, steps)


def on_device(
    tokens,
    lengths,
    expert_ids,
    places,
    buckets,
    w_attn,
    bias_table,
    norm1_gain,
    norm2_gain,
    w_router,
    w_gate,
    w_up,
    w_down,
    cotangent,
):
    span_rows, pair_count, model_width = tokens.shape
    head_count, bucket_count = bias_table.shape
    head_size = model_width // head_count
    head_scale = head_size ** (-0.5)
    n_cp = lax.axis_size("cp")
    n_ep = lax.axis_size("ep")
    seq_len = span_rows * n_cp
    row_count = span_rows * pair_count
    top_count = expert_ids.shape[2]
    experts = w_router.shape[1]
    exp_dev = w_gate.shape[0]
    capacity = (5 * row_count * top_count + 4 * experts - 1) // (4 * experts)
    my_start = lax.axis_index("cp") * span_rows
    query_pos = my_start + jnp.arange(span_rows, dtype=jnp.int32)
    live_mask = (query_pos[:, None] < lengths[None, :]).astype(jnp.float32)
    inputs = tokens.astype(jnp.float32)
    scale_first = root_scale(inputs)
    normed_first = (inputs * scale_first * norm1_gain).astype(jnp.bfloat16)
    w_qkv = w_attn[:, : 3 * model_width]
    w_out = w_attn[:, 3 * model_width :]
    qkv = jnp.einsum("csd,de->cse", normed_first, w_qkv, preferred_element_type=jnp.float32).astype(
        jnp.bfloat16
    )
    queries = qkv[..., :model_width].reshape(span_rows, pair_count, head_count, head_size)
    keyval = qkv[..., model_width:]
    keyval_all = lax.all_gather(keyval, "cp", axis=0, tiled=True)
    bucket_ids = jnp.arange(bucket_count, dtype=jnp.int32)
    rise_points = jnp.sum((buckets[:, None] < bucket_ids[None, :]).astype(jnp.int32), axis=0)
    table_step = jnp.concatenate(
        [bias_table[:, :1], bias_table[:, 1:] - bias_table[:, :-1]], axis=1
    )
    block_starts = jnp.arange(n_cp, dtype=jnp.int32) * span_rows

    def split_kv(kv_block):
        key_rows = kv_block[..., :model_width].reshape(span_rows, pair_count, head_count, head_size)
        value_rows = kv_block[..., model_width:].reshape(
            span_rows, pair_count, head_count, head_size
        )
        return (key_rows, value_rows)

    kv_blocks = keyval_all.reshape(n_cp, span_rows, pair_count, 2 * model_width)

    def max_step(state_pair, block_item):
        row_peak, row_total = state_pair
        kv_block, block_start = block_item
        key_rows, value_rows = split_kv(kv_block)
        logits, steps = block_logits(
            queries, key_rows, block_start, query_pos, lengths, table_step, rise_points, head_scale
        )
        new_peak = jnp.maximum(row_peak, jnp.max(logits, axis=-1))
        row_total = row_total * jnp.exp(row_peak - new_peak) + jnp.sum(
            jnp.exp(logits - new_peak[..., None]), axis=-1
        )
        return ((new_peak, row_total), None)

    stat_shape = (pair_count, head_count, span_rows)
    (row_peak, row_total), unused = lax.scan(
        max_step,
        (jnp.full(stat_shape, masked_value, jnp.float32), jnp.zeros(stat_shape, jnp.float32)),
        (kv_blocks, block_starts),
    )
    log_total = row_peak + jnp.log(row_total)

    def value_step(running, block_item):
        kv_block, block_start = block_item
        key_rows, value_rows = split_kv(kv_block)
        logits, steps = block_logits(
            queries, key_rows, block_start, query_pos, lengths, table_step, rise_points, head_scale
        )
        weights = jnp.exp(logits - log_total[..., None]).astype(jnp.bfloat16)
        return (
            running
            + jnp.einsum(
                "shqk,kshd->qshd", weights, value_rows, preferred_element_type=jnp.float32
            ),
            None,
        )

    attended, unused = lax.scan(
        value_step,
        jnp.zeros((span_rows, pair_count, head_count, head_size), jnp.float32),
        (kv_blocks, block_starts),
    )
    attended = attended.reshape(span_rows, pair_count, model_width)
    attended_low = attended.astype(jnp.bfloat16)
    projected = jnp.einsum("csd,de->cse", attended_low, w_out, preferred_element_type=jnp.float32)
    hidden = inputs + live_mask[..., None] * projected
    scale_second = root_scale(hidden)
    normed_second = (hidden * scale_second * norm2_gain).astype(jnp.bfloat16)
    router_logits = jnp.einsum(
        "csd,de->cse", normed_second, w_router, preferred_element_type=jnp.float32
    )
    router_probs = jax.nn.softmax(router_logits, axis=-1)
    expert_hot = (expert_ids[..., None] == jnp.arange(experts, dtype=jnp.int32)).astype(jnp.float32)
    kept_mask = (places >= 0).astype(jnp.float32)
    gate_values = jnp.sum(expert_hot * router_probs[:, :, None, :], axis=-1) * kept_mask
    target = jnp.where(places >= 0, expert_ids * capacity + places, -1).reshape(
        row_count, top_count
    )
    slot_ids = jnp.arange(experts * capacity, dtype=jnp.int32)
    route_hot = (target[None, :, :] == slot_ids[:, None, None]).astype(jnp.bfloat16)
    dispatch = jnp.sum(route_hot, axis=2)
    sent_rows = jnp.dot(
        dispatch, normed_second.reshape(row_count, model_width), preferred_element_type=jnp.float32
    )
    sent_rows = sent_rows.astype(jnp.bfloat16).reshape(n_ep, exp_dev, capacity, model_width)
    arrived = lax.all_to_all(sent_rows, "ep", split_axis=0, concat_axis=0, tiled=True)
    gate_pre = jnp.einsum("secd,edf->secf", arrived, w_gate, preferred_element_type=jnp.float32)
    up_pre = jnp.einsum("secd,edf->secf", arrived, w_up, preferred_element_type=jnp.float32)
    active, gelu_pullback = jax.vjp(gelu_tanh, gate_pre)
    inner_act = (active * up_pre).astype(jnp.bfloat16)
    produced = jnp.einsum(
        "secf,edf->secd", inner_act, w_down, preferred_element_type=jnp.float32
    ).astype(jnp.bfloat16)
    returned = lax.all_to_all(produced, "ep", split_axis=0, concat_axis=0, tiled=True).reshape(
        experts * capacity, model_width
    )
    picked = jnp.einsum("jrk,jd->rkd", route_hot, returned, preferred_element_type=jnp.float32)
    gate_flat = gate_values.reshape(row_count, top_count)
    mixed = hidden.reshape(row_count, model_width) + jnp.sum(gate_flat[..., None] * picked, axis=1)
    mixed = mixed.reshape(span_rows, pair_count, model_width).astype(jnp.bfloat16)
    grad_out = cotangent.astype(jnp.float32).reshape(row_count, model_width)
    gate_grads = jnp.sum(grad_out[:, None, :] * picked, axis=-1)
    sent_back = (gate_flat[..., None] * grad_out[:, None, :]).astype(jnp.bfloat16)
    scattered = jnp.einsum("jrk,rkd->jd", route_hot, sent_back, preferred_element_type=jnp.float32)
    scattered = scattered.astype(jnp.bfloat16).reshape(n_ep, exp_dev, capacity, model_width)
    grad_produced = lax.all_to_all(scattered, "ep", split_axis=0, concat_axis=0, tiled=True)
    down_grad = jnp.einsum(
        "secd,secf->edf", grad_produced, inner_act, preferred_element_type=jnp.float32
    )
    grad_inner = jnp.einsum(
        "secd,edf->secf", grad_produced, w_down, preferred_element_type=jnp.float32
    )
    grad_gate_pre = gelu_pullback(grad_inner * up_pre)[0].astype(jnp.bfloat16)
    grad_up_pre = (grad_inner * active).astype(jnp.bfloat16)
    gate_grad = jnp.einsum(
        "secd,secf->edf", arrived, grad_gate_pre, preferred_element_type=jnp.float32
    )
    up_grad = jnp.einsum("secd,secf->edf", arrived, grad_up_pre, preferred_element_type=jnp.float32)
    grad_arrived = jnp.einsum(
        "secf,edf->secd", grad_gate_pre, w_gate, preferred_element_type=jnp.float32
    )
    grad_arrived = (
        grad_arrived
        + jnp.einsum("secf,edf->secd", grad_up_pre, w_up, preferred_element_type=jnp.float32)
    ).astype(jnp.bfloat16)
    grad_sent = lax.all_to_all(grad_arrived, "ep", split_axis=0, concat_axis=0, tiled=True).reshape(
        experts * capacity, model_width
    )
    grad_rows = jnp.einsum("jr,jd->rd", dispatch, grad_sent, preferred_element_type=jnp.float32)
    choice_grads = gate_grads.reshape(span_rows, pair_count, top_count) * kept_mask
    prob_grads = jnp.sum(expert_hot * choice_grads[..., None], axis=2)
    logit_grads = router_probs * (
        prob_grads - jnp.sum(router_probs * prob_grads, axis=-1, keepdims=True)
    )
    logit_grads = logit_grads.astype(jnp.bfloat16)
    router_grad = jnp.einsum(
        "csd,cse->de", normed_second, logit_grads, preferred_element_type=jnp.float32
    )
    grad_normed_second = grad_rows.reshape(span_rows, pair_count, model_width)
    grad_normed_second = grad_normed_second + jnp.einsum(
        "cse,de->csd", logit_grads, w_router, preferred_element_type=jnp.float32
    )
    gain_second_grad = jnp.sum(grad_normed_second * hidden * scale_second, axis=(0, 1))
    grad_hidden = grad_out.reshape(span_rows, pair_count, model_width) + norm_back(
        grad_normed_second, hidden, scale_second, norm2_gain
    )
    grad_proj = (live_mask[..., None] * grad_hidden).astype(jnp.bfloat16)
    out_grad = jnp.einsum(
        "csd,cse->de", attended_low, grad_proj, preferred_element_type=jnp.float32
    )
    grad_att = jnp.einsum(
        "cse,de->csd", grad_proj, w_out, preferred_element_type=jnp.float32
    ).astype(jnp.bfloat16)
    grad_att_heads = grad_att.reshape(span_rows, pair_count, head_count, head_size)
    row_terms = jnp.sum(
        grad_att_heads.astype(jnp.float32)
        * attended.reshape(span_rows, pair_count, head_count, head_size),
        axis=-1,
    )
    row_terms = row_terms.transpose(1, 2, 0)
    keyval_back = lax.all_gather(keyval, "cp", axis=0, tiled=True)
    back_blocks = keyval_back.reshape(n_cp, span_rows, pair_count, 2 * model_width)

    def pair_terms(
        query_rows, grad_rows_att, row_part, total_part, key_rows, value_rows, key_start, rows_pos
    ):
        logits, steps = block_logits(
            query_rows, key_rows, key_start, rows_pos, lengths, table_step, rise_points, head_scale
        )
        weights = jnp.exp(logits - total_part[..., None])
        weight_grads = jnp.einsum(
            "qshd,kshd->shqk", grad_rows_att, value_rows, preferred_element_type=jnp.float32
        )
        score_grads = weights * (weight_grads - row_part[..., None])
        return (weights, score_grads, steps)

    def query_side_step(state_pair, kv_block, block_start):
        query_grad, step_grad = state_pair
        key_rows, value_rows = split_kv(kv_block)
        weights, score_grads, steps = pair_terms(
            queries,
            grad_att_heads,
            row_terms,
            log_total,
            key_rows,
            value_rows,
            block_start,
            query_pos,
        )
        low_grads = score_grads.astype(jnp.bfloat16)
        query_grad = (
            query_grad
            + jnp.einsum("shqk,kshd->qshd", low_grads, key_rows, preferred_element_type=jnp.float32)
            * head_scale
        )
        step_grad = step_grad + jnp.einsum(
            "hqk,qkb->hb", jnp.sum(score_grads, axis=0), steps, precision=lax.Precision.HIGHEST
        )
        return ((query_grad, step_grad), weights, low_grads)

    start_state = (
        jnp.zeros((span_rows, pair_count, head_count, head_size), jnp.float32),
        jnp.zeros((head_count, bucket_count), jnp.float32),
    )

    def grad_step(state_pair, block_item):
        kv_block, block_start = block_item
        new_state, weights, low_grads = query_side_step(state_pair, kv_block, block_start)
        value_grad = jnp.einsum(
            "shqk,qshd->kshd",
            weights.astype(jnp.bfloat16),
            grad_att_heads,
            preferred_element_type=jnp.float32,
        )
        key_grad = (
            jnp.einsum("shqk,qshd->kshd", low_grads, queries, preferred_element_type=jnp.float32)
            * head_scale
        )
        block_grad = jnp.concatenate(
            [
                key_grad.reshape(span_rows, pair_count, model_width),
                value_grad.reshape(span_rows, pair_count, model_width),
            ],
            axis=-1,
        )
        return (new_state, block_grad)

    (query_grad, step_grad), kv_terms = lax.scan(
        grad_step, start_state, (back_blocks, block_starts)
    )
    kv_terms = kv_terms.reshape(seq_len, pair_count, 2 * model_width)
    keyval_grad = lax.psum_scatter(
        kv_terms.astype(jnp.bfloat16), "cp", scatter_dimension=0, tiled=True
    )
    table_grad = step_grad - jnp.concatenate(
        [step_grad[:, 1:], jnp.zeros((head_count, 1), jnp.float32)], axis=1
    )
    qkv_grad = jnp.concatenate(
        [query_grad.reshape(span_rows, pair_count, model_width).astype(jnp.bfloat16), keyval_grad],
        axis=-1,
    )
    qkv_weight_grad = jnp.einsum(
        "csd,cse->de", normed_first, qkv_grad, preferred_element_type=jnp.float32
    )
    grad_normed_first = jnp.einsum(
        "cse,de->csd", qkv_grad, w_qkv, preferred_element_type=jnp.float32
    )
    gain_first_grad = jnp.sum(grad_normed_first * inputs * scale_first, axis=(0, 1))
    tokens_grad = (
        grad_hidden + norm_back(grad_normed_first, inputs, scale_first, norm1_gain)
    ).astype(jnp.bfloat16)
    attn_term = jnp.concatenate([qkv_weight_grad, out_grad], axis=1)
    w_attn_grad = lax.psum_scatter(attn_term, ("dp", "ep", "cp"), scatter_dimension=1, tiled=True)
    router_sum, table_sum, gain_first_sum, gain_second_sum = lax.psum(
        (router_grad, table_grad, gain_first_grad, gain_second_grad), ("dp", "ep", "cp")
    )
    gate_sum, up_sum, down_sum = (
        lax.psum_scatter(
            gate_grad.astype(jnp.bfloat16), ("dp", "cp"), scatter_dimension=2, tiled=True
        ).astype(jnp.float32),
        lax.psum_scatter(
            up_grad.astype(jnp.bfloat16), ("dp", "cp"), scatter_dimension=2, tiled=True
        ).astype(jnp.float32),
        lax.psum_scatter(
            down_grad.astype(jnp.bfloat16), ("dp", "cp"), scatter_dimension=2, tiled=True
        ).astype(jnp.float32),
    )
    return (
        mixed,
        tokens_grad,
        w_attn_grad,
        table_sum,
        gain_first_sum,
        gain_second_sum,
        router_sum,
        gate_sum,
        up_sum,
        down_sum,
    )


def solution(mesh):
    placed = (
        P("cp", ("dp", "ep"), None),
        P(("dp", "ep")),
        P("cp", ("dp", "ep"), None),
        P("cp", ("dp", "ep"), None),
        P(),
        P(),
        P(),
        P(),
        P(),
        P(),
        P("ep", None, None),
        P("ep", None, None),
        P("ep", None, None),
        P("cp", ("dp", "ep"), None),
    )
    return jax.shard_map(
        on_device,
        mesh=mesh,
        in_specs=placed,
        out_specs=(
            P("cp", ("dp", "ep"), None),
            P("cp", ("dp", "ep"), None),
            P(None, ("dp", "ep", "cp")),
            P(),
            P(),
            P(),
            P(),
            P("ep", None, ("dp", "cp")),
            P("ep", None, ("dp", "cp")),
            P("ep", None, ("dp", "cp")),
        ),
        check_vma=False,
    )
```

profile of v0, /device:TPU:0, one launch (start us, length us, event | category | flops | bytes accessed | tf_op | source)
XLA Modules:
  0.0 1769.3 jit_solution(12590671989906096099)
XLA Ops:
  8.8 6.7 fusion.102
  26.1 145.1 %all-gather.2.cloned.1.call-done = bf16[1024,2,2048]{2,0,1:T(8,128)(2,1)} async-done(((bf16[256,2,2048]{2,0,1:T(8,128)(2,1)}), bf16[1024,2,2048]{2,0,1:T(8,128)(2,1)}) %all-gather.2.cloned.1.call-update) | async-done | bytes 8388624 | tf_op jit(solution)/shard_map/all_gather | solution.py:82
  171.2 11.5 copy.158
  182.6 100.5 %while.39 = (s32[]{:T(128)}, f32[2,16,256]{2,1,0:T(8,128)S(1)}, f32[2,16,256]{2,1,0:T(8,128)S(1)}, s32[4]{0:T(128)S(1)}, s32[2]{0:T(128)S(1)}, /*index=5*/bf16[4...) while((s32[]{:T(128)}, f32[2,16,256]{2,1,0:T(8,128)S(1)}, ...), condition=%wide.region_5.6_spmd.clone, body=%wide.region_2.5_spmd.clone.sunk | while | flops 692429824 | bytes 64530744 | solution.py:113
  188.6 5.3 copy.250
  201.9 5.8 exponential_reduce_fusion.2
  213.7 5.3 copy.250
  227.0 5.8 exponential_reduce_fusion.2
  238.9 5.3 copy.250
  252.2 5.8 exponential_reduce_fusion.2
  264.0 5.3 copy.250
  277.3 5.8 exponential_reduce_fusion.2
  283.2 81.7 %while.40 = (s32[]{:T(128)}, f32[256,2,16,64]{0,3,2,1:T(8,128)}, bf16[4,256,2,2048]{1,3,2,0:T(8,128)(2,1)}, s32[4]{0:T(128)S(1)}, s32[2]{0:T(128)S(1)}, /*index=...) while((s32[]{:T(128)}, f32[256,2,16,64]{0,3,2,1:T(8,128)}, ...), condition=%wide.region_7.8_spmd.clone, body=%wide.region_6.7_spmd.clone.sunk | while | flops 953484288 | bytes 33597724 | solution.py:135
  296.5 6.8 bitcast_add_fusion.7
  309.2 5.3 copy.252
  316.3 7.4 bitcast_add_fusion.7
  329.7 5.3 copy.252
  336.9 7.4 bitcast_add_fusion.7
  357.4 7.4 bitcast_add_fusion.7
  395.3 18.4 %all-to-all-done.2 = bf16[2,2,320,1024]{3,2,1,0:T(8,128)(2,1)S(1)} async-done(((bf16[2,2,320,1024]{3,2,1,0:T(8,128)(2,1)}), bf16[2,2,320,1024]{3,2,1,0:T(8,128)(2,1)S(1)}, u32[]{:S(2)}, u32[]{:S(2)}) %all-to-all-start.2) | async-done | bytes 2621472 | tf_op jit(solution)/shard_map/all_to_all | solution.py:183
  419.0 15.8 fusion.86
  434.8 14.3 all-to-all-done
  449.1 15.9 fusion.80
  465.0 26.7 %fusion.73 = (bf16[2,2,320,2816]{3,2,0,1:T(8,128)(2,1)}, bf16[2,2,320,2816]{3,2,0,1:T(8,128)(2,1)}, bf16[2,2,320,2816]{3,2,0,1:T(8,128)(2,1)}) fusion(f32[2,2,320,2816]{3,2,1,0:T(8,128)} %fusion.80, f32[2,2,320,2816]{3,2,1,0:T(8,128)} %fusion.86, bf16[2,1024,2816]{2,1,0:T(8,128)(2,1)} %param.30, bf16[2,2,320,1024]{3,2,1,0:T(8,128)(2,1)S(1)} %all-to-all-done), kind=kOutput, calls=%fused_computation.92 | convolution fusion | flops 7475691520 | bytes 64618496 | tf_op jit(solution)/shard_map/secd,edf->secf/dot_general | solution.py:164
  491.7 12.7 convert_bitcast_fusion
  511.1 14.1 fusion.78
  525.2 13.3 fusion.106
  548.0 7.1 multiply_reduce_fusion
  555.5 19.2 %all-to-all-done.3 = bf16[2,2,320,1024]{3,2,1,0:T(8,128)(2,1)} async-done(((bf16[2,2,320,1024]{3,2,1,0:T(8,128)(2,1)}), bf16[2,2,320,1024]{3,2,1,0:T(8,128)(2,1)}, u32[]{:S(2)}, u32[]{:S(2)}) %all-to-all-start.3) | async-done | bytes 2621472 | tf_op jit(solution)/shard_map/all_to_all | solution.py:203
  597.8 251.6 %while.41 = (s32[]{:T(128)}, f32[256,2,16,64]{0,3,2,1:T(8,128)}, f32[16,32]{1,0:T(8,128)S(1)}, bf16[4,256,2,2048]{1,3,2,0:T(8,128)(2,1)}, bf16[4,256,2,2048]{1,3...) while((s32[]{:T(128)}, f32[256,2,16,64]{0,3,2,1:T(8,128)}, ...), condition=%wide.region_21.22_spmd.clone, body=%wide.region_19.21_spmd.clone.sunk | while | flops 2185037824 | bytes 161856592 | solution.py:305
  601.0 11.5 copy.255
  616.1 5.3 copy.256
  628.8 9.6 fusion.258
  639.8 7.0 fusion.260
  654.0 6.2 fusion.259
  663.2 11.5 copy.255
  678.4 5.3 copy.256
  691.1 9.6 fusion.258
  702.1 7.0 fusion.260
  716.9 6.2 fusion.259
  726.1 11.5 copy.255
  741.3 5.3 copy.256
  754.0 9.6 fusion.258
  765.0 7.0 fusion.260
  779.9 6.2 fusion.259
  789.1 11.5 copy.255
  804.3 5.3 copy.256
  816.9 9.6 fusion.258
  827.9 7.0 fusion.260
  842.8 6.2 fusion.259
  849.4 11.5 copy.177
  862.6 15.9 bitcast_convert_fusion
  880.3 15.1 bitcast_convert_fusion.2
  895.4 15.2 bitcast_convert_fusion.1
  912.9 5.6 convolution_bitcast_fusion.2
  918.5 84.3 %reduce-scatter.6.cloned.1.call-done = bf16[256,2,2048]{2,0,1:T(8,128)(2,1)} async-done(((bf16[1024,2,2048]{2,0,1:T(8,128)(2,1)}), bf16[256,2,2048]{2,0,1:T(8,128)(2,1)}) %reduce-scatter.6.cloned.1.call-update) | async-done | bytes 2097168 | tf_op jit(solution)/shard_map/reduce_scatter | solution.py:309
  1002.8 5.5 convolution_bitcast_fusion.1
  1008.3 6.3 pad_maximum_fusion
  1018.4 115.5 %reduce-scatter.14.cloned.1.call-done = bf16[2,1024,176]{1,2,0:T(8,128)(2,1)} async-done(((bf16[2,1024,2816]{1,2,0:T(8,128)(2,1)}), bf16[2,1024,176]{1,2,0:T(8,128)(2,1)}) %reduce-scatter.14.cloned.1.call-update) | async-done | bytes 720912 | tf_op jit(solution)/shard_map/reduce_scatter | solution.py:341
  1136.2 128.2 %reduce-scatter.10.cloned.1.call-done = bf16[2,1024,176]{1,2,0:T(8,128)(2,1)} async-done(((bf16[2,1024,2816]{1,2,0:T(8,128)(2,1)}), bf16[2,1024,176]{1,2,0:T(8,128)(2,1)}) %reduce-scatter.10.cloned.1.call-update) | async-done | bytes 720912 | tf_op jit(solution)/shard_map/reduce_scatter | solution.py:335
  1266.7 127.7 %reduce-scatter.12.cloned.1.call-done = bf16[2,1024,176]{1,2,0:T(8,128)(2,1)} async-done(((bf16[2,1024,2816]{1,2,0:T(8,128)(2,1)}), bf16[2,1024,176]{1,2,0:T(8,128)(2,1)}) %reduce-scatter.12.cloned.1.call-update) | async-done | bytes 720912 | tf_op jit(solution)/shard_map/reduce_scatter | solution.py:338
  1396.8 7.5 fusion.125
  1407.0 45.6 %all-reduce.1 = (f32[16,32]{1,0:T(8,128)}, f32[1024]{0:T(1024)}, f32[1024]{0:T(1024)}, f32[1024,4]{0,1:T(4,128)}) all-reduce(f32[16,32]{1,0:T(8,128)S(1)} %pad_subtract_fusion, f32[1024]{0:T(1024)S(1)} %get-tuple-element.495, f32[1024]{0:T(1024)S(1)} %copy-done.66, ...), channel_id=1, replica_groups=mesh['dp'=4,'ep'=2,'cp'=4] {'dp','ep','cp'}, use_global_device_ids=true, to_apply=%region_25.26 | all-reduce | flops 6656 | bytes 53248 | tf_op jit(solution)/shard_map/psum | solution.py:331
  1452.6 309.6 %reduce-scatter.8.cloned.1.call-done = f32[1024,128]{1,0:T(8,128)} async-done(((f32[1024,4096]{1,0:T(8,128)}), f32[1024,128]{1,0:T(8,128)}) %reduce-scatter.8.cloned.1.call-update) | async-done | bytes 524304 | tf_op jit(solution)/shard_map/reduce_scatter | solution.py:330
  (426 shorter events, 296.2 us)
Async XLA Ops:
  7.2 365.9 %copy-start = (bf16[1024,4]{0,1:T(4,128)(2,1)S(1)}, bf16[1024,4]{0,1:T(4,128)(2,1)}, u32[]{:S(2)}) copy-start(bf16[1024,4]{0,1:T(4,128)(2,1)} %param.29) | copy-start | bytes 24580
  7.2 164.0 %all-gather.2.cloned.1.call-start = ((), (), s32[]{:S(2)}) async-start(), calls=%async_computation.9 | async-start | bytes 10485760 | tf_op jit(solution)/shard_map/all_gather | solution.py:82
  8.8 6.7 copy-start.40
  21.3 361.5 %copy-start.64 = (s32[512,2]{0,1:T(2,128)}, s32[512,2]{0,1:T(2,128)S(1)}, u32[]{:S(2)}) copy-start(s32[512,2]{0,1:T(2,128)S(1)} %eq.31) | copy-start | bytes 12292
  21.6 4.4 copy-start.47
  26.1 340.9 %copy-start.70 = (f32[256,2]{0,1:T(2,128)}, f32[256,2]{0,1:T(2,128)S(1)}, u32[]{:S(2)}) copy-start(f32[256,2]{0,1:T(2,128)S(1)} %compare_convert_fusion) | copy-start | bytes 6148
  364.8 6.6 copy-start.6
  364.8 6.6 copy-start.30
  364.8 6.6 copy-start.34
  364.9 6.6 copy-start.38
  364.9 6.6 copy-start.48
  368.0 4.8 copy-start.54
  373.1 5.8 copy-start.17
  374.4 4.4 copy-start.67
  378.9 34.8 %all-to-all-start.2 = ((bf16[2,2,320,1024]{3,2,1,0:T(8,128)(2,1)}), bf16[2,2,320,1024]{3,2,1,0:T(8,128)(2,1)S(1)}, u32[]{:S(2)}, u32[]{:S(2)}) async-start(bf16[2,2,320,1024]{3,2,1,0:T(8,128)(2,1)} %bitcast.344), calls=%async_computation.2 | async-start | bytes 5242880 | tf_op jit(solution)/shard_map/all_to_all | solution.py:183
  415.2 34.0 %all-to-all-start = ((bf16[2,2,320,1024]{3,2,1,0:T(8,128)(2,1)}), bf16[2,2,320,1024]{3,2,1,0:T(8,128)(2,1)S(1)}, u32[]{:S(2)}, u32[]{:S(2)}) async-start(bf16[2,2,320,1024]{3,2,1,0:T(8,128)(2,1)} %bitcast.343), calls=%async_computation | async-start | bytes 5242880 | tf_op jit(solution)/shard_map/all_to_all | solution.py:163
  449.1 15.9 copy-start.11
  506.2 34.2 %all-to-all-start.1 = ((bf16[2,2,320,1024]{3,2,1,0:T(8,128)(2,1)}), bf16[2,2,320,1024]{3,2,1,0:T(8,128)(2,1)}, u32[]{:S(2)}, u32[]{:S(2)}) async-start(bf16[2,2,320,1024]{3,2,1,0:T(8,128)(2,1)} %copy.165), calls=%async_computation.1 | async-start | bytes 5242880 | tf_op jit(solution)/shard_map/all_to_all | solution.py:171
  538.5 7.0 copy-start.22
  540.3 7.7 copy-start.65
  540.3 7.7 copy-start.68
  540.4 34.3 %all-to-all-start.3 = ((bf16[2,2,320,1024]{3,2,1,0:T(8,128)(2,1)}), bf16[2,2,320,1024]{3,2,1,0:T(8,128)(2,1)}, u32[]{:S(2)}, u32[]{:S(2)}) async-start(bf16[2,2,320,1024]{3,2,1,0:T(8,128)(2,1)} %copy.172), calls=%async_computation.3 | async-start | bytes 5242880 | tf_op jit(solution)/shard_map/all_to_all | solution.py:203
  545.4 457.3 %reduce-scatter.6.cloned.1.call-start = ((), (), s32[]{:S(2)}) async-start(), calls=%async_computation.10 | async-start | bytes 10485760 | tf_op jit(solution)/shard_map/reduce_scatter | solution.py:309
  547.9 7.5 copy-start.57
  547.9 7.5 copy-start.59
  547.9 7.5 copy-start.43
  547.9 7.5 copy-start.52
  547.9 26.7 %copy-start.33 = (bf16[256,2,1280]{2,1,0:T(2,128)(2,1)S(1)}, bf16[256,2,1280]{2,1,0:T(2,128)(2,1)}, u32[]{:S(2)}) copy-start(bf16[256,2,1280]{2,1,0:T(2,128)(2,1)} %dot_general.121) | copy-start | bytes 3932164
  555.5 22.7 %copy-start.45 = (f32[256,2,4]{0,2,1:T(4,128)}, f32[256,2,4]{0,2,1:T(4,128)S(1)}, u32[]{:S(2)}) copy-start(f32[256,2,4]{0,2,1:T(4,128)S(1)} %select_reduce_fusion) | copy-start | bytes 24580
  555.5 22.6 %copy-start.62 = (f32[256,2]{0,1:T(2,128)}, f32[256,2]{0,1:T(2,128)S(1)}, u32[]{:S(2)}) copy-start(f32[256,2]{0,1:T(2,128)S(1)} %multiply_reduce_fusion.6) | copy-start | bytes 6148
  578.2 6.3 copy-start.24
  584.5 5.7 copy-start.71
  597.9 18.2 %copy-start.9 = (bf16[256,2,16,64]{0,3,2,1:T(8,128)(2,1)}, bf16[256,2,16,64]{0,3,2,1:T(8,128)(2,1)S(1)}, u32[]{:S(2)}) copy-start(bf16[256,2,16,64]{0,3,2,1:T(8,128)(2,1)S(1)} %get-tuple-element.946) | copy-start | bytes 3145732 | tf_op jit(solution)/shard_map/while
  624.3 4.6 copy-start.5
  638.4 8.4 copy-start.3
  649.6 4.5 copy-start.4
  654.0 6.2 copy-start.10
  660.2 18.2 %copy-start.9 = (bf16[256,2,16,64]{0,3,2,1:T(8,128)(2,1)}, bf16[256,2,16,64]{0,3,2,1:T(8,128)(2,1)S(1)}, u32[]{:S(2)}) copy-start(bf16[256,2,16,64]{0,3,2,1:T(8,128)(2,1)S(1)} %get-tuple-element.946) | copy-start | bytes 3145732 | tf_op jit(solution)/shard_map/while
  686.5 4.5 copy-start.5
  700.7 8.4 copy-start.3
  711.8 5.1 copy-start.4
  716.9 6.2 copy-start.10
  723.1 18.2 %copy-start.9 = (bf16[256,2,16,64]{0,3,2,1:T(8,128)(2,1)}, bf16[256,2,16,64]{0,3,2,1:T(8,128)(2,1)S(1)}, u32[]{:S(2)}) copy-start(bf16[256,2,16,64]{0,3,2,1:T(8,128)(2,1)S(1)} %get-tuple-element.946) | copy-start | bytes 3145732 | tf_op jit(solution)/shard_map/while
  749.4 4.6 copy-start.5
  763.6 8.4 copy-start.3
  774.7 5.1 copy-start.4
  779.8 6.2 copy-start.10
  786.1 18.2 %copy-start.9 = (bf16[256,2,16,64]{0,3,2,1:T(8,128)(2,1)}, bf16[256,2,16,64]{0,3,2,1:T(8,128)(2,1)S(1)}, u32[]{:S(2)}) copy-start(bf16[256,2,16,64]{0,3,2,1:T(8,128)(2,1)S(1)} %get-tuple-element.946) | copy-start | bytes 3145732 | tf_op jit(solution)/shard_map/while
  812.4 4.6 copy-start.5
  826.5 8.4 copy-start.3
  837.7 5.1 copy-start.4
  842.8 6.2 copy-start.10
  860.9 272.9 %reduce-scatter.14.cloned.1.call-start = ((), (), s32[]{:S(2)}) async-start(), calls=%async_computation.14 | async-start | bytes 12255232 | tf_op jit(solution)/shard_map/reduce_scatter | solution.py:341
  878.5 385.9 %reduce-scatter.10.cloned.1.call-start = ((), (), s32[]{:S(2)}) async-start(), calls=%async_computation.12 | async-start | bytes 12255232 | tf_op jit(solution)/shard_map/reduce_scatter | solution.py:335
  895.4 499.0 %reduce-scatter.12.cloned.1.call-start = ((), (), s32[]{:S(2)}) async-start(), calls=%async_computation.13 | async-start | bytes 12255232 | tf_op jit(solution)/shard_map/reduce_scatter | solution.py:338
  910.6 851.6 %reduce-scatter.8.cloned.1.call-start = ((), (), s32[]{:S(2)}) async-start(), calls=%async_computation.11 | async-start | bytes 17301504 | tf_op jit(solution)/shard_map/reduce_scatter | solution.py:330
  912.9 89.9 %copy-start.26 = (bf16[256,2,1024]{2,0,1:T(8,128)(2,1)}, bf16[256,2,1024]{2,0,1:T(8,128)(2,1)S(1)}, u32[]{:S(2)}) copy-start(bf16[256,2,1024]{2,0,1:T(8,128)(2,1)S(1)} %copy.178) | copy-start | bytes 3145732
  912.9 89.9 %copy-start.19 = (bf16[256,2,1024]{2,1,0:T(2,128)(2,1)S(1)}, bf16[256,2,1024]{2,1,0:T(2,128)(2,1)}, u32[]{:S(2)}) copy-start(bf16[256,2,1024]{2,1,0:T(2,128)(2,1)} %param.20) | copy-start | bytes 3145732
  912.9 89.9 %copy-start.37 = (f32[1024]{0:T(1024)S(1)}, f32[1024]{0:T(1024)}, u32[]{:S(2)}) copy-start(f32[1024]{0:T(1024)} %param.27) | copy-start | bytes 12292
  912.9 89.9 %copy-start.41 = (f32[256,2]{0,1:T(2,128)S(1)}, f32[256,2]{0,1:T(2,128)}, u32[]{:S(2)}) copy-start(f32[256,2]{0,1:T(2,128)} %copy-done.40) | copy-start | bytes 6148
  1002.8 5.5 copy-start.29
  1018.1 378.7 %copy-start.27 = (bf16[256,2,1024]{2,0,1:T(8,128)(2,1)S(1)}, bf16[256,2,1024]{2,0,1:T(8,128)(2,1)}, u32[]{:S(2)}) copy-start(bf16[256,2,1024]{2,0,1:T(8,128)(2,1)} %copy-done.26) | copy-start | bytes 3145732
  1396.8 7.5 copy-start.21
  1404.2 357.9 %copy-start.1 = (bf16[1024,4]{0,1:T(4,128)(2,1)S(1)}, bf16[1024,4]{0,1:T(4,128)(2,1)}, u32[]{:S(2)}) copy-start(bf16[1024,4]{0,1:T(4,128)(2,1)} %param.29) | copy-start | bytes 24580
  (40 other events, 103.7 us)
Sparse Core Ops, SparseCore 0:
  18.8 152.3 all-gather.1
  861.0 141.6 reduce-scatter.5
  1006.9 126.9 reduce-scatter.13
  1138.4 125.9 reduce-scatter.9
  1268.3 126.0 reduce-scatter.11
  1397.2 364.9 reduce-scatter.7
where the time goes:
time: 1780 us; the launch traced here: 1770 us
  waiting for transfers between devices  962 us (54%)
  matrix products  432 us (24%)
  local copies, waits for them, and re-layouts  215 us (12%)
  other arithmetic  79.8 us (4%)
  blocking collectives  45.6 us (3%)
  starting transfers between devices  18 us (1%)
    reduce_scatter x1, waiting for transfers between devices, on_device(): lax.psum_scatter(attn_term, ('dp', 'ep', 'cp'), scatter_dimension=1, tile...  310 us
    all_gather x1, waiting for transfers between devices, on_device(): keyval_all = lax.all_gather(keyval, 'cp', axis=0, tiled=True)  145 us
    reduce_scatter x1, waiting for transfers between devices, on_device(): lax.psum_scatter(gate_grad.astype(jnp.bfloat16), ('dp', 'cp'), scatter_di...  128 us
    reduce_scatter x1, waiting for transfers between devices, on_device(): lax.psum_scatter(up_grad.astype(jnp.bfloat16), ('dp', 'cp'), scatter_dime...  128 us
    reduce_scatter x1, waiting for transfers between devices, on_device(): lax.psum_scatter(down_grad.astype(jnp.bfloat16), ('dp', 'cp'), scatter_di...  115 us
    reduce_scatter x1, waiting for transfers between devices, on_device(): lax.psum_scatter(kv_terms.astype(jnp.bfloat16), 'cp', scatter_dimension=0...  84.3 us
    dot_general x12, local copies, waits for them, and re-layouts, block_logits(): jnp.einsum('hb,qkb->hqk', table_step, steps, precision=lax.Precision.HIGH...  63.4 us
    dot_general x12, matrix products, block_logits(): jnp.einsum('hb,qkb->hqk', table_step, steps, precision=lax.Precision.HIGH...  47.6 us
  transfers between devices with their start and end apart: 10, of which 10 were waited for; matrix products, arithmetic and copies ran while one was open for 9% of the time, Pallas kernels for 0%

commit v1 on v0

--- a/solution.py
+++ b/solution.py
@@ -1,6 +1,10 @@
+import functools
+
 import jax
 import jax.numpy as jnp
 from jax import lax
+from jax.experimental import pallas as pl
+from jax.experimental.pallas import tpu as pltpu
 from jax.sharding import PartitionSpec as P
 
 epsilon = 1e-06
@@ -356,6 +360,626 @@
     )
 
 
+minus_big = -1000000000.0
+vmem_bytes = 56 * 1024 * 1024
+
+
+def compiler_params():
+    return pltpu.CompilerParams(vmem_limit_bytes=vmem_bytes)
+
+
+def shear(values, leftward):
+    rows, lanes = values.shape
+    row_ids = lax.broadcasted_iota(jnp.int32, (rows, lanes), 0)
+    bit = 1
+    while bit < rows:
+        amount = lanes - bit if leftward else bit
+        moved = pltpu.roll(values, amount, 1)
+        values = jnp.where((row_ids & bit) != 0, moved, values)
+        bit *= 2
+    return values
+
+
+def bias_kernel(line_ref, bias_ref):
+    rows, columns = bias_ref.shape[1], bias_ref.shape[2]
+    lanes = rows + columns
+    line = pltpu.roll(line_ref[0], lanes - (rows - 1), 1)
+    full = jnp.broadcast_to(line, (rows, lanes))
+    bias_ref[0] = shear(full, False)[:, :columns]
+
+
+def make_bias(lines, span_rows):
+    heads, _, lanes = lines.shape
+    columns = lanes - span_rows
+    return pl.pallas_call(
+        bias_kernel,
+        grid=(heads,),
+        in_specs=[pl.BlockSpec((1, 1, lanes), lambda h: (h, 0, 0))],
+        out_specs=pl.BlockSpec((1, span_rows, columns), lambda h: (h, 0, 0)),
+        out_shape=jax.ShapeDtypeStruct((heads, span_rows, columns), jnp.float32),
+        compiler_params=compiler_params(),
+        name="bias_planes",
+    )(lines)
+
+
+def dot_nt(left, right):
+    return lax.dot_general(
+        left, right, (((1,), (1,)), ((), ())), preferred_element_type=jnp.float32
+    )
+
+
+def dot_tn(left, right):
+    return lax.dot_general(
+        left, right, (((0,), (0,)), ((), ())), preferred_element_type=jnp.float32
+    )
+
+
+def dot_nn(left, right):
+    return jnp.dot(left, right, preferred_element_type=jnp.float32)
+
+
+def key_masks(length, blocks, span_rows):
+    masks = []
+    for block in range(blocks):
+        position = block * span_rows + lax.broadcasted_iota(jnp.int32, (1, span_rows), 1)
+        masks.append(jnp.where(position < length, 0.0, minus_big))
+    return masks
+
+
+def forward_kernel(
+    scale, head_size, meta_ref, q_ref, k_ref, v_ref, bias_ref, low_ref, full_ref, total_ref
+):
+    blocks, span_rows, lanes = q_ref.shape
+    mine, length = meta_ref[0], meta_ref[1]
+    lane = lax.broadcasted_iota(jnp.int32, (1, lanes), 1)
+    masks = key_masks(length, blocks, span_rows)
+
+    def place(block):
+        return lax.rem(mine - block + blocks, blocks)
+
+    for row in range(blocks):
+        queries = q_ref[place(row)]
+        totals = jnp.zeros((span_rows, lanes), jnp.float32)
+        result = jnp.zeros((span_rows, lanes), jnp.float32)
+        for half in range(lanes // head_size):
+            own = lane // head_size == half
+            head_q = queries * jnp.where(own, scale, 0.0).astype(jnp.bfloat16)
+            head_v = jnp.where(own, 1.0, 0.0).astype(jnp.bfloat16)
+            logits = []
+            for column in range(row + 1):
+                at = (blocks - 1 - row + column) * span_rows
+                part = dot_nt(head_q, k_ref[place(column)])
+                part = part + bias_ref[half, :, at : at + span_rows] + masks[column]
+                logits.append(part)
+            peak = jnp.max(logits[0], axis=1, keepdims=True)
+            for part in logits[1:]:
+                peak = jnp.maximum(peak, jnp.max(part, axis=1, keepdims=True))
+            total = jnp.zeros((span_rows, 1), jnp.float32)
+            mixed = jnp.zeros((span_rows, lanes), jnp.float32)
+            for column in range(row + 1):
+                weights = jnp.exp(logits[column] - peak)
+                total = total + jnp.sum(weights, axis=1, keepdims=True)
+                mixed = mixed + dot_nn(
+                    weights.astype(jnp.bfloat16), v_ref[place(column)] * head_v
+                )
+            result = result + mixed / total
+            totals = jnp.where(lane == half, peak + jnp.log(total), totals)
+        low_ref[row] = result.astype(jnp.bfloat16)
+        full_ref[row] = result
+        total_ref[row] = totals
+
+
+def attend_forward(meta, qkv, bias, scale, head_size):
+    blocks, span_rows, width = qkv.shape
+    pairs = width // (3 * 128)
+    per_pair = bias.shape[0] // pairs
+
+    def part(which):
+        return pl.BlockSpec((blocks, span_rows, 128), lambda p, which=which: (0, 0, 3 * p + which))
+
+    plain = pl.BlockSpec((blocks, span_rows, 128), lambda p: (0, 0, p))
+
+    return pl.pallas_call(
+        functools.partial(forward_kernel, scale, head_size),
+        grid=(pairs,),
+        in_specs=[
+            pl.BlockSpec(memory_space=pltpu.SMEM),
+            part(0),
+            part(1),
+            part(2),
+            pl.BlockSpec((per_pair,) + bias.shape[1:], lambda p: (p, 0, 0)),
+        ],
+        out_specs=[plain, plain, plain],
+        out_shape=[
+            jax.ShapeDtypeStruct((blocks, span_rows, pairs * 128), jnp.bfloat16),
+            jax.ShapeDtypeStruct((blocks, span_rows, pairs * 128), jnp.float32),
+            jax.ShapeDtypeStruct((blocks, span_rows, pairs * 128), jnp.float32),
+        ],
+        compiler_params=compiler_params(),
+        name="attend_forward",
+    )(meta, qkv, qkv, qkv, bias)
+
+
+def backward_kernel(
+    scale,
+    head_size,
+    meta_ref,
+    q_ref,
+    k_ref,
+    v_ref,
+    bias_ref,
+    grad_ref,
+    full_ref,
+    total_ref,
+    sent_ref,
+    ring_ref,
+    line_ref,
+    key_sum,
+    value_sum,
+    plane,
+):
+    blocks, span_rows, lanes = q_ref.shape
+    mine, length = meta_ref[0], meta_ref[1]
+    lane = lax.broadcasted_iota(jnp.int32, (1, lanes), 1)
+    masks = key_masks(length, blocks, span_rows)
+    halves = lanes // head_size
+
+    def place(block):
+        return lax.rem(mine - block + blocks, blocks)
+
+    key_sum[...] = jnp.zeros_like(key_sum)
+    value_sum[...] = jnp.zeros_like(value_sum)
+    plane[...] = jnp.zeros_like(plane)
+    for row in range(blocks):
+        queries = q_ref[place(row)]
+        grads = grad_ref[row]
+        products = grads.astype(jnp.float32) * full_ref[row]
+        totals = total_ref[row]
+        query_sum = jnp.zeros((span_rows, lanes), jnp.float32)
+        for half in range(halves):
+            own = lane // head_size == half
+            one = jnp.where(own, 1.0, 0.0).astype(jnp.bfloat16)
+            head_q = queries * jnp.where(own, scale, 0.0).astype(jnp.bfloat16)
+            head_g = grads * one
+            delta = jnp.sum(jnp.where(own, products, 0.0), axis=1, keepdims=True)
+            total = totals[:, half : half + 1]
+            for column in range(row + 1):
+                at = (blocks - 1 - row + column) * span_rows
+                keys = k_ref[place(column)]
+                logits = dot_nt(head_q, keys)
+                logits = logits + bias_ref[half, :, at : at + span_rows] + masks[column]
+                weights = jnp.exp(logits - total)
+                weight_grads = dot_nt(head_g, v_ref[place(column)])
+                score_grads = weights * (weight_grads - delta)
+                plane[half, :, at : at + span_rows] += score_grads
+                low_weights = weights.astype(jnp.bfloat16)
+                low_grads = score_grads.astype(jnp.bfloat16)
+                query_sum = query_sum + dot_nn(low_grads, keys * one)
+                key_sum[column] += dot_tn(low_grads, head_q)
+                value_sum[column] += dot_tn(low_weights, head_g)
+        result = (query_sum * scale).astype(jnp.bfloat16)
+        sent_ref[row, :, :lanes] = result
+        ring_ref[place(row), :, :lanes] = result
+    for row in range(blocks):
+        result = key_sum[row].astype(jnp.bfloat16)
+        sent_ref[row, :, lanes : 2 * lanes] = result
+        ring_ref[place(row), :, lanes : 2 * lanes] = result
+        result = value_sum[row].astype(jnp.bfloat16)
+        sent_ref[row, :, 2 * lanes :] = result
+        ring_ref[place(row), :, 2 * lanes :] = result
+    for half in range(halves):
+        full = jnp.concatenate(
+            [plane[half], jnp.zeros((span_rows, span_rows), jnp.float32)], axis=1
+        )
+        summed = jnp.sum(shear(full, True), axis=0, keepdims=True)
+        line_ref[half] = pltpu.roll(summed, span_rows - 1, 1)
+
+
+def attend_backward(meta, qkv, bias, grads, full, totals, scale, head_size):
+    blocks, span_rows, width = qkv.shape
+    pairs = width // (3 * 128)
+    per_pair = bias.shape[0] // pairs
+    lanes = bias.shape[2] + span_rows
+
+    def part(which):
+        return pl.BlockSpec((blocks, span_rows, 128), lambda p, which=which: (0, 0, 3 * p + which))
+
+    plain = pl.BlockSpec((blocks, span_rows, 128), lambda p: (0, 0, p))
+    wide = pl.BlockSpec((blocks, span_rows, 384), lambda p: (0, 0, p))
+    return pl.pallas_call(
+        functools.partial(backward_kernel, scale, head_size),
+        grid=(pairs,),
+        in_specs=[
+            pl.BlockSpec(memory_space=pltpu.SMEM),
+            part(0),
+            part(1),
+            part(2),
+            pl.BlockSpec((per_pair,) + bias.shape[1:], lambda p: (p, 0, 0)),
+            plain,
+            plain,
+            plain,
+        ],
+        out_specs=[wide, wide, pl.BlockSpec((per_pair, 1, lanes), lambda p: (p, 0, 0))],
+        out_shape=[
+            jax.ShapeDtypeStruct(qkv.shape, jnp.bfloat16),
+            jax.ShapeDtypeStruct(qkv.shape, jnp.bfloat16),
+            jax.ShapeDtypeStruct((bias.shape[0], 1, lanes), jnp.float32),
+        ],
+        scratch_shapes=[
+            pltpu.VMEM((blocks, span_rows, 128), jnp.float32),
+            pltpu.VMEM((blocks, span_rows, 128), jnp.float32),
+            pltpu.VMEM((per_pair,) + bias.shape[1:], jnp.float32),
+        ],
+        compiler_params=compiler_params(),
+        name="attend_backward",
+    )(meta, qkv, qkv, qkv, bias, grads, full, totals)
+
+
+gelu_inner = 0.7978845608028654
+gelu_cubic = 0.044715
+
+
+def expert_kernel(
+    experts,
+    expert_ref,
+    rows_ref,
+    grads_ref,
+    router_ref,
+    gate_ref,
+    up_ref,
+    down_ref,
+    back_ref,
+    out_ref,
+    weight_ref,
+    total,
+):
+    step = pl.program_id(0)
+    model_width = rows_ref.shape[1]
+    pieces, _, piece, _ = weight_ref.shape
+    rows, grads = rows_ref[...], grads_ref[...]
+    lane = lax.broadcasted_iota(jnp.int32, (1, router_ref.shape[1]), 1)
+    expert = expert_ref[0]
+    router = jnp.where(lane < experts, dot_nn(rows, router_ref[...]), minus_big)
+    router = jnp.exp(router - jnp.max(router, axis=1, keepdims=True))
+    gates = jnp.sum(jnp.where(lane == expert, router, 0.0), axis=1, keepdims=True) / jnp.sum(
+        router, axis=1, keepdims=True
+    )
+    gate_pre = dot_nn(rows, gate_ref[...])
+    up_pre = dot_nn(rows, up_ref[...])
+    square = gate_pre * gate_pre
+    tanh = jnp.tanh(gelu_inner * gate_pre * (1.0 + gelu_cubic * square))
+    half = 0.5 + 0.5 * tanh
+    active = gate_pre * half
+    slope = half + active * (1.0 - tanh) * (
+        gelu_inner * (1.0 + 3.0 * gelu_cubic * square)
+    )
+    inner = active * up_pre
+    low_inner = inner.astype(jnp.bfloat16)
+    plain_grads = dot_nn(grads, down_ref[...])
+    gate_grads = jnp.sum(plain_grads * low_inner.astype(jnp.float32), axis=1, keepdims=True)
+    inner_grads = plain_grads * gates
+    low_gate = (inner_grads * up_pre * slope).astype(jnp.bfloat16)
+    low_up = (inner_grads * active).astype(jnp.bfloat16)
+    gated = (inner * gates).astype(jnp.bfloat16)
+    back = dot_nt(low_gate, gate_ref[...]) + dot_nt(low_up, up_ref[...])
+    back_ref[:, :model_width] = back.astype(jnp.bfloat16)
+    back_ref[:, model_width:] = jnp.where(lane == expert, gate_grads, 0.0).astype(jnp.bfloat16)
+    out_ref[...] = (gates * dot_nt(low_inner, down_ref[...])).astype(jnp.bfloat16)
+
+    @pl.when(step == 0)
+    def _():
+        total[...] = jnp.zeros_like(total)
+
+    total[0] += dot_tn(low_gate, rows)
+    total[1] += dot_tn(low_up, rows)
+    total[2] += dot_tn(gated, grads)
+
+    @pl.when(step == pl.num_programs(0) - 1)
+    def _():
+        for at in range(pieces):
+            weight_ref[at] = total[:, at * piece : (at + 1) * piece].astype(jnp.bfloat16)
+
+
+def run_expert(expert, rows, grads, router, gate_w, up_w, down_w, experts, pieces, tile):
+    count, model_width = rows.shape
+    hidden_units = gate_w.shape[1]
+    whole = lambda shape: pl.BlockSpec(shape, lambda i: (0,) * len(shape))
+    tiled = lambda width: pl.BlockSpec((tile, width), lambda i: (i, 0))
+    grad_shape = (pieces, 3, hidden_units // pieces, model_width)
+    return pl.pallas_call(
+        functools.partial(expert_kernel, experts),
+        grid=(count // tile,),
+        in_specs=[
+            pl.BlockSpec(memory_space=pltpu.SMEM),
+            tiled(model_width),
+            tiled(model_width),
+            whole(router.shape),
+            whole(gate_w.shape),
+            whole(up_w.shape),
+            whole(down_w.shape),
+        ],
+        out_specs=[tiled(model_width + 128), tiled(model_width), whole(grad_shape)],
+        out_shape=[
+            jax.ShapeDtypeStruct((count, model_width + 128), jnp.bfloat16),
+            jax.ShapeDtypeStruct((count, model_width), jnp.bfloat16),
+            jax.ShapeDtypeStruct(grad_shape, jnp.bfloat16),
+        ],
+        scratch_shapes=[pltpu.VMEM((3, hidden_units, model_width), jnp.float32)],
+        compiler_params=compiler_params(),
+        name="expert_rows",
+    )(expert, rows, grads, router, gate_w, up_w, down_w)
+
+
+def send(values, axis, pairs):
+    return lax.ppermute(values, axis, pairs)
+
+
+def fast_device(
+    tokens,
+    lengths,
+    expert_ids,
+    places,
+    buckets,
+    w_attn,
+    bias_table,
+    norm1_gain,
+    norm2_gain,
+    w_router,
+    w_gate,
+    w_up,
+    w_down,
+    cotangent,
+):
+    span_rows, slots, model_width = tokens.shape
+    head_count, bucket_count = bias_table.shape
+    head_size = model_width // head_count
+    scale = head_size ** (-0.5)
+    n_dp = lax.axis_size("dp")
+    n_ep = lax.axis_size("ep")
+    n_cp = lax.axis_size("cp")
+    my_dp, my_ep, my_cp = (lax.axis_index(name) for name in ("dp", "ep", "cp"))
+    seq_len = span_rows * n_cp
+    rows = span_rows * slots
+    top_count = expert_ids.shape[2]
+    experts = w_router.shape[1]
+    exp_dev = w_gate.shape[0]
+    units = w_gate.shape[2] // n_dp
+    piece = units // n_cp
+    capacity = (5 * rows * top_count + 4 * experts - 1) // (4 * experts)
+    groups = model_width // (128 * n_cp)
+    own_width = 3 * groups * 128
+    heads_own = head_count // n_cp
+    over_core = [(i, i ^ 1) for i in range(n_dp)]
+    over_x = [(i, i ^ 2) for i in range(n_dp)]
+    over_y = [(i, i ^ 1) for i in range(n_ep)]
+    ring = [(i, (i + 1) % n_cp) for i in range(n_cp)]
+    f32, bf16 = jnp.float32, jnp.bfloat16
+
+    slot_tokens = tokens.transpose(1, 0, 2).astype(f32)
+    scale_first = root_scale(slot_tokens)
+    normed_first = (slot_tokens * scale_first * norm1_gain).astype(bf16)
+
+    def ring_gather(values):
+        parts = [values]
+        for _ in range(n_cp - 1):
+            parts.append(send(parts[-1], "cp", ring))
+        return jnp.stack(parts)
+
+    normed_all = [ring_gather(normed_first[s]) for s in range(slots)]
+
+    w_qkv = (
+        w_attn[:, : 3 * model_width]
+        .reshape(model_width, 3, groups, n_cp, 128)
+        .transpose(0, 3, 2, 1, 4)
+        .reshape(model_width, 3 * model_width)
+    )
+    w_own = lax.dynamic_slice(w_qkv, (0, my_cp * own_width), (model_width, own_width))
+    w_out = (
+        w_attn[:, 3 * model_width :]
+        .reshape(groups, n_cp, 128, model_width)
+        .transpose(1, 0, 2, 3)
+        .reshape(model_width, model_width)
+    )
+    per_group = 128 // head_size
+    own_heads = (
+        jnp.arange(groups)[:, None] * (n_cp * per_group)
+        + my_cp * per_group
+        + jnp.arange(per_group)[None, :]
+    ).reshape(heads_own)
+    head_hot = (own_heads[:, None] == jnp.arange(head_count)[None, :]).astype(f32)
+    bucket_hot = (buckets[:, None] == jnp.arange(bucket_count)[None, :]).astype(f32)
+    exact = lax.Precision.HIGHEST
+    own_table = jnp.dot(head_hot, bias_table, precision=exact)
+    lines = jnp.einsum("hb,db->hd", own_table, bucket_hot[::-1], precision=exact)
+    lines = jnp.concatenate([lines, jnp.full((heads_own, span_rows), minus_big, f32)], axis=1)
+    bias = make_bias(lines[:, None, :], span_rows)
+
+    def plane_gather(values):
+        over = send(values, "dp", over_x)
+        up = send(values, "ep", over_y)
+        half = values.shape[0] // 2
+        across = jnp.concatenate(
+            [send(over[:half], "ep", over_y), send(up[half:], "dp", over_x)], axis=0
+        )
+        return [values, over, up, across]
+
+    target = jnp.where(places >= 0, expert_ids * capacity + places, -1)
+    target = target.transpose(2, 1, 0).reshape(top_count, rows)
+    targets = plane_gather(target)
+    row_ids = my_ep * (exp_dev * capacity) + jnp.arange(exp_dev * capacity, dtype=jnp.int32)
+
+    def hot_rows(chosen):
+        hot = jnp.zeros((exp_dev * capacity, rows), f32)
+        for c in range(top_count):
+            hot = hot + (row_ids[:, None] == chosen[c][None, :]).astype(f32)
+        return hot.astype(bf16)
+
+    hots = [hot_rows(chosen) for chosen in targets]
+
+    def pick_rows(blocks):
+        picked = [
+            jnp.dot(hot, block, preferred_element_type=f32).astype(bf16)
+            for hot, block in zip(hots, blocks)
+        ]
+        mine = jnp.stack(picked)
+        theirs = send(mine, "dp", over_core)
+        whole = jnp.stack([mine, theirs]).reshape(2 * len(blocks), exp_dev, capacity, model_width)
+        return [whole[:, e].reshape(-1, model_width) for e in range(exp_dev)]
+
+    low_out = cotangent.transpose(1, 0, 2)
+    grad_out = low_out.astype(f32).reshape(rows, model_width)
+    grad_picked = pick_rows(plane_gather(low_out.reshape(rows, model_width)))
+    units_at = my_dp * units
+    gate_own = lax.dynamic_slice_in_dim(w_gate, units_at, units, axis=2)
+    up_own = lax.dynamic_slice_in_dim(w_up, units_at, units, axis=2)
+    down_own = lax.dynamic_slice_in_dim(w_down, units_at, units, axis=2)
+    router_wide = jnp.concatenate(
+        [w_router, jnp.zeros((model_width, 128 - experts), w_router.dtype)], axis=1
+    )
+
+    metas = [jnp.stack([my_cp.astype(jnp.int32), lengths[s]]) for s in range(slots)]
+    qkvs, fulls, totals, returned = [], [], [], []
+    for s in range(slots):
+        qkv = jnp.dot(
+            normed_all[s].reshape(seq_len, model_width), w_own, preferred_element_type=f32
+        )
+        qkv = qkv.astype(bf16).reshape(n_cp, span_rows, own_width)
+        low, full, total = attend_forward(metas[s], qkv, bias, scale, head_size)
+        qkvs.append(qkv)
+        fulls.append(full)
+        totals.append(total)
+        back = lax.all_to_all(low, "cp", split_axis=0, concat_axis=0, tiled=True)
+        returned.append(back.transpose(1, 0, 2).reshape(span_rows, model_width))
+    attended = jnp.concatenate(returned, axis=0)
+    projected = jnp.dot(attended, w_out, preferred_element_type=f32)
+    positions = my_cp * span_rows + jnp.arange(span_rows, dtype=jnp.int32)
+    live = (positions[None, :] < lengths[:, None]).astype(f32).reshape(rows, 1)
+    inputs = slot_tokens.reshape(rows, model_width)
+    hidden = inputs + live * projected
+    scale_second = root_scale(hidden)
+    normed_second = (hidden * scale_second * norm2_gain).astype(bf16)
+    router_logits = jnp.dot(normed_second, w_router, preferred_element_type=f32)
+    router_probs = jax.nn.softmax(router_logits, axis=-1)
+
+    rows_picked = pick_rows(plane_gather(normed_second))
+    sources = len(hots)
+
+    def combine(per_expert, e):
+        mine, theirs = per_expert[: sources * capacity], per_expert[sources * capacity :]
+        theirs = send(theirs, "dp", over_core)
+        both = (mine.astype(f32) + theirs.astype(f32)).astype(bf16)
+        both = both.reshape(sources, capacity, -1)
+        at = e * capacity
+        return [dot_tn(hots[k][at : at + capacity], both[k]) for k in range(sources)]
+
+    def plane_sum(blocks):
+        here, over, up, across = blocks
+        half = rows // 2
+        got = send(jnp.stack([over[:half], across[:half]]), "dp", over_x).astype(f32)
+        first, next_first = here[:half] + got[0], up[:half] + got[1]
+        got = send(jnp.stack([up[half:], across[half:]]), "ep", over_y).astype(f32)
+        second, next_second = here[half:] + got[0], over[half:] + got[1]
+        first = first + send(next_first.astype(bf16), "ep", over_y).astype(f32)
+        second = second + send(next_second.astype(bf16), "dp", over_x).astype(f32)
+        return jnp.concatenate([first, second], axis=0)
+
+    back_parts, out_parts, weight_sums = [], [], []
+    for e in range(exp_dev):
+        expert = (my_ep * exp_dev + e).astype(jnp.int32).reshape(1)
+        back, out, weight = run_expert(
+            expert,
+            rows_picked[e],
+            grad_picked[e],
+            router_wide,
+            gate_own[e],
+            up_own[e],
+            down_own[e],
+            experts,
+            n_cp,
+            2 * capacity,
+        )
+        weight_sums.append(lax.psum_scatter(weight, "cp", scatter_dimension=0, tiled=False))
+        back_parts.append(combine(back, e))
+        out_parts.append(combine(out, e))
+
+    def merged(parts):
+        return plane_sum(
+            [sum(part[k] for part in parts).astype(bf16) for k in range(sources)]
+        )
+
+    back_rows = merged(back_parts)
+    mixed = hidden + merged(out_parts)
+    mixed = mixed.astype(bf16).reshape(slots, span_rows, model_width).transpose(1, 0, 2)
+
+    prob_grads = back_rows[:, model_width : model_width + experts]
+    logit_grads = router_probs * (
+        prob_grads - jnp.sum(router_probs * prob_grads, axis=-1, keepdims=True)
+    )
+    logit_grads = logit_grads.astype(bf16)
+    router_grad = dot_tn(normed_second, logit_grads)
+    grad_normed_second = back_rows[:, :model_width] + dot_nt(logit_grads, w_router)
+    gain_second_grad = jnp.sum(grad_normed_second * hidden * scale_second, axis=0)
+    grad_hidden = grad_out + norm_back(grad_normed_second, hidden, scale_second, norm2_gain)
+    grad_proj = (live * grad_hidden).astype(bf16)
+    grad_att = dot_nt(grad_proj, w_out).astype(bf16)
+
+    sents, rings = [], []
+    line_grads = jnp.zeros((heads_own, seq_len + span_rows), f32)
+    for s in range(slots):
+        leaving = grad_att[s * span_rows : (s + 1) * span_rows]
+        leaving = leaving.reshape(span_rows, n_cp, groups * 128).transpose(1, 0, 2)
+        grads = lax.all_to_all(leaving, "cp", split_axis=0, concat_axis=0, tiled=True)
+        sent, ringed, line = attend_backward(
+            metas[s], qkvs[s], bias, grads, fulls[s], totals[s], scale, head_size
+        )
+        line_grads = line_grads + line[:, 0]
+        rings.append(ringed.reshape(seq_len, own_width))
+        sent = lax.all_to_all(sent, "cp", split_axis=0, concat_axis=0, tiled=True)
+        sents.append(sent.transpose(1, 0, 2).reshape(span_rows, 3 * model_width))
+
+    out_grad = dot_tn(attended, grad_proj).astype(bf16)
+    out_grad = out_grad.reshape(n_cp, groups, 128, n_ep, n_cp, 128)
+    out_grad = out_grad.transpose(4, 3, 1, 0, 2, 5).reshape(n_cp, n_ep, model_width, 128)
+    out_grad = lax.psum_scatter(out_grad, "cp", scatter_dimension=0, tiled=False)
+    qkv_grad = sum(
+        dot_tn(normed_all[s].reshape(seq_len, model_width), rings[s]) for s in range(slots)
+    )
+    gain_first_grad = jnp.sum(qkv_grad * w_own.astype(f32), axis=1) / norm1_gain
+    attn_term = qkv_grad.reshape(model_width, groups, 3, 128).transpose(2, 1, 0, 3)
+    attn_term = jnp.concatenate(
+        [attn_term.reshape(3 * groups, model_width, 128).astype(bf16), out_grad], axis=0
+    )
+    attn_sum = lax.psum_scatter(attn_term, ("dp", "ep"), scatter_dimension=0, tiled=False)
+    distance_grads = line_grads[:, :seq_len][:, ::-1]
+    table_grad = jnp.dot(distance_grads, bucket_hot, precision=exact)
+    table_grad = jnp.einsum("hg,hb->gb", head_hot, table_grad, precision=exact)
+    router_sum, table_sum, gain_first_sum, gain_second_sum = lax.psum(
+        (router_grad, table_grad, gain_first_grad, gain_second_grad), ("dp", "ep", "cp")
+    )
+
+    grad_normed_first = dot_nt(jnp.concatenate(sents, axis=0), w_qkv)
+    tokens_grad = grad_hidden + norm_back(
+        grad_normed_first, inputs, scale_first.reshape(rows, 1), norm1_gain
+    )
+    tokens_grad = tokens_grad.astype(bf16).reshape(slots, span_rows, model_width).transpose(1, 0, 2)
+    weight_all = jnp.stack(weight_sums)
+    gate_sum, up_sum, down_sum = (
+        weight_all[:, which].transpose(0, 2, 1).astype(f32) for which in range(3)
+    )
+    return (
+        mixed,
+        tokens_grad,
+        attn_sum.astype(f32),
+        table_sum,
+        gain_first_sum,
+        gain_second_sum,
+        router_sum,
+        gate_sum,
+        up_sum,
+        down_sum,
+    )
+
+
 def solution(mesh):
     placed = (
         P("cp", ("dp", "ep"), None),
@@ -373,8 +997,10 @@
         P("ep", None, None),
         P("cp", ("dp", "ep"), None),
     )
+    sizes = dict(mesh.shape)
+    square = sizes["dp"] == 4 and sizes["ep"] == 2 and sizes["cp"] == 4
     return jax.shard_map(
-        on_device,
+        fast_device if square else on_device,
         mesh=mesh,
         in_specs=placed,
         out_specs=(

time: 1780 us -> 833 us (0.47)
  waiting for transfers between devices: 962 us -> 267 us
  matrix products: 432 us -> 61.9 us
  Pallas kernels: 0 us -> 176 us
  local copies, waits for them, and re-layouts: 215 us -> 123 us
  starting transfers between devices: 18 us -> 60.8 us
    reduce_scatter x5 -> x4, waiting for transfers between devices: 765 us -> 80.2 us  [the longest x1 41.6 us: fast_device(): lax.psum_scatter(attn_term, ('dp', 'ep'), scatter_dimension=0, tiled=False)]
    dot_general x65 -> x39, matrix products: 432 us -> 61.9 us  [the longest x20 25.1 us: dot_tn(): lax.dot_general(left, right, (((0,), (0,)), ((), ())), preferred_element_...]
    pallas_call x0 -> x7, Pallas kernels: none -> 176 us  [the longest x2 102 us: run_expert(): pl.pallas_call(functools.partial(expert_kernel, experts), grid=(count //...]
    all_gather x1 -> x0, waiting for transfers between devices: 145 us -> none  [on_device(): keyval_all = lax.all_gather(keyval, 'cp', axis=0, tiled=True)]
    ppermute x0 -> x32, waiting for transfers between devices: none -> 104 us  [send(): return lax.ppermute(values, axis, pairs)]
    dot_general x14 -> x0, local copies, waits for them, and re-layouts: 65.8 us -> none  [the longest x12 63.4 us: block_logits(): jnp.einsum('hb,qkb->hqk', table_step, steps, precision=lax.Precision.HIGH...]
    ge x12 -> x0, local copies, waits for them, and re-layouts: 47.2 us -> none  [the longest x4 45.8 us: block_logits(): distance[:, :, None] >= rise_points[None, None, :]]
    reshape x3 -> x10, local copies, waits for them, and re-layouts: 2.56 us -> 41.8 us  [the longest x2 22.8 us: fast_device(): w_qkv = w_attn[:, :3 * model_width].reshape(model_width, 3, groups, n_cp,...]
  transfers between devices with their start and end apart: 10 -> 42, of which waited for: 10 -> 16; matrix products, arithmetic and copies ran while one was open for 9% -> 25% of each run, Pallas kernels for 0% -> 15%
where the time goes in v1:
time: 833 us; the launch traced here: 822 us
  waiting for transfers between devices  267 us (32%)
  Pallas kernels  176 us (21%)
  local copies, waits for them, and re-layouts  123 us (15%)
  other arithmetic  62.6 us (8%)
  matrix products  61.9 us (7%)
  starting transfers between devices  60.8 us (7%)
  blocking collectives  55.6 us (7%)
  between operations  15.1 us (2%)
    ppermute x32, waiting for transfers between devices, send(): return lax.ppermute(values, axis, pairs)  104 us
    pallas_call x2, Pallas kernels, run_expert(): pl.pallas_call(functools.partial(expert_kernel, experts), grid=(count //...  102 us
    psum x1, blocking collectives, fast_device(): lax.psum((router_grad, table_grad, gain_first_grad, gain_second_grad), ('...  55.6 us
    all_to_all x2, waiting for transfers between devices, fast_device(): sent = lax.all_to_all(sent, 'cp', split_axis=0, concat_axis=0, tiled=True)  53.9 us
    pallas_call x2, Pallas kernels, attend_backward(): pl.pallas_call(functools.partial(backward_kernel, scale, head_size), grid...  46.6 us
    reduce_scatter x1, waiting for transfers between devices, fast_device(): lax.psum_scatter(attn_term, ('dp', 'ep'), scatter_dimension=0, tiled=False)  41.6 us
    reduce_scatter x2, waiting for transfers between devices, fast_device(): lax.psum_scatter(weight, 'cp', scatter_dimension=0, tiled=False)  38.6 us
    ppermute x32, starting transfers between devices, send(): return lax.ppermute(values, axis, pairs)  31.8 us
  transfers between devices with their start and end apart: 42, of which 16 were waited for; matrix products, arithmetic and copies ran while one was open for 25% of the time, Pallas kernels for 15%

profile of v1, /device:TPU:0, one launch (start us, length us, event | category | flops | bytes accessed | tf_op | source)
XLA Modules:
  0.0 822.2 jit_solution(3146465521655375047)
XLA Ops:
  12.3 3.0 collective-permute-start
  20.0 2.6 copy.94
  23.7 6.7 collective-permute-done
  30.5 5.9 slice.300
  36.4 12.1 %reshape.250 = bf16[1024,3,2,4,128]{4,3,2,1,0:T(4,128)(2,1)} reshape(bf16[1024,3072]{1,0:T(8,128)(2,1)} %slice.300) | data formatting | bytes 12582912 | tf_op jit(solution)/shard_map/reshape | solution.py:772
  48.6 10.6 %copy.88 = bf16[1024,3,2,4,128]{0,4,1,2,3:T(8,128)(2,1)} copy(bf16[1024,3,2,4,128]{4,3,2,1,0:T(4,128)(2,1)} %reshape.250) | data formatting | bytes 12582912 | tf_op jit(solution)/shard_map/reshape | solution.py:772
  60.9 8.9 %bias_planes.1.bias_ref = f32[4,256,1024]{2,1,0:T(8,128)} custom-call(f32[4,1,1280]{2,1,0:T(1,128)} %broadcast_in_dim.5.line_ref), custom_call_target="tpu_custom_call" | custom-call | tf_op jit(solution)/shard_map/bias_planes/pallas_call | solution.py:394
  77.1 9.6 %collective-permute-done.4 = bf16[256,1024]{1,0:T(8,128)(2,1)} collective-permute-done((bf16[256,1024]{1,0:T(8,128)(2,1)}, bf16[256,1024]{1,0:T(8,128)(2,1)}, u32[]{:S(2)}, u32[]{:S(2)}) %collective-permute-start.4) | collective-permute-done | bytes 524320 | tf_op jit(solution)/shard_map/ppermute | solution.py:714
  88.4 6.8 collective-permute-done.2
  96.9 4.4 convolution_convert_fusion.2
  101.3 9.7 %attend_forward.2 = (bf16[4,256,256]{2,1,0:T(8,128)(2,1)}, f32[4,256,256]{2,1,0:T(8,128)}, f32[4,256,256]{2,1,0:T(8,128)}) custom-call(s32[2]{0:T(128)} %get-tuple-element.111.meta_ref, bf16[4,256,768]{2,1,0:T(8,128)(2,1)} %bitcast.247, bf16[4,256,768]{2,1,0:T(8,128)(2,1)} %bitcast.248, bf16[4,256,768]{2,1,0:T(8,128)(2,1)} %bitcast.249, ...), custom_call_target="tpu_custom_call" | custom-call | tf_op jit(solution)/shard_map/attend_forward/pallas_call | solution.py:482
  111.0 5.3 all-to-all-start
  118.0 4.4 convolution_convert_fusion.1
  122.4 9.7 %attend_forward.3 = (bf16[4,256,256]{2,1,0:T(8,128)(2,1)}, f32[4,256,256]{2,1,0:T(8,128)}, f32[4,256,256]{2,1,0:T(8,128)}) custom-call(s32[2]{0:T(128)} %get-tuple-element.112.meta_ref, bf16[4,256,768]{2,1,0:T(8,128)(2,1)} %bitcast.253, bf16[4,256,768]{2,1,0:T(8,128)(2,1)} %bitcast.254, bf16[4,256,768]{2,1,0:T(8,128)(2,1)} %bitcast.255, ...), custom_call_target="tpu_custom_call" | custom-call | tf_op jit(solution)/shard_map/attend_forward/pallas_call | solution.py:482
  132.1 5.1 all-to-all-start.1
  139.3 3.1 copy.150
  152.8 3.8 multiply_reduce_fusion.4
  164.8 17.4 %collective-permute-done.11 = s32[1,512]{1,0:T(1,128)S(1)} collective-permute-done((s32[1,512]{1,0:T(1,128)S(1)}, s32[1,512]{1,0:T(1,128)S(1)}, u32[]{:S(2)}, u32[]{:S(2)}) %collective-permute-start.11) | collective-permute-done | bytes 2080 | tf_op jit(solution)/shard_map/ppermute | solution.py:714
  182.2 2.2 fusion.21
  184.4 4.3 fusion.105
  194.0 9.2 %collective-permute-done.12 = bf16[256,1024]{0,1:T(8,128)(2,1)S(1)} collective-permute-done((bf16[256,1024]{0,1:T(8,128)(2,1)S(1)}, bf16[256,1024]{0,1:T(8,128)(2,1)S(1)}, u32[]{:S(2)}, u32[]{:S(2)}) %collective-permute-start.12) | collective-permute-done | bytes 524320 | tf_op jit(solution)/shard_map/ppermute | solution.py:714
  204.7 4.4 fusion.106
  210.2 5.3 dynamic-slice_bitcast_fusion.5
  215.5 9.4 %dynamic-slice_bitcast_fusion.3 = (bf16[1024,704]{1,0:T(8,128)(2,1)}, bf16[1024,704]{1,0:T(8,128)(2,1)}, bf16[1024,704]{1,0:T(8,128)(2,1)}, bf16[1024,704]{1,0:T(8,128)(2,1)}) fusion(bf16[2,1024,2816]{2,1,0:T(8,128)(2,1)} %param.26, s32[]{:T(128)S(6)} %select_n.14, s32[]{:T(128)S(6)} %add.276, bf16[2,1024,2816]{2,1,0:T(8,128)(2,1)} %param.25), kind=kLoop, calls=%fused_computation.63 | loop fusion | bytes 11534344 | tf_op jit(solution)/shard_map/squeeze | solution.py:896
  224.9 9.0 %pad_maximum_fusion.1 = bf16[2,4,640,1024]{3,2,1,0:T(8,128)(2,1)} fusion(bf16[1,4,640,1024]{3,2,1,0:T(8,128)(2,1)} %bitcast.50, bf16[1,4,640,1024]{3,2,1,0:T(8,128)(2,1)} %get-tuple-element.65), kind=kLoop, calls=%fused_computation.1 | loop fusion | flops 5242880 | bytes 20971520 | tf_op jit(solution)/shard_map/stack | solution.py:826
  233.9 9.6 %fusion.108 = (bf16[8,1,320,1024]{3,2,1,0:T(8,128)(2,1)}, bf16[8,1,320,1024]{3,2,1,0:T(8,128)(2,1)}) fusion(bf16[8,2,320,1024]{3,2,1,0:T(8,128)(2,1)} %bitcast.259), kind=kLoop, calls=%fused_computation.216 | loop fusion | bytes 20971520 | tf_op jit(solution)/shard_map/slice | solution.py:827
  243.6 9.0 %pad_maximum_fusion = bf16[2,4,640,1024]{3,2,1,0:T(8,128)(2,1)} fusion(bf16[1,4,640,1024]{3,2,1,0:T(8,128)(2,1)} %bitcast.41, bf16[1,4,640,1024]{3,2,1,0:T(8,128)(2,1)} %get-tuple-element.67), kind=kLoop, calls=%fused_computation | loop fusion | flops 5242880 | bytes 20971520 | tf_op jit(solution)/shard_map/stack | solution.py:826
  252.6 9.7 %fusion.109 = (bf16[8,1,320,1024]{3,2,1,0:T(8,128)(2,1)}, bf16[8,1,320,1024]{3,2,1,0:T(8,128)(2,1)}) fusion(bf16[8,2,320,1024]{3,2,1,0:T(8,128)(2,1)} %bitcast.260), kind=kLoop, calls=%fused_computation.217 | loop fusion | bytes 20971520 | tf_op jit(solution)/shard_map/slice | solution.py:827
  262.3 50.6 %expert_rows.3 = (bf16[2560,1152]{1,0:T(8,128)(2,1)}, bf16[2560,1024]{1,0:T(8,128)(2,1)}, bf16[4,3,176,1024]{3,2,1,0:T(8,128)(2,1)}) custom-call(s32[1]{0:T(128)} %bitcast.56.expert_ref, bf16[2560,1024]{1,0:T(8,128)(2,1)} %bitcast.264, bf16[2560,1024]{1,0:T(8,128)(2,1)} %bitcast.263, bf16[1024,128]{1,0:T(8,128)(2,1)} %concatenate.31.router_ref, ...), custom_call_target="tpu_custom_call" | custom-call | tf_op jit(solution)/shard_map/expert_rows/pallas_call | solution.py:689
  312.9 3.5 slice.330
  316.8 50.9 %expert_rows.2 = (bf16[2560,1152]{1,0:T(8,128)(2,1)}, bf16[2560,1024]{1,0:T(8,128)(2,1)}, bf16[4,3,176,1024]{3,2,1,0:T(8,128)(2,1)}) custom-call(s32[1]{0:T(128)} %bitcast.27.expert_ref, bf16[2560,1024]{1,0:T(8,128)(2,1)} %bitcast.262, bf16[2560,1024]{1,0:T(8,128)(2,1)} %bitcast.261, bf16[1024,128]{1,0:T(8,128)(2,1)} %concatenate.31.router_ref, ...), custom_call_target="tpu_custom_call" | custom-call | tf_op jit(solution)/shard_map/expert_rows/pallas_call | solution.py:689
  377.6 2.5 add_convert_fusion.2
  380.9 3.8 add_convert_fusion.3
  393.9 2.6 add_convert_fusion
  406.3 8.1 collective-permute-done.24
  415.7 2.6 collective-permute-done.22
  419.5 20.2 %collective-permute-done.30 = bf16[2,256,1152]{1,2,0:T(8,128)(2,1)S(1)} collective-permute-done((bf16[2,256,1152]{1,2,0:T(8,128)(2,1)S(1)}, bf16[2,256,1152]{1,2,0:T(8,128)(2,1)S(1)}, u32[]{:S(2)}, u32[]{:S(2)}) %collective-permute-start.30) | collective-permute-done | bytes 1179680 | tf_op jit(solution)/shard_map/ppermute | solution.py:714
  441.1 2.5 collective-permute-done.28
  445.7 9.2 %collective-permute-done.25 = bf16[256,1024]{0,1:T(8,128)(2,1)S(1)} collective-permute-done((bf16[256,1024]{0,1:T(8,128)(2,1)S(1)}, bf16[256,1024]{0,1:T(8,128)(2,1)S(1)}, u32[]{:S(2)}, u32[]{:S(2)}) %collective-permute-start.25) | collective-permute-done | bytes 524320 | tf_op jit(solution)/shard_map/ppermute | solution.py:714
  455.1 11.1 %collective-permute-done.31 = bf16[256,1152]{0,1:T(8,128)(2,1)S(1)} collective-permute-done((bf16[256,1152]{0,1:T(8,128)(2,1)S(1)}, bf16[256,1152]{0,1:T(8,128)(2,1)S(1)}, u32[]{:S(2)}, u32[]{:S(2)}) %collective-permute-start.31) | collective-permute-done | bytes 589856 | tf_op jit(solution)/shard_map/ppermute | solution.py:714
  470.9 2.6 convolution_convert_fusion
  473.5 3.2 reshape.272
  481.4 2.9 convolution_convert_fusion.11
  485.7 4.8 all-to-all-start.2
  491.7 27.9 %all-to-all-done.2.grad_ref = bf16[4,256,256]{2,1,0:T(8,128)(2,1)S(1)} async-done(((bf16[4,256,256]{2,1,0:T(8,128)(2,1)}), bf16[4,256,256]{2,1,0:T(8,128)(2,1)S(1)}, u32[]{:S(2)}, u32[]{:S(2)}) %all-to-all-start.2) | async-done | bytes 524320 | tf_op jit(solution)/shard_map/all_to_all | solution.py:931
  519.6 3.5 all-to-all-start.4
  523.1 23.1 %attend_backward.2 = (bf16[4,256,768]{2,1,0:T(8,128)(2,1)}, bf16[4,256,768]{2,1,0:T(8,128)(2,1)}, f32[4,1,1280]{2,1,0:T(1,128)}) custom-call(s32[2]{0:T(128)} %get-tuple-element.111.meta_ref, bf16[4,256,768]{2,1,0:T(8,128)(2,1)} %bitcast.250, bf16[4,256,768]{2,1,0:T(8,128)(2,1)} %bitcast.251, bf16[4,256,768]{2,1,0:T(8,128)(2,1)} %bitcast.252, ...), custom_call_target="tpu_custom_call" | custom-call | tf_op jit(solution)/shard_map/attend_backward/pallas_call | solution.py:589
  546.2 5.3 all-to-all-start.3
  551.4 23.6 %attend_backward.3 = (bf16[4,256,768]{2,1,0:T(8,128)(2,1)}, bf16[4,256,768]{2,1,0:T(8,128)(2,1)}, f32[4,1,1280]{2,1,0:T(1,128)}) custom-call(s32[2]{0:T(128)} %get-tuple-element.112.meta_ref, bf16[4,256,768]{2,1,0:T(8,128)(2,1)} %bitcast.256, bf16[4,256,768]{2,1,0:T(8,128)(2,1)} %bitcast.257, bf16[4,256,768]{2,1,0:T(8,128)(2,1)} %bitcast.258, ...), custom_call_target="tpu_custom_call" | custom-call | tf_op jit(solution)/shard_map/attend_backward/pallas_call | solution.py:589
  575.0 53.9 %all-to-all-done.3 = bf16[4,256,768]{2,1,0:T(8,128)(2,1)S(1)} async-done(((bf16[4,256,768]{2,1,0:T(8,128)(2,1)}), bf16[4,256,768]{2,1,0:T(8,128)(2,1)S(1)}, u32[]{:S(2)}, u32[]{:S(2)}) %all-to-all-start.3) | async-done | bytes 1572896 | tf_op jit(solution)/shard_map/all_to_all | solution.py:937
  628.9 4.4 all-to-all-start.5
  633.6 2.1 reshape.265
  635.7 4.8 copy.107
  640.6 4.1 fusion.104
  644.7 5.1 multiply_reduce_fusion
  649.8 2.6 copy.127
  652.4 3.1 pad_maximum_fusion.6
  657.6 55.6 %all-reduce.2 = (f32[16,32]{1,0:T(8,128)}, f32[1024]{0:T(1024)}, f32[1024]{0:T(1024)}, f32[1024,4]{0,1:T(4,128)}) all-reduce(f32[16,32]{1,0:T(8,128)S(1)} %fusion.92, f32[1024]{0:T(1024)S(1)} %div.33, f32[1024]{0:T(1024)S(1)} %get-tuple-element.46, f32[1024,4]{0,1:T(4,128)S(1)} %fusion.117), channel_id=1, replica_groups=mesh['dp'=4,'ep'=2,'cp'=4] {'dp','ep','cp'}, use_global_device_ids=true, to_apply=%region_9.10 | all-reduce | flops 6656 | bytes 53248 | tf_op jit(solution)/shard_map/psum | solution.py:956
  714.8 2.7 copy.122
  717.5 6.7 multiply_reduce_fusion.2
  725.1 3.5 copy.124
  729.9 38.6 %reduce-scatter.11.cloned.1.call-done = bf16[1,3,176,1024]{3,2,1,0:T(8,128)(2,1)} async-done(((bf16[4,3,176,1024]{3,2,1,0:T(8,128)(2,1)}), bf16[1,3,176,1024]{3,2,1,0:T(8,128)(2,1)}) %reduce-scatter.11.cloned.1.call-update) | async-done | bytes 1081360 | tf_op jit(solution)/shard_map/reduce_scatter | solution.py:901
  769.9 2.2 convert_bitcast_fusion
  772.1 41.6 %reduce-scatter.7.cloned.1.call-done = bf16[1,1024,128]{2,1,0:T(8,128)(2,1)} async-done(((bf16[8,1024,128]{2,1,0:T(8,128)(2,1)}), bf16[1,1024,128]{2,1,0:T(8,128)(2,1)}) %reduce-scatter.7.cloned.1.call-update) | async-done | bytes 262160 | tf_op jit(solution)/shard_map/reduce_scatter | solution.py:952
  (269 shorter events, 110.5 us)
Async XLA Ops:
  7.2 52.3 %copy-start = (f32[16,32]{1,0:T(8,128)S(1)}, f32[16,32]{1,0:T(8,128)}, u32[]{:S(2)}) copy-start(f32[16,32]{1,0:T(8,128)} %param.20) | copy-start | bytes 6148
  10.9 4.3 copy-start.36
  11.0 4.3 copy-start.37
  11.0 9.0 %copy-start.19 = (bf16[256,2,1024]{2,1,0:T(2,128)(2,1)S(1)}, bf16[256,2,1024]{2,1,0:T(2,128)(2,1)}, u32[]{:S(2)}) copy-start(bf16[256,2,1024]{2,1,0:T(2,128)(2,1)} %param.27) | copy-start | bytes 3145732
  12.3 83.0 %copy-start.17 = (bf16[1,256,1024]{2,1,0:T(8,128)(2,1)}, bf16[1,256,1024]{2,1,0:T(8,128)(2,1)S(1)}, u32[]{:S(2)}) copy-start(bf16[1,256,1024]{2,1,0:T(8,128)(2,1)S(1)} %get-tuple-element.86) | copy-start | bytes 1572868
  12.3 104.0 %copy-start.15 = (bf16[1,256,1024]{2,1,0:T(8,128)(2,1)}, bf16[1,256,1024]{2,1,0:T(8,128)(2,1)S(1)}, u32[]{:S(2)}) copy-start(bf16[1,256,1024]{2,1,0:T(8,128)(2,1)S(1)} %get-tuple-element.89) | copy-start | bytes 1572868
  12.3 18.1 %collective-permute-start = (bf16[256,1024]{1,0:T(8,128)(2,1)}, bf16[256,1024]{1,0:T(8,128)(2,1)}, u32[]{:S(2)}, u32[]{:S(2)}) collective-permute-start(bf16[256,1024]{1,0:T(8,128)(2,1)} %get-tuple-element.87), channel_id=1, source_target_pairs={{0,1},{1,2},{2,3},{3,0},{4,5},{5,6},{6,7},{7,4},{8,9},{9,10},{10,1... | collective-permute-start | bytes 1572872 | tf_op jit(solution)/shard_map/ppermute | solution.py:714
  15.3 128.7 %collective-permute-start.6 = (s32[2,512]{1,0:T(2,128)S(1)}, s32[2,512]{1,0:T(2,128)S(1)}, u32[]{:S(2)}, u32[]{:S(2)}) collective-permute-start(s32[2,512]{1,0:T(2,128)S(1)} %bitcast.305), channel_id=1, source_target_pairs={{0,16},{8,24},{16,0},{24,8},{1,17},{9,25},{17,1},{25,9},{2,18},{10... | collective-permute-start | bytes 12296 | tf_op jit(solution)/shard_map/ppermute | solution.py:714
  16.9 128.5 %collective-permute-start.8 = (s32[2,512]{1,0:T(2,128)S(1)}, s32[2,512]{1,0:T(2,128)S(1)}, u32[]{:S(2)}, u32[]{:S(2)}) collective-permute-start(s32[2,512]{1,0:T(2,128)S(1)} %bitcast.306), channel_id=1, source_target_pairs={{0,4},{4,0},{1,5},{5,1},{2,6},{6,2},{3,7},{7,3},{8,12},{12,8},{9,1... | collective-permute-start | bytes 12296 | tf_op jit(solution)/shard_map/ppermute | solution.py:714
  18.4 51.4 %collective-permute-start.3 = (bf16[256,1024]{1,0:T(8,128)(2,1)}, bf16[256,1024]{1,0:T(8,128)(2,1)}, u32[]{:S(2)}, u32[]{:S(2)}) collective-permute-start(bf16[256,1024]{1,0:T(8,128)(2,1)} %get-tuple-element.88), channel_id=1, source_target_pairs={{0,1},{1,2},{2,3},{3,0},{4,5},{5,6},{6,7},{7,4},{8,9},{9,10},{10,1... | collective-permute-start | bytes 1572872 | tf_op jit(solution)/shard_map/ppermute | solution.py:714
  22.8 114.4 %copy-start.9 = (bf16[128,8,2,256]{3,1,2,0:T(8,128)(2,1)}, bf16[128,8,2,256]{3,1,2,0:T(8,128)(2,1)S(1)}, u32[]{:S(2)}) copy-start(bf16[128,8,2,256]{3,1,2,0:T(8,128)(2,1)S(1)} %copy.157) | copy-start | bytes 3145732
  22.8 122.5 %collective-permute-start.15 = (bf16[512,1024]{0,1:T(8,128)(2,1)S(1)}, bf16[512,1024]{0,1:T(8,128)(2,1)}, u32[]{:S(2)}, u32[]{:S(2)}) collective-permute-start(bf16[512,1024]{0,1:T(8,128)(2,1)S(1)} %bitcast.277), channel_id=1, source_target_pairs={{0,16},{8,24},{16,0},{24,8},{1,17},{9,25},{17,1},{25,9},{2,18},{10... | collective-permute-start | bytes 3145736 | tf_op jit(solution)/shard_map/ppermute | solution.py:714
  30.4 40.9 %collective-permute-start.1 = (bf16[256,1024]{1,0:T(8,128)(2,1)}, bf16[256,1024]{1,0:T(8,128)(2,1)}, u32[]{:S(2)}, u32[]{:S(2)}) collective-permute-start(bf16[256,1024]{1,0:T(8,128)(2,1)} %collective-permute-done), channel_id=1, source_target_pairs={{0,1},{1,2},{2,3},{3,0},{4,5},{5,6},{6,7},{7,4},{8,9},{9,10},{10,1... | collective-permute-start | bytes 1572872 | tf_op jit(solution)/shard_map/ppermute | solution.py:714
  60.8 12.0 %copy-start.33 = (s32[2]{0:T(128)S(1)}, s32[2]{0:T(128)}, u32[]{:S(2)}) copy-start(s32[2]{0:T(128)} %param.15) | copy-start | bytes 28
  60.8 14.6 %copy-start.2 = (bf16[256,2,1024]{2,1,0:T(2,128)(2,1)S(1)}, bf16[256,2,1024]{2,1,0:T(2,128)(2,1)}, u32[]{:S(2)}) copy-start(bf16[256,2,1024]{2,1,0:T(2,128)(2,1)} %param.14) | copy-start | bytes 3145732
  69.7 17.0 %collective-permute-start.4 = (bf16[256,1024]{1,0:T(8,128)(2,1)}, bf16[256,1024]{1,0:T(8,128)(2,1)}, u32[]{:S(2)}, u32[]{:S(2)}) collective-permute-start(bf16[256,1024]{1,0:T(8,128)(2,1)} %collective-permute-done.3), channel_id=1, source_target_pairs={{0,1},{1,2},{2,3},{3,0},{4,5},{5,6},{6,7},{7,4},{8,9},{9,10},{10,1... | collective-permute-start | bytes 1572872 | tf_op jit(solution)/shard_map/ppermute | solution.py:714
  71.3 23.9 %collective-permute-start.2 = (bf16[256,1024]{1,0:T(8,128)(2,1)}, bf16[256,1024]{1,0:T(8,128)(2,1)S(1)}, u32[]{:S(2)}, u32[]{:S(2)}) collective-permute-start(bf16[256,1024]{1,0:T(8,128)(2,1)} %collective-permute-done.1), channel_id=1, source_target_pairs={{0,1},{1,2},{2,3},{3,0},{4,5},{5,6},{6,7},{7,4},{8,9},{9,10},{10,1... | collective-permute-start | bytes 1572872 | tf_op jit(solution)/shard_map/ppermute | solution.py:714
  86.7 61.3 %collective-permute-start.16 = (bf16[512,1024]{0,1:T(8,128)(2,1)S(1)}, bf16[512,1024]{0,1:T(8,128)(2,1)}, u32[]{:S(2)}, u32[]{:S(2)}) collective-permute-start(bf16[512,1024]{0,1:T(8,128)(2,1)S(1)} %bitcast.278), channel_id=1, source_target_pairs={{0,4},{4,0},{1,5},{5,1},{2,6},{6,2},{3,7},{7,3},{8,12},{12,8},{9,1... | collective-permute-start | bytes 3145736 | tf_op jit(solution)/shard_map/ppermute | solution.py:714
  95.2 21.1 %collective-permute-start.5 = (bf16[256,1024]{1,0:T(8,128)(2,1)}, bf16[256,1024]{1,0:T(8,128)(2,1)S(1)}, u32[]{:S(2)}, u32[]{:S(2)}) collective-permute-start(bf16[256,1024]{1,0:T(8,128)(2,1)} %collective-permute-done.4), channel_id=1, source_target_pairs={{0,1},{1,2},{2,3},{3,0},{4,5},{5,6},{6,7},{7,4},{8,9},{9,10},{10,1... | collective-permute-start | bytes 1572872 | tf_op jit(solution)/shard_map/ppermute | solution.py:714
  111.0 21.1 %all-to-all-start = ((bf16[4,256,256]{2,1,0:T(8,128)(2,1)}), bf16[4,256,256]{2,1,0:T(8,128)(2,1)S(1)}, u32[]{:S(2)}, u32[]{:S(2)}) async-start(bf16[4,256,256]{2,1,0:T(8,128)(2,1)} %get-tuple-element.28), calls=%async_computation | async-start | bytes 1048576 | tf_op jit(solution)/shard_map/all_to_all | solution.py:851
  132.1 7.1 copy-start.13
  132.1 19.2 %all-to-all-start.1 = ((bf16[4,256,256]{2,1,0:T(8,128)(2,1)}), bf16[4,256,256]{2,1,0:T(8,128)(2,1)}, u32[]{:S(2)}, u32[]{:S(2)}) async-start(bf16[4,256,256]{2,1,0:T(8,128)(2,1)} %get-tuple-element.29), calls=%async_computation.1 | async-start | bytes 1048576 | tf_op jit(solution)/shard_map/all_to_all | solution.py:851
  137.2 515.1 %reduce-scatter.5.cloned.1.call-start = ((), (), s32[]{:S(2)}) async-start(), calls=%async_computation.10 | async-start | bytes 2621440 | tf_op jit(solution)/shard_map/reduce_scatter | solution.py:943
  144.0 7.1 copy-start.14
  144.0 17.1 %collective-permute-start.10 = (s32[1,512]{1,0:T(1,128)S(1)}, s32[1,512]{1,0:T(1,128)S(1)}, u32[]{:S(2)}, u32[]{:S(2)}) collective-permute-start(s32[1,512]{1,0:T(1,128)S(1)} %get-tuple-element.97), channel_id=1, source_target_pairs={{0,4},{4,0},{1,5},{5,1},{2,6},{6,2},{3,7},{7,3},{8,12},{12,8},{9,1... | collective-permute-start | bytes 6152 | tf_op jit(solution)/shard_map/ppermute | solution.py:714
  147.2 35.0 %collective-permute-start.17 = (bf16[256,1024]{0,1:T(8,128)(2,1)}, bf16[256,1024]{0,1:T(8,128)(2,1)}, u32[]{:S(2)}, u32[]{:S(2)}) collective-permute-start(bf16[256,1024]{0,1:T(8,128)(2,1)} %slice.400), channel_id=1, source_target_pairs={{0,4},{4,0},{1,5},{5,1},{2,6},{6,2},{3,7},{7,3},{8,12},{12,8},{9,1... | collective-permute-start | bytes 1572872 | tf_op jit(solution)/shard_map/ppermute | solution.py:714
  149.8 32.4 %collective-permute-start.18 = (bf16[256,1024]{0,1:T(8,128)(2,1)}, bf16[256,1024]{0,1:T(8,128)(2,1)}, u32[]{:S(2)}, u32[]{:S(2)}) collective-permute-start(bf16[256,1024]{0,1:T(8,128)(2,1)} %slice.401), channel_id=1, source_target_pairs={{0,16},{8,24},{16,0},{24,8},{1,17},{9,25},{17,1},{25,9},{2,18},{10... | collective-permute-start | bytes 1572872 | tf_op jit(solution)/shard_map/ppermute | solution.py:714
  151.3 5.3 copy-start.20
  156.9 31.8 %collective-permute-start.7 = (bf16[512,1024]{0,1:T(8,128)(2,1)S(1)}, bf16[512,1024]{0,1:T(8,128)(2,1)S(1)}, u32[]{:S(2)}, u32[]{:S(2)}) collective-permute-start(bf16[512,1024]{0,1:T(8,128)(2,1)S(1)} %multiply_convert_fusion.1), channel_id=1, source_target_pairs={{0,16},{8,24},{16,0},{24,8},{1,17},{9,25},{17,1},{25,9},{2,18},{10... | collective-permute-start | bytes 3145736 | tf_op jit(solution)/shard_map/ppermute | solution.py:714
  157.7 31.9 %collective-permute-start.9 = (bf16[512,1024]{0,1:T(8,128)(2,1)S(1)}, bf16[512,1024]{0,1:T(8,128)(2,1)S(1)}, u32[]{:S(2)}, u32[]{:S(2)}) collective-permute-start(bf16[512,1024]{0,1:T(8,128)(2,1)S(1)} %multiply_convert_fusion.1), channel_id=1, source_target_pairs={{0,4},{4,0},{1,5},{5,1},{2,6},{6,2},{3,7},{7,3},{8,12},{12,8},{9,1... | collective-permute-start | bytes 3145736 | tf_op jit(solution)/shard_map/ppermute | solution.py:714
  161.1 21.1 %collective-permute-start.11 = (s32[1,512]{1,0:T(1,128)S(1)}, s32[1,512]{1,0:T(1,128)S(1)}, u32[]{:S(2)}, u32[]{:S(2)}) collective-permute-start(s32[1,512]{1,0:T(1,128)S(1)} %get-tuple-element.99), channel_id=1, source_target_pairs={{0,16},{8,24},{16,0},{24,8},{1,17},{9,25},{17,1},{25,9},{2,18},{10... | collective-permute-start | bytes 6152 | tf_op jit(solution)/shard_map/ppermute | solution.py:714
  188.7 36.2 %collective-permute-start.19 = (bf16[4,640,1024]{2,1,0:T(8,128)(2,1)}, bf16[4,640,1024]{2,1,0:T(8,128)(2,1)}, u32[]{:S(2)}, u32[]{:S(2)}) collective-permute-start(bf16[4,640,1024]{2,1,0:T(8,128)(2,1)} %get-tuple-element.66), channel_id=1, source_target_pairs={{0,8},{8,0},{16,24},{24,16},{1,9},{9,1},{17,25},{25,17},{2,10},{10... | collective-permute-start | bytes 15728648 | tf_op jit(solution)/shard_map/ppermute | solution.py:714
  188.8 14.4 %collective-permute-start.12 = (bf16[256,1024]{0,1:T(8,128)(2,1)S(1)}, bf16[256,1024]{0,1:T(8,128)(2,1)S(1)}, u32[]{:S(2)}, u32[]{:S(2)}) collective-permute-start(bf16[256,1024]{0,1:T(8,128)(2,1)S(1)} %slice.397), channel_id=1, source_target_pairs={{0,4},{4,0},{1,5},{5,1},{2,6},{6,2},{3,7},{7,3},{8,12},{12,8},{9,1... | collective-permute-start | bytes 1572872 | tf_op jit(solution)/shard_map/ppermute | solution.py:714
  189.7 14.1 %collective-permute-start.13 = (bf16[256,1024]{0,1:T(8,128)(2,1)S(1)}, bf16[256,1024]{0,1:T(8,128)(2,1)S(1)}, u32[]{:S(2)}, u32[]{:S(2)}) collective-permute-start(bf16[256,1024]{0,1:T(8,128)(2,1)S(1)} %slice.398), channel_id=1, source_target_pairs={{0,16},{8,24},{16,0},{24,8},{1,17},{9,25},{17,1},{25,9},{2,18},{10... | collective-permute-start | bytes 1572872 | tf_op jit(solution)/shard_map/ppermute | solution.py:714
  204.7 4.5 copy-start.27
  209.1 34.4 %collective-permute-start.14 = (bf16[4,640,1024]{2,1,0:T(8,128)(2,1)}, bf16[4,640,1024]{2,1,0:T(8,128)(2,1)}, u32[]{:S(2)}, u32[]{:S(2)}) collective-permute-start(bf16[4,640,1024]{2,1,0:T(8,128)(2,1)} %get-tuple-element.68), channel_id=1, source_target_pairs={{0,8},{8,0},{16,24},{24,16},{1,9},{9,1},{17,25},{25,17},{2,10},{10... | collective-permute-start | bytes 15728648 | tf_op jit(solution)/shard_map/ppermute | solution.py:714
  316.4 59.5 %collective-permute-start.21 = (bf16[1280,1024]{1,0:T(8,128)(2,1)}, bf16[1280,1024]{1,0:T(8,128)(2,1)}, u32[]{:S(2)}, u32[]{:S(2)}) collective-permute-start(bf16[1280,1024]{1,0:T(8,128)(2,1)} %slice.330), channel_id=1, source_target_pairs={{0,8},{8,0},{16,24},{24,16},{1,9},{9,1},{17,25},{25,17},{2,10},{10... | collective-permute-start | bytes 7864328 | tf_op jit(solution)/shard_map/ppermute | solution.py:714
  367.8 6.3 slice-start.1
  369.9 4.1 slice-start.2
  369.9 10.9 %collective-permute-start.20 = (bf16[1280,1024]{1,0:T(8,128)(2,1)S(1)}, bf16[1280,1024]{1,0:T(8,128)(2,1)}, u32[]{:S(2)}, u32[]{:S(2)}) collective-permute-start(bf16[1280,1024]{1,0:T(8,128)(2,1)S(1)} %slice.321), channel_id=1, source_target_pairs={{0,8},{8,0},{16,24},{24,16},{1,9},{9,1},{17,25},{25,17},{2,10},{10... | collective-permute-start | bytes 7864328 | tf_op jit(solution)/shard_map/ppermute | solution.py:714
  373.6 25.6 %collective-permute-start.26 = (bf16[1280,1152]{1,0:T(8,128)(2,1)}, bf16[1280,1152]{1,0:T(8,128)(2,1)S(1)}, u32[]{:S(2)}, u32[]{:S(2)}) collective-permute-start(bf16[1280,1152]{1,0:T(8,128)(2,1)} %slice.357), channel_id=1, source_target_pairs={{0,8},{8,0},{16,24},{24,16},{1,9},{9,1},{17,25},{25,17},{2,10},{10... | collective-permute-start | bytes 8847368 | tf_op jit(solution)/shard_map/ppermute | solution.py:714
  375.9 18.1 %collective-permute-start.27 = (bf16[1280,1152]{1,0:T(8,128)(2,1)}, bf16[1280,1152]{1,0:T(8,128)(2,1)}, u32[]{:S(2)}, u32[]{:S(2)}) collective-permute-start(bf16[1280,1152]{1,0:T(8,128)(2,1)} %slice.360), channel_id=1, source_target_pairs={{0,8},{8,0},{16,24},{24,16},{1,9},{9,1},{17,25},{25,17},{2,10},{10... | collective-permute-start | bytes 8847368 | tf_op jit(solution)/shard_map/ppermute | solution.py:714
  388.2 26.2 %collective-permute-start.24 = (bf16[2,256,1024]{1,2,0:T(8,128)(2,1)}, bf16[2,256,1024]{1,2,0:T(8,128)(2,1)S(1)}, u32[]{:S(2)}, u32[]{:S(2)}) collective-permute-start(bf16[2,256,1024]{1,2,0:T(8,128)(2,1)} %pad_maximum_fusion.11), channel_id=1, source_target_pairs={{0,4},{4,0},{1,5},{5,1},{2,6},{6,2},{3,7},{7,3},{8,12},{12,8},{9,1... | collective-permute-start | bytes 3145736 | tf_op jit(solution)/shard_map/ppermute | solution.py:714
  392.0 26.3 %collective-permute-start.22 = (bf16[2,256,1024]{1,2,0:T(8,128)(2,1)}, bf16[2,256,1024]{1,2,0:T(8,128)(2,1)S(1)}, u32[]{:S(2)}, u32[]{:S(2)}) collective-permute-start(bf16[2,256,1024]{1,2,0:T(8,128)(2,1)} %pad_maximum_fusion.10), channel_id=1, source_target_pairs={{0,16},{8,24},{16,0},{24,8},{1,17},{9,25},{17,1},{25,9},{2,18},{10... | collective-permute-start | bytes 3145736 | tf_op jit(solution)/shard_map/ppermute | solution.py:714
  401.9 37.8 %collective-permute-start.30 = (bf16[2,256,1152]{1,2,0:T(8,128)(2,1)S(1)}, bf16[2,256,1152]{1,2,0:T(8,128)(2,1)S(1)}, u32[]{:S(2)}, u32[]{:S(2)}) collective-permute-start(bf16[2,256,1152]{1,2,0:T(8,128)(2,1)S(1)} %pad_maximum_fusion.8), channel_id=1, source_target_pairs={{0,4},{4,0},{1,5},{5,1},{2,6},{6,2},{3,7},{7,3},{8,12},{12,8},{9,1... | collective-permute-start | bytes 3538952 | tf_op jit(solution)/shard_map/ppermute | solution.py:714
  404.4 39.1 %collective-permute-start.28 = (bf16[2,256,1152]{1,2,0:T(8,128)(2,1)S(1)}, bf16[2,256,1152]{1,2,0:T(8,128)(2,1)S(1)}, u32[]{:S(2)}, u32[]{:S(2)}) collective-permute-start(bf16[2,256,1152]{1,2,0:T(8,128)(2,1)S(1)} %pad_maximum_fusion.7), channel_id=1, source_target_pairs={{0,16},{8,24},{16,0},{24,8},{1,17},{9,25},{17,1},{25,9},{2,18},{10... | collective-permute-start | bytes 3538952 | tf_op jit(solution)/shard_map/ppermute | solution.py:714
  414.7 40.1 %collective-permute-start.25 = (bf16[256,1024]{0,1:T(8,128)(2,1)S(1)}, bf16[256,1024]{0,1:T(8,128)(2,1)S(1)}, u32[]{:S(2)}, u32[]{:S(2)}) collective-permute-start(bf16[256,1024]{0,1:T(8,128)(2,1)S(1)} %fusion.33), channel_id=1, source_target_pairs={{0,16},{8,24},{16,0},{24,8},{1,17},{9,25},{17,1},{25,9},{2,18},{10... | collective-permute-start | bytes 1572872 | tf_op jit(solution)/shard_map/ppermute | solution.py:714
  418.6 36.2 %collective-permute-start.23 = (bf16[256,1024]{0,1:T(8,128)(2,1)S(1)}, bf16[256,1024]{0,1:T(8,128)(2,1)S(1)}, u32[]{:S(2)}, u32[]{:S(2)}) collective-permute-start(bf16[256,1024]{0,1:T(8,128)(2,1)S(1)} %fusion.37), channel_id=1, source_target_pairs={{0,4},{4,0},{1,5},{5,1},{2,6},{6,2},{3,7},{7,3},{8,12},{12,8},{9,1... | collective-permute-start | bytes 1572872 | tf_op jit(solution)/shard_map/ppermute | solution.py:714
  440.0 26.2 %collective-permute-start.31 = (bf16[256,1152]{0,1:T(8,128)(2,1)S(1)}, bf16[256,1152]{0,1:T(8,128)(2,1)S(1)}, u32[]{:S(2)}, u32[]{:S(2)}) collective-permute-start(bf16[256,1152]{0,1:T(8,128)(2,1)S(1)} %fusion.25), channel_id=1, source_target_pairs={{0,16},{8,24},{16,0},{24,8},{1,17},{9,25},{17,1},{25,9},{2,18},{10... | collective-permute-start | bytes 1769480 | tf_op jit(solution)/shard_map/ppermute | solution.py:714
  444.0 22.3 %collective-permute-start.29 = (bf16[256,1152]{0,1:T(8,128)(2,1)S(1)}, bf16[256,1152]{0,1:T(8,128)(2,1)S(1)}, u32[]{:S(2)}, u32[]{:S(2)}) collective-permute-start(bf16[256,1152]{0,1:T(8,128)(2,1)S(1)} %fusion.29), channel_id=1, source_target_pairs={{0,4},{4,0},{1,5},{5,1},{2,6},{6,2},{3,7},{7,3},{8,12},{12,8},{9,1... | collective-permute-start | bytes 1769480 | tf_op jit(solution)/shard_map/ppermute | solution.py:714
  478.6 250.0 %reduce-scatter.9.cloned.1.call-start = ((), (), s32[]{:S(2)}) async-start(), calls=%async_computation.12 | async-start | bytes 5406720 | tf_op jit(solution)/shard_map/reduce_scatter | solution.py:901
  479.4 289.2 %reduce-scatter.11.cloned.1.call-start = ((), (), s32[]{:S(2)}) async-start(), calls=%async_computation.13 | async-start | bytes 5406720 | tf_op jit(solution)/shard_map/reduce_scatter | solution.py:901
  485.7 33.9 %all-to-all-start.2 = ((bf16[4,256,256]{2,1,0:T(8,128)(2,1)}), bf16[4,256,256]{2,1,0:T(8,128)(2,1)S(1)}, u32[]{:S(2)}, u32[]{:S(2)}) async-start(bf16[4,256,256]{2,1,0:T(8,128)(2,1)} %bitcast.80), calls=%async_computation.2 | async-start | bytes 1048576 | tf_op jit(solution)/shard_map/all_to_all | solution.py:931
  519.6 26.6 %all-to-all-start.4 = ((bf16[4,256,256]{2,1,0:T(8,128)(2,1)}), bf16[4,256,256]{2,1,0:T(8,128)(2,1)S(1)}, u32[]{:S(2)}, u32[]{:S(2)}) async-start(bf16[4,256,256]{2,1,0:T(8,128)(2,1)} %bitcast.84), calls=%async_computation.4 | async-start | bytes 1048576 | tf_op jit(solution)/shard_map/all_to_all | solution.py:931
  546.1 5.3 copy-start.11
  546.2 82.8 %all-to-all-start.3 = ((bf16[4,256,768]{2,1,0:T(8,128)(2,1)}), bf16[4,256,768]{2,1,0:T(8,128)(2,1)S(1)}, u32[]{:S(2)}, u32[]{:S(2)}) async-start(bf16[4,256,768]{2,1,0:T(8,128)(2,1)} %get-tuple-element.36), calls=%async_computation.3 | async-start | bytes 3145728 | tf_op jit(solution)/shard_map/all_to_all | solution.py:937
  575.0 58.5 %copy-start.32 = (f32[1,2,2,128]{3,2,1,0:T(2,128)S(1)}, f32[1,2,2,128]{3,2,1,0:T(2,128)}, u32[]{:S(2)}) copy-start(f32[1,2,2,128]{3,2,1,0:T(2,128)} %get-tuple-element.100) | copy-start | bytes 6148
  628.9 85.8 %all-to-all-start.5 = ((bf16[4,256,768]{2,1,0:T(8,128)(2,1)}), bf16[4,256,768]{2,1,0:T(8,128)(2,1)}, u32[]{:S(2)}, u32[]{:S(2)}) async-start(bf16[4,256,768]{2,1,0:T(8,128)(2,1)} %get-tuple-element.39), calls=%async_computation.5 | async-start | bytes 3145728 | tf_op jit(solution)/shard_map/all_to_all | solution.py:937
  633.3 180.4 %reduce-scatter.7.cloned.1.call-start = ((), (), s32[]{:S(2)}) async-start(), calls=%async_computation.11 | async-start | bytes 2359296 | tf_op jit(solution)/shard_map/reduce_scatter | solution.py:952
  640.6 4.1 copy-start.16
  640.6 4.1 copy-start.26
  640.6 4.1 copy-start.38
  717.5 6.8 copy-start.6
  768.6 46.9 %copy-start.1 = (f32[16,32]{1,0:T(8,128)S(1)}, f32[16,32]{1,0:T(8,128)}, u32[]{:S(2)}) copy-start(f32[16,32]{1,0:T(8,128)} %param.20) | copy-start | bytes 6148
  (22 other events, 51.2 us)
Sparse Core Ops, SparseCore 0:
  478.7 57.0 reduce-scatter.4
  538.3 127.5 reduce-scatter.8
  668.3 100.2 reduce-scatter.10
  772.1 41.6 reduce-scatter.6

commit v2 on v1

--- a/solution.py
+++ b/solution.py
@@ -364,6 +364,10 @@
 vmem_bytes = 56 * 1024 * 1024
 
 
+def cost(flops, moved):
+    return pl.CostEstimate(flops=int(flops), bytes_accessed=int(moved), transcendentals=0)
+
+
 def compiler_params():
     return pltpu.CompilerParams(vmem_limit_bytes=vmem_bytes)
 
@@ -380,28 +384,6 @@
     return values
 
 
-def bias_kernel(line_ref, bias_ref):
-    rows, columns = bias_ref.shape[1], bias_ref.shape[2]
-    lanes = rows + columns
-    line = pltpu.roll(line_ref[0], lanes - (rows - 1), 1)
-    full = jnp.broadcast_to(line, (rows, lanes))
-    bias_ref[0] = shear(full, False)[:, :columns]
-
-
-def make_bias(lines, span_rows):
-    heads, _, lanes = lines.shape
-    columns = lanes - span_rows
-    return pl.pallas_call(
-        bias_kernel,
-        grid=(heads,),
-        in_specs=[pl.BlockSpec((1, 1, lanes), lambda h: (h, 0, 0))],
-        out_specs=pl.BlockSpec((1, span_rows, columns), lambda h: (h, 0, 0)),
-        out_shape=jax.ShapeDtypeStruct((heads, span_rows, columns), jnp.float32),
-        compiler_params=compiler_params(),
-        name="bias_planes",
-    )(lines)
-
-
 def dot_nt(left, right):
     return lax.dot_general(
         left, right, (((1,), (1,)), ((), ())), preferred_element_type=jnp.float32
@@ -416,6 +398,76 @@
 
 def dot_nn(left, right):
     return jnp.dot(left, right, preferred_element_type=jnp.float32)
+
+
+def gather_kernel(normed_ref, weight_ref, line_ref, all_ref, qkv_ref, bias_ref, send_sem, recv_sem):
+    slots, count, span_rows, _ = all_ref.shape
+    mine = lax.axis_index("cp")
+    right, left = lax.rem(mine + 1, count), lax.rem(mine + count - 1, count)
+    barrier = pltpu.get_barrier_semaphore()
+    for near in (left, right):
+        pl.semaphore_signal(
+            barrier, inc=1, device_id={"cp": near}, device_id_type=pl.DeviceIdType.MESH
+        )
+    pl.semaphore_wait(barrier, 2)
+
+    def copy(slot, hop):
+        return pltpu.make_async_remote_copy(
+            src_ref=normed_ref.at[slot] if hop == 0 else all_ref.at[slot, hop],
+            dst_ref=all_ref.at[slot, hop + 1],
+            send_sem=send_sem.at[slot, hop],
+            recv_sem=recv_sem.at[slot, hop],
+            device_id={"cp": right},
+            device_id_type=pl.DeviceIdType.MESH,
+        )
+
+    for slot in range(slots):
+        copy(slot, 0).start()
+    for slot in range(slots):
+        rows = normed_ref[slot]
+        all_ref[slot, 0] = rows
+        qkv_ref[slot, 0] = dot_nn(rows, weight_ref[...]).astype(jnp.bfloat16)
+    columns = bias_ref.shape[2]
+    lanes = span_rows + columns
+    for head in range(bias_ref.shape[0]):
+        line = pltpu.roll(line_ref[head], lanes - (span_rows - 1), 1)
+        full = jnp.broadcast_to(line, (span_rows, lanes))
+        bias_ref[head] = shear(full, False)[:, :columns]
+    for hop in range(1, count):
+        for slot in range(slots):
+            copy(slot, hop - 1).wait_recv()
+            if hop < count - 1:
+                copy(slot, hop).start()
+            rows = all_ref[slot, hop]
+            qkv_ref[slot, hop] = dot_nn(rows, weight_ref[...]).astype(jnp.bfloat16)
+    for hop in range(count - 1):
+        for slot in range(slots):
+            copy(slot, hop).wait_send()
+
+
+def gather_project(normed, weight, lines, count):
+    slots, span_rows, model_width = normed.shape
+    columns = lines.shape[2] - span_rows
+    whole = pl.BlockSpec(memory_space=pltpu.VMEM)
+    return pl.pallas_call(
+        gather_kernel,
+        in_specs=[whole] * 3,
+        out_specs=[whole] * 3,
+        out_shape=[
+            jax.ShapeDtypeStruct((slots, count, span_rows, model_width), jnp.bfloat16),
+            jax.ShapeDtypeStruct((slots, count, span_rows, weight.shape[1]), jnp.bfloat16),
+            jax.ShapeDtypeStruct((lines.shape[0], span_rows, columns), jnp.float32),
+        ],
+        scratch_shapes=[
+            pltpu.SemaphoreType.DMA((slots, count - 1)),
+            pltpu.SemaphoreType.DMA((slots, count - 1)),
+        ],
+        cost_estimate=cost(60e9, 20e6),
+        compiler_params=pltpu.CompilerParams(
+            vmem_limit_bytes=vmem_bytes, collective_id=0, has_side_effects=True
+        ),
+        name="gather_project",
+    )(normed, weight, lines)
 
 
 def key_masks(length, blocks, span_rows):
@@ -429,7 +481,7 @@
 def forward_kernel(
     scale, head_size, meta_ref, q_ref, k_ref, v_ref, bias_ref, low_ref, full_ref, total_ref
 ):
-    blocks, span_rows, lanes = q_ref.shape
+    _, blocks, span_rows, lanes = q_ref.shape
     mine, length = meta_ref[0], meta_ref[1]
     lane = lax.broadcasted_iota(jnp.int32, (1, lanes), 1)
     masks = key_masks(length, blocks, span_rows)
@@ -438,7 +490,7 @@
         return lax.rem(mine - block + blocks, blocks)
 
     for row in range(blocks):
-        queries = q_ref[place(row)]
+        queries = q_ref[0, place(row)]
         totals = jnp.zeros((span_rows, lanes), jnp.float32)
         result = jnp.zeros((span_rows, lanes), jnp.float32)
         for half in range(lanes // head_size):
@@ -448,7 +500,7 @@
             logits = []
             for column in range(row + 1):
                 at = (blocks - 1 - row + column) * span_rows
-                part = dot_nt(head_q, k_ref[place(column)])
+                part = dot_nt(head_q, k_ref[0, place(column)])
                 part = part + bias_ref[half, :, at : at + span_rows] + masks[column]
                 logits.append(part)
             peak = jnp.max(logits[0], axis=1, keepdims=True)
@@ -460,22 +512,22 @@
                 weights = jnp.exp(logits[column] - peak)
                 total = total + jnp.sum(weights, axis=1, keepdims=True)
                 mixed = mixed + dot_nn(
-                    weights.astype(jnp.bfloat16), v_ref[place(column)] * head_v
+                    weights.astype(jnp.bfloat16), v_ref[0, place(column)] * head_v
                 )
             result = result + mixed / total
             totals = jnp.where(lane == half, peak + jnp.log(total), totals)
-        low_ref[row] = result.astype(jnp.bfloat16)
+        low_ref[place(row)] = result.astype(jnp.bfloat16)
         full_ref[row] = result
         total_ref[row] = totals
 
 
-def attend_forward(meta, qkv, bias, scale, head_size):
-    blocks, span_rows, width = qkv.shape
+def attend_forward(meta, slot, qkv, bias, scale, head_size):
+    _, blocks, span_rows, width = qkv.shape
     pairs = width // (3 * 128)
     per_pair = bias.shape[0] // pairs
 
     def part(which):
-        return pl.BlockSpec((blocks, span_rows, 128), lambda p, which=which: (0, 0, 3 * p + which))
+        return pl.BlockSpec((1, blocks, span_rows, 128), lambda p: (slot, 0, 0, 3 * p + which))
 
     plain = pl.BlockSpec((blocks, span_rows, 128), lambda p: (0, 0, p))
 
@@ -495,6 +547,7 @@
             jax.ShapeDtypeStruct((blocks, span_rows, pairs * 128), jnp.float32),
             jax.ShapeDtypeStruct((blocks, span_rows, pairs * 128), jnp.float32),
         ],
+        cost_estimate=cost(8e9, 8e6),
         compiler_params=compiler_params(),
         name="attend_forward",
     )(meta, qkv, qkv, qkv, bias)
@@ -511,14 +564,13 @@
     grad_ref,
     full_ref,
     total_ref,
-    sent_ref,
     ring_ref,
     line_ref,
     key_sum,
     value_sum,
     plane,
 ):
-    blocks, span_rows, lanes = q_ref.shape
+    _, blocks, span_rows, lanes = q_ref.shape
     mine, length = meta_ref[0], meta_ref[1]
     lane = lax.broadcasted_iota(jnp.int32, (1, lanes), 1)
     masks = key_masks(length, blocks, span_rows)
@@ -531,8 +583,8 @@
     value_sum[...] = jnp.zeros_like(value_sum)
     plane[...] = jnp.zeros_like(plane)
     for row in range(blocks):
-        queries = q_ref[place(row)]
-        grads = grad_ref[row]
+        queries = q_ref[0, place(row)]
+        grads = grad_ref[lax.rem(row - mine + blocks, blocks)]
         products = grads.astype(jnp.float32) * full_ref[row]
         totals = total_ref[row]
         query_sum = jnp.zeros((span_rows, lanes), jnp.float32)
@@ -545,11 +597,11 @@
             total = totals[:, half : half + 1]
             for column in range(row + 1):
                 at = (blocks - 1 - row + column) * span_rows
-                keys = k_ref[place(column)]
+                keys = k_ref[0, place(column)]
                 logits = dot_nt(head_q, keys)
                 logits = logits + bias_ref[half, :, at : at + span_rows] + masks[column]
                 weights = jnp.exp(logits - total)
-                weight_grads = dot_nt(head_g, v_ref[place(column)])
+                weight_grads = dot_nt(head_g, v_ref[0, place(column)])
                 score_grads = weights * (weight_grads - delta)
                 plane[half, :, at : at + span_rows] += score_grads
                 low_weights = weights.astype(jnp.bfloat16)
@@ -558,14 +610,11 @@
                 key_sum[column] += dot_tn(low_grads, head_q)
                 value_sum[column] += dot_tn(low_weights, head_g)
         result = (query_sum * scale).astype(jnp.bfloat16)
-        sent_ref[row, :, :lanes] = result
         ring_ref[place(row), :, :lanes] = result
     for row in range(blocks):
         result = key_sum[row].astype(jnp.bfloat16)
-        sent_ref[row, :, lanes : 2 * lanes] = result
         ring_ref[place(row), :, lanes : 2 * lanes] = result
         result = value_sum[row].astype(jnp.bfloat16)
-        sent_ref[row, :, 2 * lanes :] = result
         ring_ref[place(row), :, 2 * lanes :] = result
     for half in range(halves):
         full = jnp.concatenate(
@@ -575,14 +624,14 @@
         line_ref[half] = pltpu.roll(summed, span_rows - 1, 1)
 
 
-def attend_backward(meta, qkv, bias, grads, full, totals, scale, head_size):
-    blocks, span_rows, width = qkv.shape
+def attend_backward(meta, slot, qkv, bias, grads, full, totals, scale, head_size):
+    _, blocks, span_rows, width = qkv.shape
     pairs = width // (3 * 128)
     per_pair = bias.shape[0] // pairs
     lanes = bias.shape[2] + span_rows
 
     def part(which):
-        return pl.BlockSpec((blocks, span_rows, 128), lambda p, which=which: (0, 0, 3 * p + which))
+        return pl.BlockSpec((1, blocks, span_rows, 128), lambda p: (slot, 0, 0, 3 * p + which))
 
     plain = pl.BlockSpec((blocks, span_rows, 128), lambda p: (0, 0, p))
     wide = pl.BlockSpec((blocks, span_rows, 384), lambda p: (0, 0, p))
@@ -599,10 +648,9 @@
             plain,
             plain,
         ],
-        out_specs=[wide, wide, pl.BlockSpec((per_pair, 1, lanes), lambda p: (p, 0, 0))],
+        out_specs=[wide, pl.BlockSpec((per_pair, 1, lanes), lambda p: (p, 0, 0))],
         out_shape=[
-            jax.ShapeDtypeStruct(qkv.shape, jnp.bfloat16),
-            jax.ShapeDtypeStruct(qkv.shape, jnp.bfloat16),
+            jax.ShapeDtypeStruct(qkv.shape[1:], jnp.bfloat16),
             jax.ShapeDtypeStruct((bias.shape[0], 1, lanes), jnp.float32),
         ],
         scratch_shapes=[
@@ -610,108 +658,408 @@
             pltpu.VMEM((blocks, span_rows, 128), jnp.float32),
             pltpu.VMEM((per_pair,) + bias.shape[1:], jnp.float32),
         ],
+        cost_estimate=cost(20e9, 12e6),
         compiler_params=compiler_params(),
         name="attend_backward",
     )(meta, qkv, qkv, qkv, bias, grads, full, totals)
 
 
+def own_rows(meta_ref, span_rows):
+    position = meta_ref[0] * span_rows + lax.broadcasted_iota(jnp.int32, (span_rows, 1), 0)
+    return jnp.where(position < meta_ref[1], 1.0, 0.0)
+
+
+def router_of(rows, router_w, experts):
+    lane = lax.broadcasted_iota(jnp.int32, (1, router_w.shape[1]), 1)
+    logits = jnp.where(lane < experts, dot_nn(rows, router_w), minus_big)
+    shares = jnp.exp(logits - jnp.max(logits, axis=1, keepdims=True))
+    return shares / jnp.sum(shares, axis=1, keepdims=True)
+
+
+def project_kernel(meta_ref, input_ref, gain_ref, weight_ref, *refs):
+    attended_ref, hidden_ref, normed_ref = refs[-3:]
+    parts = refs[:-3]
+    count = len(parts)
+    for j, part in enumerate(parts):
+        owner = lax.rem(meta_ref[0] + j, count)
+        for group in range(part.shape[1] // 128):
+            at = pl.multiple_of((group * count + owner) * 128, 128)
+            attended_ref[:, pl.ds(at, 128)] = part[:, group * 128 : (group + 1) * 128]
+    projected = dot_nn(attended_ref[...], weight_ref[...])
+    hidden = input_ref[...].astype(jnp.float32) + own_rows(meta_ref, projected.shape[0]) * projected
+    hidden_ref[...] = hidden
+    normed_ref[...] = (hidden * root_scale(hidden) * gain_ref[...]).astype(jnp.bfloat16)
+
+
+def project_rows(meta, inputs, gain, w_attn, parts):
+    span_rows, model_width = inputs.shape
+    whole = pl.BlockSpec(memory_space=pltpu.VMEM)
+    return pl.pallas_call(
+        project_kernel,
+        grid=(1,),
+        in_specs=[
+            pl.BlockSpec(memory_space=pltpu.SMEM),
+            whole,
+            whole,
+            pl.BlockSpec((model_width, model_width), lambda i: (0, 3)),
+        ]
+        + [whole] * len(parts),
+        out_specs=[whole] * 3,
+        out_shape=[
+            jax.ShapeDtypeStruct((span_rows, model_width), jnp.bfloat16),
+            jax.ShapeDtypeStruct((span_rows, model_width), jnp.float32),
+            jax.ShapeDtypeStruct((span_rows, model_width), jnp.bfloat16),
+        ],
+        cost_estimate=cost(2e9, 6e6),
+        compiler_params=compiler_params(),
+        name="project_rows",
+    )(meta, inputs, gain, w_attn, *parts)
+
+
+def hidden_kernel(
+    experts,
+    meta_ref,
+    own_ref,
+    first_ref,
+    last_ref,
+    grad_ref,
+    hidden_ref,
+    normed_ref,
+    gain_ref,
+    router_ref,
+    weight_ref,
+    *refs,
+):
+    hidden_grad_ref, proj_ref, router_grad_ref, gain_grad_ref = refs[:4]
+    leaving, attended = refs[4:-1], refs[-1]
+    count = len(leaving)
+    span_rows, model_width = hidden_ref.shape
+    back = (
+        own_ref[...].astype(jnp.float32)
+        + first_ref[...].astype(jnp.float32)
+        + last_ref[...].astype(jnp.float32)
+    )
+    normed = normed_ref[...]
+    probs = router_of(normed, router_ref[...], experts)
+    shares = back[:, model_width:]
+    logit_grads = probs * (shares - jnp.sum(probs * shares, axis=1, keepdims=True))
+    logit_grads = logit_grads.astype(jnp.bfloat16)
+    router_grad_ref[...] = dot_tn(normed, logit_grads)
+    grads = back[:, :model_width] + dot_nt(logit_grads, router_ref[...])
+    hidden = hidden_ref[...]
+    scale_rows = root_scale(hidden)
+    gain_grad_ref[...] = jnp.sum(grads * hidden * scale_rows, axis=0, keepdims=True)
+    hidden_grads = grad_ref[...].astype(jnp.float32) + norm_back(
+        grads, hidden, scale_rows, gain_ref[...]
+    )
+    hidden_grad_ref[...] = hidden_grads
+    proj = (own_rows(meta_ref, span_rows) * hidden_grads).astype(jnp.bfloat16)
+    proj_ref[...] = proj
+    attended[...] = dot_nt(proj, weight_ref[...]).astype(jnp.bfloat16)
+    for j, part in enumerate(leaving):
+        owner = lax.rem(meta_ref[0] + (count - j), count)
+        for group in range(part.shape[1] // 128):
+            at = pl.multiple_of((group * count + owner) * 128, 128)
+            part[:, group * 128 : (group + 1) * 128] = attended[:, pl.ds(at, 128)]
+
+
+def hidden_back(meta, own, first, last, grads, hidden, normed, gain, router, w_attn, experts, count):
+    span_rows, model_width = hidden.shape
+    whole = pl.BlockSpec(memory_space=pltpu.VMEM)
+    f32, bf16 = jnp.float32, jnp.bfloat16
+    return pl.pallas_call(
+        functools.partial(hidden_kernel, experts),
+        grid=(1,),
+        in_specs=[pl.BlockSpec(memory_space=pltpu.SMEM)]
+        + [whole] * 8
+        + [pl.BlockSpec((model_width, model_width), lambda i: (0, 3))],
+        out_specs=[whole] * (4 + count),
+        out_shape=[
+            jax.ShapeDtypeStruct((span_rows, model_width), f32),
+            jax.ShapeDtypeStruct((span_rows, model_width), bf16),
+            jax.ShapeDtypeStruct((model_width, router.shape[1]), f32),
+            jax.ShapeDtypeStruct((1, model_width), f32),
+        ]
+        + [jax.ShapeDtypeStruct((span_rows, model_width // count), bf16)] * count,
+        scratch_shapes=[pltpu.VMEM((span_rows, model_width), bf16)],
+        cost_estimate=cost(3e9, 8e6),
+        compiler_params=compiler_params(),
+        name="hidden_back",
+    )(meta, own, first, last, grads, hidden, normed, gain, router, w_attn)
+
+
+def token_kernel(meta_ref, input_ref, hidden_ref, gain_ref, weight_ref, *refs):
+    parts, out_ref = refs[:-1], refs[-1]
+    count = len(parts)
+    model_width = input_ref.shape[1]
+    total = None
+    for j, part in enumerate(parts):
+        owner = lax.rem(meta_ref[0] + j, count)
+        pieces = []
+        for group in range(part.shape[1] // 384):
+            for which in range(3):
+                at = which * model_width + (group * count + owner) * 128
+                pieces.append(weight_ref[:, pl.ds(pl.multiple_of(at, 128), 128)])
+        term = dot_nt(part[...], jnp.concatenate(pieces, axis=1))
+        total = term if total is None else total + term
+    inputs = input_ref[...].astype(jnp.float32)
+    back = norm_back(total, inputs, root_scale(inputs), gain_ref[...])
+    out_ref[...] = (hidden_ref[...] + back).astype(jnp.bfloat16)
+
+
+def token_grads(meta, inputs, hidden_grads, gain, w_attn, parts):
+    span_rows, model_width = inputs.shape
+    whole = pl.BlockSpec(memory_space=pltpu.VMEM)
+    return pl.pallas_call(
+        token_kernel,
+        grid=(1,),
+        in_specs=[
+            pl.BlockSpec(memory_space=pltpu.SMEM),
+            whole,
+            whole,
+            whole,
+            pl.BlockSpec((model_width, 3 * model_width), lambda i: (0, 0)),
+        ]
+        + [whole] * len(parts),
+        out_specs=whole,
+        out_shape=jax.ShapeDtypeStruct((span_rows, model_width), jnp.bfloat16),
+        cost_estimate=cost(4e9, 8e6),
+        compiler_params=compiler_params(),
+        name="token_grads",
+    )(meta, inputs, hidden_grads, gain, w_attn, *parts)
+
+
 gelu_inner = 0.7978845608028654
 gelu_cubic = 0.044715
 
 
+def pick_kernel(base_ref, target_ref, *refs):
+    out_ref = refs[-1]
+    sources, experts, capacity, _ = out_ref.shape
+    parts = (len(refs) - 1) // sources
+    for source in range(sources):
+        for expert in range(experts):
+            picked = None
+            for at in range(parts):
+                part = refs[source * parts + at]
+                span = part.shape[0]
+                ids = lax.broadcasted_iota(jnp.int32, (capacity, span), 0)
+                ids = ids + (base_ref[0] + expert * capacity)
+                hot = jnp.zeros((capacity, span), jnp.float32)
+                for choice in range(target_ref.shape[1]):
+                    chosen = target_ref[source, choice : choice + 1, at * span : (at + 1) * span]
+                    hot = hot + jnp.where(ids == chosen, 1.0, 0.0)
+                term = dot_nn(hot.astype(jnp.bfloat16), part[...])
+                picked = term if picked is None else picked + term
+            out_ref[source, expert] = picked.astype(jnp.bfloat16)
+
+
+def pick_rows(base, targets, blocks, experts, capacity):
+    flat = [part for parts in blocks for part in parts]
+    width = flat[0].shape[1]
+    whole = pl.BlockSpec(memory_space=pltpu.VMEM)
+    return pl.pallas_call(
+        pick_kernel,
+        in_specs=[pl.BlockSpec(memory_space=pltpu.SMEM)] + [whole] * (1 + len(flat)),
+        out_specs=whole,
+        out_shape=jax.ShapeDtypeStruct((len(blocks), experts, capacity, width), jnp.bfloat16),
+        cost_estimate=cost(1.6e9 * len(blocks), 3e6 * len(blocks)),
+        compiler_params=compiler_params(),
+        name="pick_rows",
+    )(base, targets, *flat)
+
+
+def place_kernel(base_ref, target_ref, mine_ref, theirs_ref, *out_refs):
+    sources, experts, capacity, _ = mine_ref.shape
+    parts = len(out_refs) // sources
+    span = out_refs[0].shape[0]
+    for source in range(sources):
+        both = [
+            (
+                mine_ref[source, expert].astype(jnp.float32)
+                + theirs_ref[source, expert].astype(jnp.float32)
+            ).astype(jnp.bfloat16)
+            for expert in range(experts)
+        ]
+        for at in range(parts):
+            total = None
+            for expert in range(experts):
+                ids = lax.broadcasted_iota(jnp.int32, (span, capacity), 1)
+                ids = ids + (base_ref[0] + expert * capacity)
+                hot = jnp.zeros((span, capacity), jnp.float32)
+                for choice in range(target_ref.shape[2]):
+                    chosen = target_ref[source, at * span : (at + 1) * span, choice : choice + 1]
+                    hot = hot + jnp.where(ids == chosen, 1.0, 0.0)
+                term = dot_nn(hot.astype(jnp.bfloat16), both[expert])
+                total = term if total is None else total + term
+            out_refs[source * parts + at][...] = total.astype(jnp.bfloat16)
+
+
+def place_rows(base, targets, mine, theirs, parts):
+    sources, experts, capacity, width = mine.shape
+    span = targets.shape[1] // parts
+    whole = pl.BlockSpec(memory_space=pltpu.VMEM)
+    return pl.pallas_call(
+        place_kernel,
+        in_specs=[pl.BlockSpec(memory_space=pltpu.SMEM), whole, whole, whole],
+        out_specs=[whole] * (sources * parts),
+        out_shape=[jax.ShapeDtypeStruct((span, width), jnp.bfloat16)] * (sources * parts),
+        cost_estimate=cost(1.6e9 * sources, 4e6 * sources),
+        compiler_params=compiler_params(),
+        name="place_rows",
+    )(base, targets, mine, theirs)
+
+
 def expert_kernel(
     experts,
-    expert_ref,
-    rows_ref,
-    grads_ref,
+    own_units,
+    kept_count,
+    first_ref,
+    window_ref,
+    rows_mine,
+    rows_theirs,
+    grads_mine,
+    grads_theirs,
     router_ref,
     gate_ref,
     up_ref,
     down_ref,
-    back_ref,
-    out_ref,
-    weight_ref,
-    total,
+    *refs,
 ):
-    step = pl.program_id(0)
-    model_width = rows_ref.shape[1]
-    pieces, _, piece, _ = weight_ref.shape
-    rows, grads = rows_ref[...], grads_ref[...]
+    back_mine, back_theirs, out_mine, out_theirs = refs[kept_count : kept_count + 4]
+    kept_rows, kept_grads, kept_gate, kept_up, kept_inner = refs[kept_count + 4 :]
+    capacity, model_width = rows_mine.shape[2:]
+    rows = jnp.concatenate([rows_mine[0, 0], rows_theirs[0, 0]], axis=0)
+    grads = jnp.concatenate([grads_mine[0, 0], grads_theirs[0, 0]], axis=0)
+    kept_rows[0, 0] = rows
+    kept_grads[0, 0] = grads
     lane = lax.broadcasted_iota(jnp.int32, (1, router_ref.shape[1]), 1)
-    expert = expert_ref[0]
-    router = jnp.where(lane < experts, dot_nn(rows, router_ref[...]), minus_big)
-    router = jnp.exp(router - jnp.max(router, axis=1, keepdims=True))
-    gates = jnp.sum(jnp.where(lane == expert, router, 0.0), axis=1, keepdims=True) / jnp.sum(
-        router, axis=1, keepdims=True
-    )
-    gate_pre = dot_nn(rows, gate_ref[...])
-    up_pre = dot_nn(rows, up_ref[...])
+    expert = first_ref[0] + pl.program_id(0)
+    probs = router_of(rows, router_ref[...], experts)
+    gates = jnp.sum(jnp.where(lane == expert, probs, 0.0), axis=1, keepdims=True)
+    unit = lax.broadcasted_iota(jnp.int32, (1, gate_ref.shape[2]), 1) - window_ref[1]
+    own = jnp.logical_and(unit >= 0, unit < own_units)
+    gate_w, up_w, down_w = gate_ref[0], up_ref[0], down_ref[0]
+    gate_pre = dot_nn(rows, gate_w)
+    up_pre = jnp.where(own, dot_nn(rows, up_w), 0.0)
     square = gate_pre * gate_pre
     tanh = jnp.tanh(gelu_inner * gate_pre * (1.0 + gelu_cubic * square))
     half = 0.5 + 0.5 * tanh
     active = gate_pre * half
-    slope = half + active * (1.0 - tanh) * (
-        gelu_inner * (1.0 + 3.0 * gelu_cubic * square)
-    )
+    slope = half + active * (1.0 - tanh) * (gelu_inner * (1.0 + 3.0 * gelu_cubic * square))
     inner = active * up_pre
     low_inner = inner.astype(jnp.bfloat16)
-    plain_grads = dot_nn(grads, down_ref[...])
+    plain_grads = jnp.where(own, dot_nn(grads, down_w), 0.0)
     gate_grads = jnp.sum(plain_grads * low_inner.astype(jnp.float32), axis=1, keepdims=True)
     inner_grads = plain_grads * gates
     low_gate = (inner_grads * up_pre * slope).astype(jnp.bfloat16)
     low_up = (inner_grads * active).astype(jnp.bfloat16)
-    gated = (inner * gates).astype(jnp.bfloat16)
-    back = dot_nt(low_gate, gate_ref[...]) + dot_nt(low_up, up_ref[...])
-    back_ref[:, :model_width] = back.astype(jnp.bfloat16)
-    back_ref[:, model_width:] = jnp.where(lane == expert, gate_grads, 0.0).astype(jnp.bfloat16)
-    out_ref[...] = (gates * dot_nt(low_inner, down_ref[...])).astype(jnp.bfloat16)
+    kept_gate[0, 0] = low_gate
+    kept_up[0, 0] = low_up
+    kept_inner[0, 0] = (inner * gates).astype(jnp.bfloat16)
+    back = (dot_nt(low_gate, gate_w) + dot_nt(low_up, up_w)).astype(jnp.bfloat16)
+    shares = jnp.where(lane == expert, gate_grads, 0.0).astype(jnp.bfloat16)
+    out = (gates * dot_nt(low_inner, down_w)).astype(jnp.bfloat16)
+    for at, back_ref, out_ref in ((0, back_mine, out_mine), (1, back_theirs, out_theirs)):
+        part = slice(at * capacity, (at + 1) * capacity)
+        back_ref[0, 0, :, :model_width] = back[part]
+        back_ref[0, 0, :, model_width:] = shares[part]
+        out_ref[0, 0] = out[part]
+
+
+def run_experts(
+    first, window, mine, theirs, grads_mine, grads_theirs, router, weights, kept, at, total, experts, units
+):
+    sources, exp_dev, capacity, model_width = mine.shape
+    wide_units = aligned_units(units)
+    tile = 2 * capacity
+    rows = pl.BlockSpec((1, 1, capacity, model_width), lambda e, k, f, w: (k, e, 0, 0))
+    wide = pl.BlockSpec((1, 1, capacity, model_width + 128), lambda e, k, f, w: (k, e, 0, 0))
+    weight = pl.BlockSpec(
+        (pl.Element(1), pl.Element(model_width), pl.Element(wide_units)),
+        lambda e, k, f, w: (e, 0, pl.multiple_of(w[0], 128)),
+    )
+    keep = lambda width: pl.BlockSpec((1, 1, tile, width), lambda e, k, f, w: (e, at + k, 0, 0))
+    keep_widths = (model_width, model_width, wide_units, wide_units, wide_units)
+    kept = list(kept)
+    back_shape = jax.ShapeDtypeStruct((sources, exp_dev, capacity, model_width + 128), jnp.bfloat16)
+    out_shape = jax.ShapeDtypeStruct((sources, exp_dev, capacity, model_width), jnp.bfloat16)
+    got = pl.pallas_call(
+        functools.partial(expert_kernel, experts, units, len(kept)),
+        grid_spec=pltpu.PrefetchScalarGridSpec(
+            num_scalar_prefetch=2,
+            grid=(exp_dev, sources),
+            in_specs=[
+                rows,
+                rows,
+                rows,
+                rows,
+                pl.BlockSpec(router.shape, lambda e, k, f, w: (0, 0)),
+                weight,
+                weight,
+                weight,
+            ]
+            + [pl.BlockSpec(memory_space=pl.ANY)] * len(kept),
+            out_specs=[wide, wide, rows, rows] + [keep(width) for width in keep_widths],
+        ),
+        out_shape=[back_shape, back_shape, out_shape, out_shape]
+        + [jax.ShapeDtypeStruct((exp_dev, total, tile, w), jnp.bfloat16) for w in keep_widths],
+        input_output_aliases={10 + i: 4 + i for i in range(len(kept))},
+        cost_estimate=cost(20e9 * sources, 8e6 * sources),
+        compiler_params=compiler_params(),
+        name="expert_rows",
+    )(first, window, mine, theirs, grads_mine, grads_theirs, router, *weights, *kept)
+    return got[:4], got[4:]
+
+
+def aligned_units(units):
+    return (units + 127) // 128 * 128
+
+
+def weight_kernel(window_ref, rows_ref, grads_ref, gate_ref, up_ref, inner_ref, weight_ref, total):
+    step = pl.program_id(0)
+    pieces, _, piece, _ = weight_ref.shape
 
     @pl.when(step == 0)
     def _():
         total[...] = jnp.zeros_like(total)
 
-    total[0] += dot_tn(low_gate, rows)
-    total[1] += dot_tn(low_up, rows)
-    total[2] += dot_tn(gated, grads)
+    total[0] += dot_tn(gate_ref[0, 0], rows_ref[0, 0])
+    total[1] += dot_tn(up_ref[0, 0], rows_ref[0, 0])
+    total[2] += dot_tn(inner_ref[0, 0], grads_ref[0, 0])
 
     @pl.when(step == pl.num_programs(0) - 1)
     def _():
+        skip = pl.multiple_of(window_ref[1], 64)
         for at in range(pieces):
-            weight_ref[at] = total[:, at * piece : (at + 1) * piece].astype(jnp.bfloat16)
-
-
-def run_expert(expert, rows, grads, router, gate_w, up_w, down_w, experts, pieces, tile):
-    count, model_width = rows.shape
-    hidden_units = gate_w.shape[1]
-    whole = lambda shape: pl.BlockSpec(shape, lambda i: (0,) * len(shape))
-    tiled = lambda width: pl.BlockSpec((tile, width), lambda i: (i, 0))
-    grad_shape = (pieces, 3, hidden_units // pieces, model_width)
+            got = total[:, pl.ds(skip + at * piece, piece), :]
+            weight_ref[at] = got.astype(jnp.bfloat16)
+
+
+def weight_grads(window, kept, expert, pieces, units):
+    _, tiles, tile, model_width = kept[0].shape
+    wide_units = kept[2].shape[3]
+    block = lambda a: pl.BlockSpec((1, 1) + a.shape[2:], lambda i: (expert, i, 0, 0))
+    shape = (pieces, 3, units // pieces, model_width)
     return pl.pallas_call(
-        functools.partial(expert_kernel, experts),
-        grid=(count // tile,),
-        in_specs=[
-            pl.BlockSpec(memory_space=pltpu.SMEM),
-            tiled(model_width),
-            tiled(model_width),
-            whole(router.shape),
-            whole(gate_w.shape),
-            whole(up_w.shape),
-            whole(down_w.shape),
-        ],
-        out_specs=[tiled(model_width + 128), tiled(model_width), whole(grad_shape)],
-        out_shape=[
-            jax.ShapeDtypeStruct((count, model_width + 128), jnp.bfloat16),
-            jax.ShapeDtypeStruct((count, model_width), jnp.bfloat16),
-            jax.ShapeDtypeStruct(grad_shape, jnp.bfloat16),
-        ],
-        scratch_shapes=[pltpu.VMEM((3, hidden_units, model_width), jnp.float32)],
+        weight_kernel,
+        grid=(tiles,),
+        in_specs=[pl.BlockSpec(memory_space=pltpu.SMEM)] + [block(a) for a in kept],
+        out_specs=pl.BlockSpec(shape, lambda i: (0, 0, 0, 0)),
+        out_shape=jax.ShapeDtypeStruct(shape, jnp.bfloat16),
+        scratch_shapes=[pltpu.VMEM((3, wide_units, model_width), jnp.float32)],
+        cost_estimate=cost(20e9, 20e6),
         compiler_params=compiler_params(),
-        name="expert_rows",
-    )(expert, rows, grads, router, gate_w, up_w, down_w)
+        name="weight_grads",
+    )(window, *kept)
 
 
 def send(values, axis, pairs):
     return lax.ppermute(values, axis, pairs)
+
+
+def after(values, *earlier):
+    return lax.optimization_barrier((values, earlier))[0]
 
 
 def fast_device(
@@ -744,7 +1092,6 @@
     experts = w_router.shape[1]
     exp_dev = w_gate.shape[0]
     units = w_gate.shape[2] // n_dp
-    piece = units // n_cp
     capacity = (5 * rows * top_count + 4 * experts - 1) // (4 * experts)
     groups = model_width // (128 * n_cp)
     own_width = 3 * groups * 128
@@ -754,31 +1101,24 @@
     over_y = [(i, i ^ 1) for i in range(n_ep)]
     ring = [(i, (i + 1) % n_cp) for i in range(n_cp)]
     f32, bf16 = jnp.float32, jnp.bfloat16
-
-    slot_tokens = tokens.transpose(1, 0, 2).astype(f32)
-    scale_first = root_scale(slot_tokens)
-    normed_first = (slot_tokens * scale_first * norm1_gain).astype(bf16)
-
-    def ring_gather(values):
-        parts = [values]
-        for _ in range(n_cp - 1):
-            parts.append(send(parts[-1], "cp", ring))
-        return jnp.stack(parts)
-
-    normed_all = [ring_gather(normed_first[s]) for s in range(slots)]
-
-    w_qkv = (
-        w_attn[:, : 3 * model_width]
-        .reshape(model_width, 3, groups, n_cp, 128)
-        .transpose(0, 3, 2, 1, 4)
-        .reshape(model_width, 3 * model_width)
-    )
-    w_own = lax.dynamic_slice(w_qkv, (0, my_cp * own_width), (model_width, own_width))
-    w_out = (
-        w_attn[:, 3 * model_width :]
-        .reshape(groups, n_cp, 128, model_width)
-        .transpose(1, 0, 2, 3)
-        .reshape(model_width, model_width)
+    exact = lax.Precision.HIGHEST
+    each = range(slots)
+
+    low_in = [tokens[:, s] for s in each]
+    inputs = jnp.stack(low_in).astype(f32)
+    normed_first = (inputs * root_scale(inputs) * norm1_gain).astype(bf16)
+
+    w_own = jnp.concatenate(
+        [
+            lax.dynamic_slice(
+                w_attn,
+                (0, which * model_width + (group * n_cp + my_cp) * 128),
+                (model_width, 128),
+            )
+            for group in range(groups)
+            for which in range(3)
+        ],
+        axis=1,
     )
     per_group = 128 // head_size
     own_heads = (
@@ -788,162 +1128,167 @@
     ).reshape(heads_own)
     head_hot = (own_heads[:, None] == jnp.arange(head_count)[None, :]).astype(f32)
     bucket_hot = (buckets[:, None] == jnp.arange(bucket_count)[None, :]).astype(f32)
-    exact = lax.Precision.HIGHEST
     own_table = jnp.dot(head_hot, bias_table, precision=exact)
     lines = jnp.einsum("hb,db->hd", own_table, bucket_hot[::-1], precision=exact)
     lines = jnp.concatenate([lines, jnp.full((heads_own, span_rows), minus_big, f32)], axis=1)
-    bias = make_bias(lines[:, None, :], span_rows)
-
-    def plane_gather(values):
-        over = send(values, "dp", over_x)
-        up = send(values, "ep", over_y)
-        half = values.shape[0] // 2
-        across = jnp.concatenate(
-            [send(over[:half], "ep", over_y), send(up[half:], "dp", over_x)], axis=0
-        )
-        return [values, over, up, across]
+    normed_all, qkvs, bias = gather_project(normed_first, w_own, lines[:, None, :], n_cp)
+
+    def plane_gather(parts):
+        over = [send(part, "dp", over_x) for part in parts]
+        up = [send(part, "ep", over_y) for part in parts]
+        across = [send(over[0], "ep", over_y), send(up[1], "dp", over_x)]
+        return [list(parts), over, up, across]
 
     target = jnp.where(places >= 0, expert_ids * capacity + places, -1)
-    target = target.transpose(2, 1, 0).reshape(top_count, rows)
-    targets = plane_gather(target)
-    row_ids = my_ep * (exp_dev * capacity) + jnp.arange(exp_dev * capacity, dtype=jnp.int32)
-
-    def hot_rows(chosen):
-        hot = jnp.zeros((exp_dev * capacity, rows), f32)
-        for c in range(top_count):
-            hot = hot + (row_ids[:, None] == chosen[c][None, :]).astype(f32)
-        return hot.astype(bf16)
-
-    hots = [hot_rows(chosen) for chosen in targets]
-
-    def pick_rows(blocks):
-        picked = [
-            jnp.dot(hot, block, preferred_element_type=f32).astype(bf16)
-            for hot, block in zip(hots, blocks)
-        ]
-        mine = jnp.stack(picked)
-        theirs = send(mine, "dp", over_core)
-        whole = jnp.stack([mine, theirs]).reshape(2 * len(blocks), exp_dev, capacity, model_width)
-        return [whole[:, e].reshape(-1, model_width) for e in range(exp_dev)]
-
-    low_out = cotangent.transpose(1, 0, 2)
-    grad_out = low_out.astype(f32).reshape(rows, model_width)
-    grad_picked = pick_rows(plane_gather(low_out.reshape(rows, model_width)))
-    units_at = my_dp * units
-    gate_own = lax.dynamic_slice_in_dim(w_gate, units_at, units, axis=2)
-    up_own = lax.dynamic_slice_in_dim(w_up, units_at, units, axis=2)
-    down_own = lax.dynamic_slice_in_dim(w_down, units_at, units, axis=2)
+    target_parts = plane_gather([target[:, s].T for s in each])
+    target_rows = jnp.stack([jnp.concatenate(parts, axis=1) for parts in target_parts])
+    target_columns = target_rows.transpose(0, 2, 1)
+    base = (my_ep * (exp_dev * capacity)).astype(jnp.int32).reshape(1)
+    group_at = ((0, 1), (1, 3), (3, 4))
+    sources = target_rows.shape[0]
+    target_groups = [
+        (target_rows[low:high], target_columns[low:high]) for low, high in group_at
+    ]
+
+    def pick_group(at, blocks):
+        low, high = group_at[at]
+        mine = pick_rows(base, target_groups[at][0], blocks[low:high], exp_dev, capacity)
+        return mine, send(mine, "dp", over_core)
+
+    low_out = [cotangent[:, s] for s in each]
+    grad_blocks = plane_gather(low_out)
+    window_at = my_dp * units // 128 * 128
+    window = jnp.stack([window_at, my_dp * units - window_at]).astype(jnp.int32)
     router_wide = jnp.concatenate(
         [w_router, jnp.zeros((model_width, 128 - experts), w_router.dtype)], axis=1
     )
 
-    metas = [jnp.stack([my_cp.astype(jnp.int32), lengths[s]]) for s in range(slots)]
-    qkvs, fulls, totals, returned = [], [], [], []
-    for s in range(slots):
-        qkv = jnp.dot(
-            normed_all[s].reshape(seq_len, model_width), w_own, preferred_element_type=f32
-        )
-        qkv = qkv.astype(bf16).reshape(n_cp, span_rows, own_width)
-        low, full, total = attend_forward(metas[s], qkv, bias, scale, head_size)
-        qkvs.append(qkv)
+    def deliver(blocks):
+        return [blocks[0]] + [
+            send(blocks[j], "cp", [(i, (i - j) % n_cp) for i in range(n_cp)])
+            for j in range(1, n_cp)
+        ]
+
+    metas = [jnp.stack([my_cp.astype(jnp.int32), lengths[s]]) for s in each]
+    gain_first, gain_second = norm1_gain[None, :], norm2_gain[None, :]
+    fulls, totals, returned = [], [], []
+    for s in each:
+        if s:
+            qkvs = after(qkvs, fulls[-1])
+        low, full, total = attend_forward(metas[s], s, qkvs, bias, scale, head_size)
         fulls.append(full)
         totals.append(total)
-        back = lax.all_to_all(low, "cp", split_axis=0, concat_axis=0, tiled=True)
-        returned.append(back.transpose(1, 0, 2).reshape(span_rows, model_width))
-    attended = jnp.concatenate(returned, axis=0)
-    projected = jnp.dot(attended, w_out, preferred_element_type=f32)
-    positions = my_cp * span_rows + jnp.arange(span_rows, dtype=jnp.int32)
-    live = (positions[None, :] < lengths[:, None]).astype(f32).reshape(rows, 1)
-    inputs = slot_tokens.reshape(rows, model_width)
-    hidden = inputs + live * projected
-    scale_second = root_scale(hidden)
-    normed_second = (hidden * scale_second * norm2_gain).astype(bf16)
-    router_logits = jnp.dot(normed_second, w_router, preferred_element_type=f32)
-    router_probs = jax.nn.softmax(router_logits, axis=-1)
-
-    rows_picked = pick_rows(plane_gather(normed_second))
-    sources = len(hots)
-
-    def combine(per_expert, e):
-        mine, theirs = per_expert[: sources * capacity], per_expert[sources * capacity :]
-        theirs = send(theirs, "dp", over_core)
-        both = (mine.astype(f32) + theirs.astype(f32)).astype(bf16)
-        both = both.reshape(sources, capacity, -1)
-        at = e * capacity
-        return [dot_tn(hots[k][at : at + capacity], both[k]) for k in range(sources)]
-
-    def plane_sum(blocks):
-        here, over, up, across = blocks
-        half = rows // 2
-        got = send(jnp.stack([over[:half], across[:half]]), "dp", over_x).astype(f32)
-        first, next_first = here[:half] + got[0], up[:half] + got[1]
-        got = send(jnp.stack([up[half:], across[half:]]), "ep", over_y).astype(f32)
-        second, next_second = here[half:] + got[0], over[half:] + got[1]
-        first = first + send(next_first.astype(bf16), "ep", over_y).astype(f32)
-        second = second + send(next_second.astype(bf16), "dp", over_x).astype(f32)
-        return jnp.concatenate([first, second], axis=0)
-
-    back_parts, out_parts, weight_sums = [], [], []
+        returned.append(deliver(low))
+    grad_blocks = after(grad_blocks, fulls)
+    grad_groups = [pick_group(at, grad_blocks) for at in range(len(group_at))]
+    attended, hidden, normed_second = [], [], []
+    for s in each:
+        got = project_rows(metas[s], low_in[s], gain_second, w_attn, returned[s])
+        attended.append(got[0])
+        hidden.append(got[1])
+        normed_second.append(got[2])
+
+    first = (my_ep * exp_dev).astype(jnp.int32).reshape(1)
+    row_blocks = plane_gather(normed_second)
+
+    def experts_of(at, picked, kept):
+        low, high = group_at[at]
+        results, kept = run_experts(
+            first,
+            window,
+            *picked,
+            *grad_groups[at],
+            router_wide,
+            (w_gate, w_up, w_down),
+            kept,
+            low,
+            sources,
+            experts,
+            units,
+        )
+        return results[:2], results[2:], kept
+
+    def placed(at, pair):
+        return place_rows(base, target_groups[at][1], *pair, slots)
+
+    def over_cores(pair):
+        return pair[0], send(pair[1], "dp", over_core)
+
+    picked_own = pick_group(0, row_blocks)
+    back_own, out_own, kept = experts_of(0, picked_own, ())
+    row_blocks = after(row_blocks, kept)
+    picked_near = pick_group(1, row_blocks)
+    picked_far = pick_group(2, row_blocks)
+    place_own = placed(0, over_cores(back_own))
+    picked_near = after(picked_near, picked_far[0], place_own)
+    back_near, out_near, kept = experts_of(1, picked_near, kept)
+    back_far, out_far, kept = experts_of(2, picked_far, kept)
+    pair_near = over_cores(back_near)
+    pair_far = over_cores(back_far)
+    place_near = placed(1, after(pair_near, kept))
+    weight_part = weight_grads(window, after(kept, place_near), 0, n_cp, units)
+    place_far = placed(2, after(pair_far, weight_part))
+    weight_sums = []
     for e in range(exp_dev):
-        expert = (my_ep * exp_dev + e).astype(jnp.int32).reshape(1)
-        back, out, weight = run_expert(
-            expert,
-            rows_picked[e],
-            grad_picked[e],
+        if e:
+            weight_part = weight_grads(window, after(kept, place_far, weight_part), e, n_cp, units)
+        part = after(weight_part, weight_sums)
+        weight_sums.append(lax.psum_scatter(part, "cp", scatter_dimension=0, tiled=False))
+
+    def plane_sum(own, near, far, hold=None):
+        (over, up), across = (near[:2], near[2:]), far
+        got_first = send(over[0], "dp", over_x)
+        got_second = send(up[1], "ep", over_y)
+        far_first = send(across[0], "dp", over_x).astype(f32)
+        far_second = send(across[1], "ep", over_y).astype(f32)
+        if hold is not None:
+            far_first, far_second = after((far_first, far_second), hold)
+        next_first = (up[0].astype(f32) + far_first).astype(bf16)
+        next_second = (over[1].astype(f32) + far_second).astype(bf16)
+        last_first = send(next_first, "ep", over_y)
+        last_second = send(next_second, "dp", over_x)
+        return [(own[0], got_first, last_first), (own[1], got_second, last_second)]
+
+    back_rows = plane_sum(place_own, place_near, place_far, weight_part)
+    hidden_grads, proj_grads, leaving, router_parts, gain_parts = [], [], [], [], []
+    for s in each:
+        got = hidden_back(
+            metas[s],
+            *back_rows[s],
+            low_out[s],
+            hidden[s],
+            normed_second[s],
+            gain_second,
             router_wide,
-            gate_own[e],
-            up_own[e],
-            down_own[e],
+            w_attn,
             experts,
             n_cp,
-            2 * capacity,
-        )
-        weight_sums.append(lax.psum_scatter(weight, "cp", scatter_dimension=0, tiled=False))
-        back_parts.append(combine(back, e))
-        out_parts.append(combine(out, e))
-
-    def merged(parts):
-        return plane_sum(
-            [sum(part[k] for part in parts).astype(bf16) for k in range(sources)]
-        )
-
-    back_rows = merged(back_parts)
-    mixed = hidden + merged(out_parts)
-    mixed = mixed.astype(bf16).reshape(slots, span_rows, model_width).transpose(1, 0, 2)
-
-    prob_grads = back_rows[:, model_width : model_width + experts]
-    logit_grads = router_probs * (
-        prob_grads - jnp.sum(router_probs * prob_grads, axis=-1, keepdims=True)
-    )
-    logit_grads = logit_grads.astype(bf16)
-    router_grad = dot_tn(normed_second, logit_grads)
-    grad_normed_second = back_rows[:, :model_width] + dot_nt(logit_grads, w_router)
-    gain_second_grad = jnp.sum(grad_normed_second * hidden * scale_second, axis=0)
-    grad_hidden = grad_out + norm_back(grad_normed_second, hidden, scale_second, norm2_gain)
-    grad_proj = (live * grad_hidden).astype(bf16)
-    grad_att = dot_nt(grad_proj, w_out).astype(bf16)
-
-    sents, rings = [], []
-    line_grads = jnp.zeros((heads_own, seq_len + span_rows), f32)
-    for s in range(slots):
-        leaving = grad_att[s * span_rows : (s + 1) * span_rows]
-        leaving = leaving.reshape(span_rows, n_cp, groups * 128).transpose(1, 0, 2)
-        grads = lax.all_to_all(leaving, "cp", split_axis=0, concat_axis=0, tiled=True)
-        sent, ringed, line = attend_backward(
-            metas[s], qkvs[s], bias, grads, fulls[s], totals[s], scale, head_size
+        )
+        hidden_grads.append(got[0])
+        proj_grads.append(got[1])
+        router_parts.append(got[2])
+        gain_parts.append(got[3])
+        leaving.append(deliver(got[4:]))
+    router_grad = sum(router_parts)[:, :experts]
+    gain_second_grad = sum(gain_parts)[0]
+    out_grad = sum(dot_tn(attended[s], proj_grads[s]) for s in each)
+
+    out_grad = out_grad.astype(bf16).reshape(model_width, n_ep, n_cp, 128).transpose(2, 1, 0, 3)
+    out_grad = after(out_grad, weight_sums)
+    out_grad = lax.psum_scatter(out_grad, "cp", scatter_dimension=0, tiled=False)
+    arriving = []
+    line_grads, qkv_grad = 0.0, 0.0
+    for s in each:
+        grads = jnp.stack(leaving[s])
+        ringed, line = attend_backward(
+            metas[s], s, qkvs, bias, grads, fulls[s], totals[s], scale, head_size
         )
         line_grads = line_grads + line[:, 0]
-        rings.append(ringed.reshape(seq_len, own_width))
-        sent = lax.all_to_all(sent, "cp", split_axis=0, concat_axis=0, tiled=True)
-        sents.append(sent.transpose(1, 0, 2).reshape(span_rows, 3 * model_width))
-
-    out_grad = dot_tn(attended, grad_proj).astype(bf16)
-    out_grad = out_grad.reshape(n_cp, groups, 128, n_ep, n_cp, 128)
-    out_grad = out_grad.transpose(4, 3, 1, 0, 2, 5).reshape(n_cp, n_ep, model_width, 128)
-    out_grad = lax.psum_scatter(out_grad, "cp", scatter_dimension=0, tiled=False)
-    qkv_grad = sum(
-        dot_tn(normed_all[s].reshape(seq_len, model_width), rings[s]) for s in range(slots)
-    )
+        qkv_grad = qkv_grad + dot_tn(
+            normed_all[s].reshape(seq_len, model_width), ringed.reshape(seq_len, own_width)
+        )
+        arriving.append(deliver(ringed))
+
     gain_first_grad = jnp.sum(qkv_grad * w_own.astype(f32), axis=1) / norm1_gain
     attn_term = qkv_grad.reshape(model_width, groups, 3, 128).transpose(2, 1, 0, 3)
     attn_term = jnp.concatenate(
@@ -953,27 +1298,43 @@
     distance_grads = line_grads[:, :seq_len][:, ::-1]
     table_grad = jnp.dot(distance_grads, bucket_hot, precision=exact)
     table_grad = jnp.einsum("hg,hb->gb", head_hot, table_grad, precision=exact)
-    router_sum, table_sum, gain_first_sum, gain_second_sum = lax.psum(
-        (router_grad, table_grad, gain_first_grad, gain_second_grad), ("dp", "ep", "cp")
-    )
-
-    grad_normed_first = dot_nt(jnp.concatenate(sents, axis=0), w_qkv)
-    tokens_grad = grad_hidden + norm_back(
-        grad_normed_first, inputs, scale_first.reshape(rows, 1), norm1_gain
-    )
-    tokens_grad = tokens_grad.astype(bf16).reshape(slots, span_rows, model_width).transpose(1, 0, 2)
-    weight_all = jnp.stack(weight_sums)
+    small = [router_grad.T, table_grad, gain_first_grad, gain_second_grad]
+    total = jnp.concatenate([part.reshape(-1, 128) for part in small], axis=0)
+    for axis, pairs in (("dp", over_core), ("dp", over_x), ("ep", over_y)):
+        total = total + send(total, axis, pairs)
+    step = 1
+    while step < n_cp:
+        total = total + send(total, "cp", [(i, i ^ step) for i in range(n_cp)])
+        step *= 2
+    total = total.reshape(-1)
+    cuts = [0]
+    for part in small:
+        cuts.append(cuts[-1] + part.size)
+    router_sum, table_sum, gain_first_sum, gain_second_sum = (
+        total[cuts[i] : cuts[i + 1]].reshape(part.shape) for i, part in enumerate(small)
+    )
+
+    out_pairs = after([out_own, out_near, out_far], hidden_grads)
+    out_rows = plane_sum(*(placed(at, over_cores(pair)) for at, pair in enumerate(out_pairs)))
+    mixed = [
+        (hidden[s] + sum(part.astype(f32) for part in out_rows[s])).astype(bf16) for s in each
+    ]
+    tokens_grad = [
+        token_grads(metas[s], low_in[s], hidden_grads[s], gain_first, w_attn, arriving[s])
+        for s in each
+    ]
+    weight_sum = jnp.stack(weight_sums)
     gate_sum, up_sum, down_sum = (
-        weight_all[:, which].transpose(0, 2, 1).astype(f32) for which in range(3)
+        weight_sum[:, which].transpose(0, 2, 1).astype(f32) for which in range(3)
     )
     return (
-        mixed,
-        tokens_grad,
+        jnp.stack(mixed, axis=1),
+        jnp.stack(tokens_grad, axis=1),
         attn_sum.astype(f32),
         table_sum,
         gain_first_sum,
         gain_second_sum,
-        router_sum,
+        router_sum.T,
         gate_sum,
         up_sum,
         down_sum,

time: 833 us -> 715 us (0.86)
  the two profiles are of different devices: /device:TPU:0 before, /device:TPU:18 now
where the time goes in v2:
time: 715 us; the launch traced here: 705 us
  Pallas kernels  351 us (49%)
  waiting for transfers between devices  173 us (24%)
  starting transfers between devices  84.9 us (12%)
  local copies, waits for them, and re-layouts  49.9 us (7%)
  other arithmetic  18.3 us (3%)
  between operations  15.3 us (2%)
  matrix products  12.4 us (2%)
    ppermute x65, waiting for transfers between devices, send(): return lax.ppermute(values, axis, pairs)  173 us
    ppermute x65, starting transfers between devices, send(): return lax.ppermute(values, axis, pairs)  84.8 us
    pallas_call x3, Pallas kernels, run_experts(): pl.pallas_call(functools.partial(expert_kernel, experts, units, len(kept)...  80.5 us
    pallas_call x1, Pallas kernels, gather_project(): pl.pallas_call(gather_kernel, in_specs=[whole] * 3, out_specs=[whole] * 3...  76.5 us
    pallas_call x2, Pallas kernels, attend_backward(): pl.pallas_call(functools.partial(backward_kernel, scale, head_size), grid...  46.4 us
    pallas_call x2, Pallas kernels, weight_grads(): pl.pallas_call(weight_kernel, grid=(tiles,), in_specs=[pl.BlockSpec(memor...  42.9 us
    pallas_call x6, Pallas kernels, place_rows(): pl.pallas_call(place_kernel, in_specs=[pl.BlockSpec(memory_space=pltpu.SM...  29.1 us
    pallas_call x6, Pallas kernels, pick_rows(): pl.pallas_call(pick_kernel, in_specs=[pl.BlockSpec(memory_space=pltpu.SME...  22.1 us
  transfers between devices with their start and end apart: 69, of which 30 were waited for; matrix products, arithmetic and copies ran while one was open for 6% of the time, Pallas kernels for 31%

profile of v2, /device:TPU:18, one launch (start us, length us, event | category | flops | bytes accessed | tf_op | source)
XLA Modules:
  0.0 704.9 jit_solution(17989490752096530347)
XLA Ops:
  8.6 3.5 fusion.17
  24.0 76.5 %gather_project.1 = (bf16[2,4,256,1024]{3,2,1,0:T(8,128)(2,1)}, bf16[2,4,256,768]{3,2,1,0:T(8,128)(2,1)}, f32[4,256,1024]{2,1,0:T(8,128)}) custom-call(bf16[2,256,1024]{2,1,0:T(8,128)(2,1)} %fusion.2.normed_ref, bf16[1024,768]{1,0:T(8,128)(2,1)} %copy-done.43, f32[4,1,1280]{2,1,0:T(1,128)} %broadcast_in_dim.10.line_ref), custom_call_target="tpu_custom_call" | custom-call | flops 60000002048 | bytes 20000000 | tf_op jit(solution)/shard_map/gather_project/pallas_call | solution.py:452
  100.5 10.0 %attend_forward.2 = (bf16[4,256,256]{2,1,0:T(8,128)(2,1)}, f32[4,256,256]{2,1,0:T(8,128)}, f32[4,256,256]{2,1,0:T(8,128)}) custom-call(s32[2]{0:T(128)} %get-tuple-element.338.meta_ref, bf16[2,4,256,768]{3,2,1,0:T(8,128)(2,1)} %get-tuple-element.135.q_ref.k_ref.v_ref, bf16[2,4,256,768]{3,2,1,0:T(8,128)(2,1)} %get-tuple-element.135.q_ref.k_ref.v_ref, ...), custom_call_target="tpu_custom_call" | custom-call | flops 8000000000 | bytes 8000000 | tf_op jit(solution)/shard_map/attend_forward/pallas_call | solution.py:534
  110.5 9.7 %attend_forward.3 = (bf16[4,256,256]{2,1,0:T(8,128)(2,1)}, f32[4,256,256]{2,1,0:T(8,128)}, f32[4,256,256]{2,1,0:T(8,128)}) custom-call(s32[2]{0:T(128)} %get-tuple-element.339.meta_ref, bf16[2,4,256,768]{3,2,1,0:T(8,128)(2,1)} %get-tuple-element.135.q_ref.k_ref.v_ref, bf16[2,4,256,768]{3,2,1,0:T(8,128)(2,1)} %get-tuple-element.135.q_ref.k_ref.v_ref, ...), custom_call_target="tpu_custom_call" | custom-call | flops 8000000000 | bytes 8000000 | tf_op jit(solution)/shard_map/attend_forward/pallas_call | solution.py:534
  122.1 2.5 collective-permute-start.9
  131.2 3.7 collective-permute-done.9.refs_1_
  134.9 2.6 collective-permute-start
  137.7 3.5 collective-permute-start.1
  148.4 3.9 project_rows.3
  153.0 3.9 project_rows.2
  156.9 3.1 pick_rows.6.rows_mine
  160.1 3.5 collective-permute-done.17.refs_0_
  163.6 3.5 pick_rows.7.grads_mine
  171.0 12.0 %collective-permute-done.6 = s32[2,256]{1,0:T(2,128)S(1)} collective-permute-done((s32[2,256]{1,0:T(2,128)S(1)}, s32[2,256]{1,0:T(2,128)S(1)}, u32[]{:S(2)}, u32[]{:S(2)}) %collective-permute-start.6) | collective-permute-done | bytes 2080 | tf_op jit(solution)/shard_map/ppermute | solution.py:1058
  183.4 3.2 collective-permute-done.3
  190.7 3.1 collective-permute-done.4
  198.9 22.2 %expert_rows.3 = (bf16[1,2,320,1152]{3,2,1,0:T(8,128)(2,1)}, bf16[1,2,320,1152]{3,2,1,0:T(8,128)(2,1)}, bf16[1,2,320,1024]{3,2,1,0:T(8,128)(2,1)}, bf16[1,2,320,...) custom-call(s32[1]{0:T(128)} %bitcast.21.first_ref, ...), custom_call_target="tpu_custom_call" | custom-call | flops 20000000000 | bytes 8000000 | tf_op jit(solution)/shard_map/expert_rows/pallas_call | solution.py:987
  222.1 4.6 pick_rows.8.rows_mine
  226.7 4.6 pick_rows.10.grads_mine
  237.5 3.1 pick_rows.11.grads_mine
  240.7 3.1 pick_rows.9.rows_mine
  244.3 4.3 place_rows.6
  248.6 36.1 %expert_rows.4 = (bf16[2,2,320,1152]{3,2,1,0:T(8,128)(2,1)}, bf16[2,2,320,1152]{3,2,1,0:T(8,128)(2,1)}, bf16[2,2,320,1024]{3,2,1,0:T(8,128)(2,1)}, bf16[2,2,320,...) custom-call(s32[1]{0:T(128)} %bitcast.21.first_ref, ...), custom_call_target="tpu_custom_call", output_to_operand_aliasing={{4}: (10, {}), {5}: (11, {}), {6}: (12, {}), {7}: (13, {}),... | custom-call | flops 40000000000 | bytes 16000000 | tf_op jit(solution)/shard_map/expert_rows/pallas_call | solution.py:987
  287.1 22.3 %expert_rows.5 = (bf16[1,2,320,1152]{3,2,1,0:T(8,128)(2,1)}, bf16[1,2,320,1152]{3,2,1,0:T(8,128)(2,1)}, bf16[1,2,320,1024]{3,2,1,0:T(8,128)(2,1)}, bf16[1,2,320,...) custom-call(s32[1]{0:T(128)} %bitcast.21.first_ref, ...), custom_call_target="tpu_custom_call", output_to_operand_aliasing={{4}: (10, {}), {5}: (11, {}), {6}: (12, {}), {7}: (13, {}),... | custom-call | flops 20000000000 | bytes 8000000 | tf_op jit(solution)/shard_map/expert_rows/pallas_call | solution.py:987
  310.9 6.6 place_rows.7
  317.6 21.6 %weight_grads.2 = bf16[4,3,176,1024]{3,2,1,0:T(8,128)(2,1)} custom-call(s32[2]{0:T(128)} %pad_add_fusion.6.window_ref, bf16[2,4,640,1024]{3,2,1,0:T(8,128)(2,1)} %get-tuple-element.199.rows_ref, bf16[2,4,640,1024]{3,2,1,0:T(8,128)(2,1)} %get-tuple-element.200.grads_ref, bf16[2,4,640,768]{3,2,1,0:T(8,128)(2,1)} %get-tuple-element.201.gate_ref, ...), custom_call_target="tpu_custom_call" | custom-call | flops 20000000000 | bytes 20000000 | tf_op jit(solution)/shard_map/weight_grads/pallas_call | solution.py:1044
  345.0 4.3 place_rows.8
  349.3 2.5 collective-permute-start.34
  353.9 21.3 %weight_grads.3 = bf16[4,3,176,1024]{3,2,1,0:T(8,128)(2,1)} custom-call(s32[2]{0:T(128)} %pad_add_fusion.6.window_ref, bf16[2,4,640,1024]{3,2,1,0:T(8,128)(2,1)} %get-tuple-element.199.rows_ref, bf16[2,4,640,1024]{3,2,1,0:T(8,128)(2,1)} %get-tuple-element.200.grads_ref, bf16[2,4,640,768]{3,2,1,0:T(8,128)(2,1)} %get-tuple-element.201.gate_ref, ...), custom_call_target="tpu_custom_call" | custom-call | flops 20000000000 | bytes 20000000 | tf_op jit(solution)/shard_map/weight_grads/pallas_call | solution.py:1044
  378.6 2.4 fusion.14
  381.0 10.2 %collective-permute-done.38.last_ref = bf16[256,1152]{1,0:T(8,128)(2,1)S(1)} collective-permute-done((bf16[256,1152]{1,0:T(8,128)(2,1)S(1)}, bf16[256,1152]{1,0:T(8,128)(2,1)S(1)}, u32[]{:S(2)}, u32[]{:S(2)}) %collective-permute-start.38) | collective-permute-done | bytes 589856 | tf_op jit(solution)/shard_map/ppermute | solution.py:1058
  392.0 5.9 hidden_back.3
  402.4 6.0 hidden_back.2
  409.4 2.3 collective-permute-start.49
  415.4 2.6 copy.140
  418.0 13.4 %collective-permute-done.54 = bf16[256,256]{1,0:T(8,128)(2,1)S(1)} collective-permute-done((bf16[256,256]{1,0:T(8,128)(2,1)}, bf16[256,256]{1,0:T(8,128)(2,1)S(1)}, u32[]{:S(2)}, u32[]{:S(2)}) %collective-permute-start.54) | collective-permute-done | bytes 131104 | tf_op jit(solution)/shard_map/ppermute | solution.py:1058
  432.2 5.4 collective-permute-done.50
  440.1 23.3 %attend_backward.2 = (bf16[4,256,768]{2,1,0:T(8,128)(2,1)}, f32[4,1,1280]{2,1,0:T(1,128)}) custom-call(s32[2]{0:T(128)} %get-tuple-element.338.meta_ref, bf16[2,4,256,768]{3,2,1,0:T(8,128)(2,1)} %get-tuple-element.135.q_ref.k_ref.v_ref, bf16[2,4,256,768]{3,2,1,0:T(8,128)(2,1)} %get-tuple-element.135.q_ref.k_ref.v_ref, ...), custom_call_target="tpu_custom_call" | custom-call | flops 20000000000 | bytes 12000000 | tf_op jit(solution)/shard_map/attend_backward/pallas_call | solution.py:638
  463.4 5.0 fusion.20
  468.4 23.1 %attend_backward.3 = (bf16[4,256,768]{2,1,0:T(8,128)(2,1)}, f32[4,1,1280]{2,1,0:T(1,128)}) custom-call(s32[2]{0:T(128)} %get-tuple-element.339.meta_ref, bf16[2,4,256,768]{3,2,1,0:T(8,128)(2,1)} %get-tuple-element.135.q_ref.k_ref.v_ref, bf16[2,4,256,768]{3,2,1,0:T(8,128)(2,1)} %get-tuple-element.135.q_ref.k_ref.v_ref, ...), custom_call_target="tpu_custom_call" | custom-call | flops 20000000000 | bytes 12000000 | tf_op jit(solution)/shard_map/attend_backward/pallas_call | solution.py:638
  491.5 4.6 multiply_reduce_fusion
  497.8 2.5 pad_maximum_fusion
  506.7 3.3 collective-permute-done.61
  511.5 2.4 collective-permute-done.62
  513.9 2.5 collective-permute-start.63
  522.8 2.4 collective-permute-start.58
  525.2 13.0 %collective-permute-start.59 = (bf16[256,768]{1,0:T(8,128)(2,1)S(1)}, bf16[256,768]{1,0:T(8,128)(2,1)}, u32[]{:S(2)}, u32[]{:S(2)}) collective-permute-start(bf16[256,768]{1,0:T(8,128)(2,1)S(1)} %get-tuple-element.309), channel_id=1, source_target_pairs={{0,1},{1,2},{2,3},{3,0},{4,5},{5,6},{6,7},{7,4},{8,9},{9,10},{10,1... | collective-permute-start | bytes 1179656 | tf_op jit(solution)/shard_map/ppermute | solution.py:1058
  540.9 8.4 %collective-permute-done.57.refs_1_ = bf16[256,768]{1,0:T(8,128)(2,1)} collective-permute-done((bf16[256,768]{1,0:T(8,128)(2,1)}, bf16[256,768]{1,0:T(8,128)(2,1)}, u32[]{:S(2)}, u32[]{:S(2)}) %collective-permute-start.57) | collective-permute-done | bytes 393248 | tf_op jit(solution)/shard_map/ppermute | solution.py:1058
  549.3 2.6 collective-permute-start.51
  551.9 37.6 %collective-permute-done.58.refs_2_ = bf16[256,768]{1,0:T(8,128)(2,1)} collective-permute-done((bf16[256,768]{1,0:T(8,128)(2,1)}, bf16[256,768]{1,0:T(8,128)(2,1)}, u32[]{:S(2)}, u32[]{:S(2)}) %collective-permute-start.58) | collective-permute-done | bytes 393248 | tf_op jit(solution)/shard_map/ppermute | solution.py:1058
  589.5 3.4 collective-permute-start.52
  593.6 6.9 token_grads.3
  600.5 3.9 place_rows.11
  604.4 23.4 %collective-permute-done.51.refs_1_ = bf16[256,768]{1,0:T(8,128)(2,1)S(1)} collective-permute-done((bf16[256,768]{1,0:T(8,128)(2,1)S(1)}, bf16[256,768]{1,0:T(8,128)(2,1)S(1)}, u32[]{:S(2)}, u32[]{:S(2)}) %collective-permute-start.51) | collective-permute-done | bytes 393248 | tf_op jit(solution)/shard_map/ppermute | solution.py:1058
  629.3 17.2 %collective-permute-done.52.refs_2_ = bf16[256,768]{1,0:T(8,128)(2,1)S(1)} collective-permute-done((bf16[256,768]{1,0:T(8,128)(2,1)S(1)}, bf16[256,768]{1,0:T(8,128)(2,1)S(1)}, u32[]{:S(2)}, u32[]{:S(2)}) %collective-permute-start.52) | collective-permute-done | bytes 393248 | tf_op jit(solution)/shard_map/ppermute | solution.py:1058
  646.5 3.6 collective-permute-done.53.refs_3_
  650.8 6.8 token_grads.2
  658.2 6.0 place_rows.10
  668.7 2.4 collective-permute-done.43
  676.0 4.0 place_rows.9
  680.0 2.3 collective-permute-done.47
  683.7 4.2 collective-permute-done.44
  687.8 2.2 collective-permute-done.41
  695.7 2.2 convert_bitcast_fusion
  (369 shorter events, 117.7 us)
Async XLA Ops:
  7.2 432.8 %reduce-scatter.5.cloned.1.call-start = ((), (), s32[]{:S(2)}) async-start(), calls=%async_computation.4 | async-start | bytes 5406720 | tf_op jit(solution)/shard_map/reduce_scatter | solution.py:1236
  122.1 12.9 %collective-permute-start.9 = (bf16[256,256]{1,0:T(8,128)(2,1)S(1)}, bf16[256,256]{1,0:T(8,128)(2,1)S(1)}, u32[]{:S(2)}, u32[]{:S(2)}) collective-permute-start(bf16[256,256]{1,0:T(8,128)(2,1)S(1)} %get-tuple-element.329), channel_id=1, source_target_pairs={{0,3},{1,0},{2,1},{3,2},{4,7},{5,4},{6,5},{7,6},{8,11},{9,8},{10,9... | collective-permute-start | bytes 393224 | tf_op jit(solution)/shard_map/ppermute | solution.py:1058
  124.5 13.1 %collective-permute-start.10 = (bf16[256,256]{1,0:T(8,128)(2,1)S(1)}, bf16[256,256]{1,0:T(8,128)(2,1)S(1)}, u32[]{:S(2)}, u32[]{:S(2)}) collective-permute-start(bf16[256,256]{1,0:T(8,128)(2,1)S(1)} %get-tuple-element.328), channel_id=1, source_target_pairs={{0,2},{1,3},{2,0},{3,1},{4,6},{5,7},{6,4},{7,5},{8,10},{9,11},{10,... | collective-permute-start | bytes 393224 | tf_op jit(solution)/shard_map/ppermute | solution.py:1058
  126.0 16.1 %collective-permute-start.11 = (bf16[256,256]{1,0:T(8,128)(2,1)S(1)}, bf16[256,256]{1,0:T(8,128)(2,1)S(1)}, u32[]{:S(2)}, u32[]{:S(2)}) collective-permute-start(bf16[256,256]{1,0:T(8,128)(2,1)S(1)} %get-tuple-element.327), channel_id=1, source_target_pairs={{0,1},{1,2},{2,3},{3,0},{4,5},{5,6},{6,7},{7,4},{8,9},{9,10},{10,1... | collective-permute-start | bytes 393224 | tf_op jit(solution)/shard_map/ppermute | solution.py:1058
  128.1 18.2 %collective-permute-start.13 = (bf16[256,1024]{1,0:T(8,128)(2,1)S(1)}, bf16[256,1024]{1,0:T(8,128)(2,1)S(1)}, u32[]{:S(2)}, u32[]{:S(2)}) collective-permute-start(bf16[256,1024]{1,0:T(8,128)(2,1)S(1)} %bitcast.165), channel_id=1, source_target_pairs={{0,16},{8,24},{16,0},{24,8},{1,17},{9,25},{17,1},{25,9},{2,18},{10... | collective-permute-start | bytes 1572872 | tf_op jit(solution)/shard_map/ppermute | solution.py:1058
  128.9 18.9 %collective-permute-start.16 = (bf16[256,1024]{1,0:T(8,128)(2,1)S(1)}, bf16[256,1024]{1,0:T(8,128)(2,1)S(1)}, u32[]{:S(2)}, u32[]{:S(2)}) collective-permute-start(bf16[256,1024]{1,0:T(8,128)(2,1)S(1)} %bitcast.169), channel_id=1, source_target_pairs={{0,4},{4,0},{1,5},{5,1},{2,6},{6,2},{3,7},{7,3},{8,12},{12,8},{9,1... | collective-permute-start | bytes 1572872 | tf_op jit(solution)/shard_map/ppermute | solution.py:1058
  134.9 7.8 %collective-permute-start = (bf16[256,256]{1,0:T(8,128)(2,1)S(1)}, bf16[256,256]{1,0:T(8,128)(2,1)S(1)}, u32[]{:S(2)}, u32[]{:S(2)}) collective-permute-start(bf16[256,256]{1,0:T(8,128)(2,1)S(1)} %get-tuple-element.325), channel_id=1, source_target_pairs={{0,3},{1,0},{2,1},{3,2},{4,7},{5,4},{6,5},{7,6},{8,11},{9,8},{10,9... | collective-permute-start | bytes 393224 | tf_op jit(solution)/shard_map/ppermute | solution.py:1058
  137.7 6.5 collective-permute-start.1
  142.0 18.0 %collective-permute-start.14 = (bf16[256,1024]{1,0:T(8,128)(2,1)S(1)}, bf16[256,1024]{1,0:T(8,128)(2,1)S(1)}, u32[]{:S(2)}, u32[]{:S(2)}) collective-permute-start(bf16[256,1024]{1,0:T(8,128)(2,1)S(1)} %bitcast.170), channel_id=1, source_target_pairs={{0,16},{8,24},{16,0},{24,8},{1,17},{9,25},{17,1},{25,9},{2,18},{10... | collective-permute-start | bytes 1572872 | tf_op jit(solution)/shard_map/ppermute | solution.py:1058
  142.7 17.3 %collective-permute-start.15 = (bf16[256,1024]{1,0:T(8,128)(2,1)S(1)}, bf16[256,1024]{1,0:T(8,128)(2,1)S(1)}, u32[]{:S(2)}, u32[]{:S(2)}) collective-permute-start(bf16[256,1024]{1,0:T(8,128)(2,1)S(1)} %bitcast.166), channel_id=1, source_target_pairs={{0,4},{4,0},{1,5},{5,1},{2,6},{6,2},{3,7},{7,3},{8,12},{12,8},{9,1... | collective-permute-start | bytes 1572872 | tf_op jit(solution)/shard_map/ppermute | solution.py:1058
  144.2 8.1 %collective-permute-start.2 = (bf16[256,256]{1,0:T(8,128)(2,1)S(1)}, bf16[256,256]{1,0:T(8,128)(2,1)S(1)}, u32[]{:S(2)}, u32[]{:S(2)}) collective-permute-start(bf16[256,256]{1,0:T(8,128)(2,1)S(1)} %get-tuple-element.323), channel_id=1, source_target_pairs={{0,1},{1,2},{2,3},{3,0},{4,5},{5,6},{6,7},{7,4},{8,9},{9,10},{10,1... | collective-permute-start | bytes 393224 | tf_op jit(solution)/shard_map/ppermute | solution.py:1058
  146.3 17.3 %collective-permute-start.17 = (bf16[256,1024]{1,0:T(8,128)(2,1)S(1)}, bf16[256,1024]{1,0:T(8,128)(2,1)S(1)}, u32[]{:S(2)}, u32[]{:S(2)}) collective-permute-start(bf16[256,1024]{1,0:T(8,128)(2,1)S(1)} %collective-permute-done.13.refs_0_), channel_id=1, source_target_pairs={{0,4},{4,0},{1,5},{5,1},{2,6},{6,2},{3,7},{7,3},{8,12},{12,8},{9,1... | collective-permute-start | bytes 1572872 | tf_op jit(solution)/shard_map/ppermute | solution.py:1058
  147.9 15.8 %collective-permute-start.18 = (bf16[256,1024]{1,0:T(8,128)(2,1)S(1)}, bf16[256,1024]{1,0:T(8,128)(2,1)S(1)}, u32[]{:S(2)}, u32[]{:S(2)}) collective-permute-start(bf16[256,1024]{1,0:T(8,128)(2,1)S(1)} %collective-permute-done.16.refs_3_), channel_id=1, source_target_pairs={{0,16},{8,24},{16,0},{24,8},{1,17},{9,25},{17,1},{25,9},{2,18},{10... | collective-permute-start | bytes 1572872 | tf_op jit(solution)/shard_map/ppermute | solution.py:1058
  160.0 37.2 %collective-permute-start.12 = (bf16[1,2,320,1024]{3,2,1,0:T(8,128)(2,1)}, bf16[1,2,320,1024]{3,2,1,0:T(8,128)(2,1)}, u32[]{:S(2)}, u32[]{:S(2)}) collective-permute-start(bf16[1,2,320,1024]{3,2,1,0:T(8,128)(2,1)} %pick_rows.6.rows_mine), channel_id=1, source_target_pairs={{0,8},{8,0},{16,24},{24,16},{1,9},{9,1},{17,25},{25,17},{2,10},{10... | collective-permute-start | bytes 3932168 | tf_op jit(solution)/shard_map/ppermute | solution.py:1058
  167.2 31.7 %collective-permute-start.19 = (bf16[1,2,320,1024]{3,2,1,0:T(8,128)(2,1)}, bf16[1,2,320,1024]{3,2,1,0:T(8,128)(2,1)}, u32[]{:S(2)}, u32[]{:S(2)}) collective-permute-start(bf16[1,2,320,1024]{3,2,1,0:T(8,128)(2,1)} %pick_rows.7.grads_mine), channel_id=1, source_target_pairs={{0,8},{8,0},{16,24},{24,16},{1,9},{9,1},{17,25},{25,17},{2,10},{10... | collective-permute-start | bytes 3932168 | tf_op jit(solution)/shard_map/ppermute | solution.py:1058
  167.3 27.9 %collective-permute-start.20 = (bf16[256,1024]{1,0:T(8,128)(2,1)S(1)}, bf16[256,1024]{1,0:T(8,128)(2,1)S(1)}, u32[]{:S(2)}, u32[]{:S(2)}) collective-permute-start(bf16[256,1024]{1,0:T(8,128)(2,1)S(1)} %copy-done.26), channel_id=1, source_target_pairs={{0,16},{8,24},{16,0},{24,8},{1,17},{9,25},{17,1},{25,9},{2,18},{10... | collective-permute-start | bytes 1572872 | tf_op jit(solution)/shard_map/ppermute | solution.py:1058
  169.0 27.9 %collective-permute-start.23 = (bf16[256,1024]{1,0:T(8,128)(2,1)S(1)}, bf16[256,1024]{1,0:T(8,128)(2,1)S(1)}, u32[]{:S(2)}, u32[]{:S(2)}) collective-permute-start(bf16[256,1024]{1,0:T(8,128)(2,1)S(1)} %copy-done.27), channel_id=1, source_target_pairs={{0,4},{4,0},{1,5},{5,1},{2,6},{6,2},{3,7},{7,3},{8,12},{12,8},{9,1... | collective-permute-start | bytes 1572872 | tf_op jit(solution)/shard_map/ppermute | solution.py:1058
  170.6 12.5 %collective-permute-start.6 = (s32[2,256]{1,0:T(2,128)S(1)}, s32[2,256]{1,0:T(2,128)S(1)}, u32[]{:S(2)}, u32[]{:S(2)}) collective-permute-start(s32[2,256]{1,0:T(2,128)S(1)} %get-tuple-element.334), channel_id=1, source_target_pairs={{0,4},{4,0},{1,5},{5,1},{2,6},{6,2},{3,7},{7,3},{8,12},{12,8},{9,1... | collective-permute-start | bytes 6152 | tf_op jit(solution)/shard_map/ppermute | solution.py:1058
  183.0 3.6 collective-permute-start.3
  194.8 26.3 %collective-permute-start.21 = (bf16[256,1024]{1,0:T(8,128)(2,1)S(1)}, bf16[256,1024]{1,0:T(8,128)(2,1)S(1)}, u32[]{:S(2)}, u32[]{:S(2)}) collective-permute-start(bf16[256,1024]{1,0:T(8,128)(2,1)S(1)} %copy-done.27), channel_id=1, source_target_pairs={{0,16},{8,24},{16,0},{24,8},{1,17},{9,25},{17,1},{25,9},{2,18},{10... | collective-permute-start | bytes 1572872 | tf_op jit(solution)/shard_map/ppermute | solution.py:1058
  195.2 26.0 %collective-permute-start.22 = (bf16[256,1024]{1,0:T(8,128)(2,1)S(1)}, bf16[256,1024]{1,0:T(8,128)(2,1)S(1)}, u32[]{:S(2)}, u32[]{:S(2)}) collective-permute-start(bf16[256,1024]{1,0:T(8,128)(2,1)S(1)} %copy-done.26), channel_id=1, source_target_pairs={{0,4},{4,0},{1,5},{5,1},{2,6},{6,2},{3,7},{7,3},{8,12},{12,8},{9,1... | collective-permute-start | bytes 1572872 | tf_op jit(solution)/shard_map/ppermute | solution.py:1058
  196.9 24.3 %collective-permute-start.24 = (bf16[256,1024]{1,0:T(8,128)(2,1)S(1)}, bf16[256,1024]{1,0:T(8,128)(2,1)S(1)}, u32[]{:S(2)}, u32[]{:S(2)}) collective-permute-start(bf16[256,1024]{1,0:T(8,128)(2,1)S(1)} %collective-permute-done.20.refs_0_), channel_id=1, source_target_pairs={{0,4},{4,0},{1,5},{5,1},{2,6},{6,2},{3,7},{7,3},{8,12},{12,8},{9,1... | collective-permute-start | bytes 1572872 | tf_op jit(solution)/shard_map/ppermute | solution.py:1058
  197.2 24.0 %collective-permute-start.25 = (bf16[256,1024]{1,0:T(8,128)(2,1)S(1)}, bf16[256,1024]{1,0:T(8,128)(2,1)S(1)}, u32[]{:S(2)}, u32[]{:S(2)}) collective-permute-start(bf16[256,1024]{1,0:T(8,128)(2,1)S(1)} %collective-permute-done.23.refs_3_), channel_id=1, source_target_pairs={{0,16},{8,24},{16,0},{24,8},{1,17},{9,25},{17,1},{25,9},{2,18},{10... | collective-permute-start | bytes 1572872 | tf_op jit(solution)/shard_map/ppermute | solution.py:1058
  226.7 21.9 %collective-permute-start.26 = (bf16[2,2,320,1024]{3,2,1,0:T(8,128)(2,1)}, bf16[2,2,320,1024]{3,2,1,0:T(8,128)(2,1)}, u32[]{:S(2)}, u32[]{:S(2)}) collective-permute-start(bf16[2,2,320,1024]{3,2,1,0:T(8,128)(2,1)} %pick_rows.8.rows_mine), channel_id=1, source_target_pairs={{0,8},{8,0},{16,24},{24,16},{1,9},{9,1},{17,25},{25,17},{2,10},{10... | collective-permute-start | bytes 7864328 | tf_op jit(solution)/shard_map/ppermute | solution.py:1058
  231.3 17.3 %collective-permute-start.28 = (bf16[2,2,320,1024]{3,2,1,0:T(8,128)(2,1)}, bf16[2,2,320,1024]{3,2,1,0:T(8,128)(2,1)}, u32[]{:S(2)}, u32[]{:S(2)}) collective-permute-start(bf16[2,2,320,1024]{3,2,1,0:T(8,128)(2,1)} %pick_rows.10.grads_mine), channel_id=1, source_target_pairs={{0,8},{8,0},{16,24},{24,16},{1,9},{9,1},{17,25},{25,17},{2,10},{10... | collective-permute-start | bytes 7864328 | tf_op jit(solution)/shard_map/ppermute | solution.py:1058
  231.8 12.5 %collective-permute-start.27 = (bf16[1,2,320,1152]{3,2,1,0:T(8,128)(2,1)}, bf16[1,2,320,1152]{3,2,1,0:T(8,128)(2,1)}, u32[]{:S(2)}, u32[]{:S(2)}) collective-permute-start(bf16[1,2,320,1152]{3,2,1,0:T(8,128)(2,1)} %get-tuple-element.155), channel_id=1, source_target_pairs={{0,8},{8,0},{16,24},{24,16},{1,9},{9,1},{17,25},{25,17},{2,10},{10... | collective-permute-start | bytes 4423688 | tf_op jit(solution)/shard_map/ppermute | solution.py:1058
  231.8 3.6 collective-permute-start.8
  240.7 45.0 %collective-permute-start.30 = (bf16[1,2,320,1024]{3,2,1,0:T(8,128)(2,1)}, bf16[1,2,320,1024]{3,2,1,0:T(8,128)(2,1)S(1)}, u32[]{:S(2)}, u32[]{:S(2)}) collective-permute-start(bf16[1,2,320,1024]{3,2,1,0:T(8,128)(2,1)} %pick_rows.11.grads_mine), channel_id=1, source_target_pairs={{0,8},{8,0},{16,24},{24,16},{1,9},{9,1},{17,25},{25,17},{2,10},{10... | collective-permute-start | bytes 3932168 | tf_op jit(solution)/shard_map/ppermute | solution.py:1058
  243.8 41.8 %collective-permute-start.29 = (bf16[1,2,320,1024]{3,2,1,0:T(8,128)(2,1)}, bf16[1,2,320,1024]{3,2,1,0:T(8,128)(2,1)S(1)}, u32[]{:S(2)}, u32[]{:S(2)}) collective-permute-start(bf16[1,2,320,1024]{3,2,1,0:T(8,128)(2,1)} %pick_rows.9.rows_mine), channel_id=1, source_target_pairs={{0,8},{8,0},{16,24},{24,16},{1,9},{9,1},{17,25},{25,17},{2,10},{10... | collective-permute-start | bytes 3932168 | tf_op jit(solution)/shard_map/ppermute | solution.py:1058
  284.7 24.7 %collective-permute-start.31 = (bf16[2,2,320,1152]{3,2,1,0:T(8,128)(2,1)}, bf16[2,2,320,1152]{3,2,1,0:T(8,128)(2,1)S(1)}, u32[]{:S(2)}, u32[]{:S(2)}) collective-permute-start(bf16[2,2,320,1152]{3,2,1,0:T(8,128)(2,1)} %get-tuple-element.176), channel_id=1, source_target_pairs={{0,8},{8,0},{16,24},{24,16},{1,9},{9,1},{17,25},{25,17},{2,10},{10... | collective-permute-start | bytes 8847368 | tf_op jit(solution)/shard_map/ppermute | solution.py:1058
  339.2 158.6 %reduce-scatter.7.cloned.1.call-start = ((), (), s32[]{:S(2)}) async-start(), calls=%async_computation.5 | async-start | bytes 2621440 | tf_op jit(solution)/shard_map/reduce_scatter | solution.py:1278
  341.0 60.4 %collective-permute-start.32 = (bf16[256,1152]{1,0:T(8,128)(2,1)S(1)}, bf16[256,1152]{1,0:T(8,128)(2,1)S(1)}, u32[]{:S(2)}, u32[]{:S(2)}) collective-permute-start(bf16[256,1152]{1,0:T(8,128)(2,1)S(1)} %copy-done.60), channel_id=1, source_target_pairs={{0,16},{8,24},{16,0},{24,8},{1,17},{9,25},{17,1},{25,9},{2,18},{10... | collective-permute-start | bytes 1769480 | tf_op jit(solution)/shard_map/ppermute | solution.py:1058
  349.3 25.9 %collective-permute-start.34 = (bf16[256,1152]{1,0:T(8,128)(2,1)}, bf16[256,1152]{1,0:T(8,128)(2,1)S(1)}, u32[]{:S(2)}, u32[]{:S(2)}) collective-permute-start(bf16[256,1152]{1,0:T(8,128)(2,1)} %get-tuple-element.197), channel_id=1, source_target_pairs={{0,16},{8,24},{16,0},{24,8},{1,17},{9,25},{17,1},{25,9},{2,18},{10... | collective-permute-start | bytes 1769480 | tf_op jit(solution)/shard_map/ppermute | solution.py:1058
  351.9 23.4 %collective-permute-start.35 = (bf16[256,1152]{1,0:T(8,128)(2,1)}, bf16[256,1152]{1,0:T(8,128)(2,1)S(1)}, u32[]{:S(2)}, u32[]{:S(2)}) collective-permute-start(bf16[256,1152]{1,0:T(8,128)(2,1)} %get-tuple-element.198), channel_id=1, source_target_pairs={{0,4},{4,0},{1,5},{5,1},{2,6},{6,2},{3,7},{7,3},{8,12},{12,8},{9,1... | collective-permute-start | bytes 1769480 | tf_op jit(solution)/shard_map/ppermute | solution.py:1058
  353.4 27.6 %collective-permute-start.37 = (bf16[256,1152]{1,0:T(8,128)(2,1)}, bf16[256,1152]{1,0:T(8,128)(2,1)S(1)}, u32[]{:S(2)}, u32[]{:S(2)}) collective-permute-start(bf16[256,1152]{1,0:T(8,128)(2,1)} %get-tuple-element.189), channel_id=1, source_target_pairs={{0,4},{4,0},{1,5},{5,1},{2,6},{6,2},{3,7},{7,3},{8,12},{12,8},{9,1... | collective-permute-start | bytes 1769480 | tf_op jit(solution)/shard_map/ppermute | solution.py:1058
  376.4 14.8 %collective-permute-start.38 = (bf16[256,1152]{1,0:T(8,128)(2,1)S(1)}, bf16[256,1152]{1,0:T(8,128)(2,1)S(1)}, u32[]{:S(2)}, u32[]{:S(2)}) collective-permute-start(bf16[256,1152]{1,0:T(8,128)(2,1)S(1)} %add_convert_fusion.1), channel_id=1, source_target_pairs={{0,16},{8,24},{16,0},{24,8},{1,17},{9,25},{17,1},{25,9},{2,18},{10... | collective-permute-start | bytes 1769480 | tf_op jit(solution)/shard_map/ppermute | solution.py:1058
  376.6 24.8 %collective-permute-start.36 = (bf16[256,1152]{1,0:T(8,128)(2,1)S(1)}, bf16[256,1152]{1,0:T(8,128)(2,1)S(1)}, u32[]{:S(2)}, u32[]{:S(2)}) collective-permute-start(bf16[256,1152]{1,0:T(8,128)(2,1)S(1)} %add_convert_fusion.2), channel_id=1, source_target_pairs={{0,4},{4,0},{1,5},{5,1},{2,6},{6,2},{3,7},{7,3},{8,12},{12,8},{9,1... | collective-permute-start | bytes 1769480 | tf_op jit(solution)/shard_map/ppermute | solution.py:1058
  397.9 16.3 %collective-permute-start.56 = (bf16[256,256]{1,0:T(8,128)(2,1)}, bf16[256,256]{1,0:T(8,128)(2,1)S(1)}, u32[]{:S(2)}, u32[]{:S(2)}) collective-permute-start(bf16[256,256]{1,0:T(8,128)(2,1)} %get-tuple-element.232), channel_id=1, source_target_pairs={{0,1},{1,2},{2,3},{3,0},{4,5},{5,6},{6,7},{7,4},{8,9},{9,10},{10,1... | collective-permute-start | bytes 393224 | tf_op jit(solution)/shard_map/ppermute | solution.py:1058
  399.7 18.3 %collective-permute-start.55 = (bf16[256,256]{1,0:T(8,128)(2,1)}, bf16[256,256]{1,0:T(8,128)(2,1)S(1)}, u32[]{:S(2)}, u32[]{:S(2)}) collective-permute-start(bf16[256,256]{1,0:T(8,128)(2,1)} %get-tuple-element.231), channel_id=1, source_target_pairs={{0,2},{1,3},{2,0},{3,1},{4,6},{5,7},{6,4},{7,5},{8,10},{9,11},{10,... | collective-permute-start | bytes 393224 | tf_op jit(solution)/shard_map/ppermute | solution.py:1058
  400.3 31.1 %collective-permute-start.54 = (bf16[256,256]{1,0:T(8,128)(2,1)}, bf16[256,256]{1,0:T(8,128)(2,1)S(1)}, u32[]{:S(2)}, u32[]{:S(2)}) collective-permute-start(bf16[256,256]{1,0:T(8,128)(2,1)} %get-tuple-element.230), channel_id=1, source_target_pairs={{0,3},{1,0},{2,1},{3,2},{4,7},{5,4},{6,5},{7,6},{8,11},{9,8},{10,9... | collective-permute-start | bytes 393224 | tf_op jit(solution)/shard_map/ppermute | solution.py:1058
  408.4 29.2 %collective-permute-start.50 = (bf16[256,256]{1,0:T(8,128)(2,1)}, bf16[256,256]{1,0:T(8,128)(2,1)S(1)}, u32[]{:S(2)}, u32[]{:S(2)}) collective-permute-start(bf16[256,256]{1,0:T(8,128)(2,1)} %get-tuple-element.226), channel_id=1, source_target_pairs={{0,1},{1,2},{2,3},{3,0},{4,5},{5,6},{6,7},{7,4},{8,9},{9,10},{10,1... | collective-permute-start | bytes 393224 | tf_op jit(solution)/shard_map/ppermute | solution.py:1058
  409.4 28.2 %collective-permute-start.49 = (bf16[256,256]{1,0:T(8,128)(2,1)}, bf16[256,256]{1,0:T(8,128)(2,1)S(1)}, u32[]{:S(2)}, u32[]{:S(2)}) collective-permute-start(bf16[256,256]{1,0:T(8,128)(2,1)} %get-tuple-element.225), channel_id=1, source_target_pairs={{0,2},{1,3},{2,0},{3,1},{4,6},{5,7},{6,4},{7,5},{8,10},{9,11},{10,... | collective-permute-start | bytes 393224 | tf_op jit(solution)/shard_map/ppermute | solution.py:1058
  414.2 24.9 %collective-permute-start.48 = (bf16[256,256]{1,0:T(8,128)(2,1)S(1)}, bf16[256,256]{1,0:T(8,128)(2,1)S(1)}, u32[]{:S(2)}, u32[]{:S(2)}) collective-permute-start(bf16[256,256]{1,0:T(8,128)(2,1)S(1)} %copy-done.78), channel_id=1, source_target_pairs={{0,3},{1,0},{2,1},{3,2},{4,7},{5,4},{6,5},{7,6},{8,11},{9,8},{10,9... | collective-permute-start | bytes 393224 | tf_op jit(solution)/shard_map/ppermute | solution.py:1058
  440.0 252.6 %reduce-scatter.9.cloned.1.call-start = ((), (), s32[]{:S(2)}) async-start(), calls=%async_computation.6 | async-start | bytes 2359296 | tf_op jit(solution)/shard_map/reduce_scatter | solution.py:1297
  500.3 194.1 %reduce-scatter.11.cloned.1.call-start = ((), (), s32[]{:S(2)}) async-start(), calls=%async_computation.7 | async-start | bytes 5406720 | tf_op jit(solution)/shard_map/reduce_scatter | solution.py:1236
  501.0 157.2 %collective-permute-start.40 = (bf16[2,2,320,1024]{3,2,1,0:T(8,128)(2,1)}, bf16[2,2,320,1024]{3,2,1,0:T(8,128)(2,1)}, u32[]{:S(2)}, u32[]{:S(2)}) collective-permute-start(bf16[2,2,320,1024]{3,2,1,0:T(8,128)(2,1)} %get-tuple-element.213), channel_id=1, source_target_pairs={{0,8},{8,0},{16,24},{24,16},{1,9},{9,1},{17,25},{25,17},{2,10},{10... | collective-permute-start | bytes 7864328 | tf_op jit(solution)/shard_map/ppermute | solution.py:1058
  503.5 96.9 %collective-permute-start.42 = (bf16[1,2,320,1024]{3,2,1,0:T(8,128)(2,1)}, bf16[1,2,320,1024]{3,2,1,0:T(8,128)(2,1)}, u32[]{:S(2)}, u32[]{:S(2)}) collective-permute-start(bf16[1,2,320,1024]{3,2,1,0:T(8,128)(2,1)} %get-tuple-element.217), channel_id=1, source_target_pairs={{0,8},{8,0},{16,24},{24,16},{1,9},{9,1},{17,25},{25,17},{2,10},{10... | collective-permute-start | bytes 3932168 | tf_op jit(solution)/shard_map/ppermute | solution.py:1058
  506.1 3.9 collective-permute-start.61
  510.0 3.9 collective-permute-start.62
  513.9 4.3 collective-permute-start.63
  518.2 6.9 collective-permute-start.64
  520.8 28.5 %collective-permute-start.57 = (bf16[256,768]{1,0:T(8,128)(2,1)}, bf16[256,768]{1,0:T(8,128)(2,1)}, u32[]{:S(2)}, u32[]{:S(2)}) collective-permute-start(bf16[256,768]{1,0:T(8,128)(2,1)} %get-tuple-element.311), channel_id=1, source_target_pairs={{0,3},{1,0},{2,1},{3,2},{4,7},{5,4},{6,5},{7,6},{8,11},{9,8},{10,9... | collective-permute-start | bytes 1179656 | tf_op jit(solution)/shard_map/ppermute | solution.py:1058
  522.8 66.7 %collective-permute-start.58 = (bf16[256,768]{1,0:T(8,128)(2,1)}, bf16[256,768]{1,0:T(8,128)(2,1)}, u32[]{:S(2)}, u32[]{:S(2)}) collective-permute-start(bf16[256,768]{1,0:T(8,128)(2,1)} %get-tuple-element.310), channel_id=1, source_target_pairs={{0,2},{1,3},{2,0},{3,1},{4,6},{5,7},{6,4},{7,5},{8,10},{9,11},{10,... | collective-permute-start | bytes 1179656 | tf_op jit(solution)/shard_map/ppermute | solution.py:1058
  525.2 68.2 %collective-permute-start.59 = (bf16[256,768]{1,0:T(8,128)(2,1)S(1)}, bf16[256,768]{1,0:T(8,128)(2,1)}, u32[]{:S(2)}, u32[]{:S(2)}) collective-permute-start(bf16[256,768]{1,0:T(8,128)(2,1)S(1)} %get-tuple-element.309), channel_id=1, source_target_pairs={{0,1},{1,2},{2,3},{3,0},{4,5},{5,6},{6,7},{7,4},{8,9},{9,10},{10,1... | collective-permute-start | bytes 1179656 | tf_op jit(solution)/shard_map/ppermute | solution.py:1058
  549.3 78.6 %collective-permute-start.51 = (bf16[256,768]{1,0:T(8,128)(2,1)S(1)}, bf16[256,768]{1,0:T(8,128)(2,1)S(1)}, u32[]{:S(2)}, u32[]{:S(2)}) collective-permute-start(bf16[256,768]{1,0:T(8,128)(2,1)S(1)} %get-tuple-element.307), channel_id=1, source_target_pairs={{0,3},{1,0},{2,1},{3,2},{4,7},{5,4},{6,5},{7,6},{8,11},{9,8},{10,9... | collective-permute-start | bytes 1179656 | tf_op jit(solution)/shard_map/ppermute | solution.py:1058
  589.5 57.0 %collective-permute-start.52 = (bf16[256,768]{1,0:T(8,128)(2,1)S(1)}, bf16[256,768]{1,0:T(8,128)(2,1)S(1)}, u32[]{:S(2)}, u32[]{:S(2)}) collective-permute-start(bf16[256,768]{1,0:T(8,128)(2,1)S(1)} %get-tuple-element.306), channel_id=1, source_target_pairs={{0,2},{1,3},{2,0},{3,1},{4,6},{5,7},{6,4},{7,5},{8,10},{9,11},{10,... | collective-permute-start | bytes 1179656 | tf_op jit(solution)/shard_map/ppermute | solution.py:1058
  593.3 56.7 %collective-permute-start.53 = (bf16[256,768]{1,0:T(8,128)(2,1)S(1)}, bf16[256,768]{1,0:T(8,128)(2,1)S(1)}, u32[]{:S(2)}, u32[]{:S(2)}) collective-permute-start(bf16[256,768]{1,0:T(8,128)(2,1)S(1)} %get-tuple-element.305), channel_id=1, source_target_pairs={{0,1},{1,2},{2,3},{3,0},{4,5},{5,6},{6,7},{7,4},{8,9},{9,10},{10,1... | collective-permute-start | bytes 1179656 | tf_op jit(solution)/shard_map/ppermute | solution.py:1058
  600.4 75.5 %collective-permute-start.39 = (bf16[1,2,320,1024]{3,2,1,0:T(8,128)(2,1)S(1)}, bf16[1,2,320,1024]{3,2,1,0:T(8,128)(2,1)}, u32[]{:S(2)}, u32[]{:S(2)}) collective-permute-start(bf16[1,2,320,1024]{3,2,1,0:T(8,128)(2,1)S(1)} %copy-done.59), channel_id=1, source_target_pairs={{0,8},{8,0},{16,24},{24,16},{1,9},{9,1},{17,25},{25,17},{2,10},{10... | collective-permute-start | bytes 3932168 | tf_op jit(solution)/shard_map/ppermute | solution.py:1058
  627.8 36.4 %collective-permute-start.46 = (bf16[256,1024]{1,0:T(8,128)(2,1)}, bf16[256,1024]{1,0:T(8,128)(2,1)S(1)}, u32[]{:S(2)}, u32[]{:S(2)}) collective-permute-start(bf16[256,1024]{1,0:T(8,128)(2,1)} %get-tuple-element.222), channel_id=1, source_target_pairs={{0,4},{4,0},{1,5},{5,1},{2,6},{6,2},{3,7},{7,3},{8,12},{12,8},{9,1... | collective-permute-start | bytes 1572872 | tf_op jit(solution)/shard_map/ppermute | solution.py:1058
  657.7 13.4 %collective-permute-start.43 = (bf16[256,1024]{1,0:T(8,128)(2,1)S(1)}, bf16[256,1024]{1,0:T(8,128)(2,1)S(1)}, u32[]{:S(2)}, u32[]{:S(2)}) collective-permute-start(bf16[256,1024]{1,0:T(8,128)(2,1)S(1)} %copy-done.72), channel_id=1, source_target_pairs={{0,16},{8,24},{16,0},{24,8},{1,17},{9,25},{17,1},{25,9},{2,18},{10... | collective-permute-start | bytes 1572872 | tf_op jit(solution)/shard_map/ppermute | solution.py:1058
  665.6 16.7 %collective-permute-start.47 = (bf16[256,1024]{1,0:T(8,128)(2,1)S(1)}, bf16[256,1024]{1,0:T(8,128)(2,1)S(1)}, u32[]{:S(2)}, u32[]{:S(2)}) collective-permute-start(bf16[256,1024]{1,0:T(8,128)(2,1)S(1)} %add_convert_fusion.4), channel_id=1, source_target_pairs={{0,16},{8,24},{16,0},{24,8},{1,17},{9,25},{17,1},{25,9},{2,18},{10... | collective-permute-start | bytes 1572872 | tf_op jit(solution)/shard_map/ppermute | solution.py:1058
  667.2 15.1 %collective-permute-start.45 = (bf16[256,1024]{1,0:T(8,128)(2,1)}, bf16[256,1024]{1,0:T(8,128)(2,1)S(1)}, u32[]{:S(2)}, u32[]{:S(2)}) collective-permute-start(bf16[256,1024]{1,0:T(8,128)(2,1)} %get-tuple-element.220), channel_id=1, source_target_pairs={{0,4},{4,0},{1,5},{5,1},{2,6},{6,2},{3,7},{7,3},{8,12},{12,8},{9,1... | collective-permute-start | bytes 1572872 | tf_op jit(solution)/shard_map/ppermute | solution.py:1058
  672.3 15.6 %collective-permute-start.44 = (bf16[256,1024]{1,0:T(8,128)(2,1)S(1)}, bf16[256,1024]{1,0:T(8,128)(2,1)S(1)}, u32[]{:S(2)}, u32[]{:S(2)}) collective-permute-start(bf16[256,1024]{1,0:T(8,128)(2,1)S(1)} %add_convert_fusion.6), channel_id=1, source_target_pairs={{0,4},{4,0},{1,5},{5,1},{2,6},{6,2},{3,7},{7,3},{8,12},{12,8},{9,1... | collective-permute-start | bytes 1572872 | tf_op jit(solution)/shard_map/ppermute | solution.py:1058
  673.8 16.2 %collective-permute-start.41 = (bf16[256,1024]{1,0:T(8,128)(2,1)S(1)}, bf16[256,1024]{1,0:T(8,128)(2,1)S(1)}, u32[]{:S(2)}, u32[]{:S(2)}) collective-permute-start(bf16[256,1024]{1,0:T(8,128)(2,1)S(1)} %copy-done.71), channel_id=1, source_target_pairs={{0,16},{8,24},{16,0},{24,8},{1,17},{9,25},{17,1},{25,9},{2,18},{10... | collective-permute-start | bytes 1572872 | tf_op jit(solution)/shard_map/ppermute | solution.py:1058
  (86 other events, 608.5 us)
Sparse Core Ops, SparseCore 0:
  339.3 98.9 reduce-scatter.4
  440.6 44.6 reduce-scatter.6
  500.4 43.8 reduce-scatter.8
  546.6 113.7 reduce-scatter.10

commit v3 on v2

--- a/solution.py
+++ b/solution.py
@@ -364,8 +364,24 @@
 vmem_bytes = 56 * 1024 * 1024
 
 
+cost_share = 0.05
+
+
 def cost(flops, moved):
-    return pl.CostEstimate(flops=int(flops), bytes_accessed=int(moved), transcendentals=0)
+    return pl.CostEstimate(
+        flops=int(flops * cost_share), bytes_accessed=int(moved * cost_share), transcendentals=0
+    )
+
+
+def held(kernel, at, count):
+    def run(*refs):
+        kernel(*refs[:at], *refs[at + count :])
+
+    return run
+
+
+def anywhere(arrays):
+    return [pl.BlockSpec(memory_space=pl.ANY)] * len(arrays)
 
 
 def compiler_params():
@@ -553,25 +569,13 @@
     )(meta, qkv, qkv, qkv, bias)
 
 
-def backward_kernel(
-    scale,
-    head_size,
-    meta_ref,
-    q_ref,
-    k_ref,
-    v_ref,
-    bias_ref,
-    grad_ref,
-    full_ref,
-    total_ref,
-    ring_ref,
-    line_ref,
-    key_sum,
-    value_sum,
-    plane,
+def backward_body(
+    mine, length, scale, head_size, qkv_ref, bias_ref, grad_ref, full_ref, total_ref, ring_ref, line_ref, work,
+    after_pair=None,
 ):
-    _, blocks, span_rows, lanes = q_ref.shape
-    mine, length = meta_ref[0], meta_ref[1]
+    key_sum, value_sum, plane = work
+    blocks, span_rows, width = qkv_ref.shape
+    lanes = 128
     lane = lax.broadcasted_iota(jnp.int32, (1, lanes), 1)
     masks = key_masks(length, blocks, span_rows)
     halves = lanes // head_size
@@ -579,94 +583,112 @@
     def place(block):
         return lax.rem(mine - block + blocks, blocks)
 
-    key_sum[...] = jnp.zeros_like(key_sum)
-    value_sum[...] = jnp.zeros_like(value_sum)
-    plane[...] = jnp.zeros_like(plane)
-    for row in range(blocks):
-        queries = q_ref[0, place(row)]
-        grads = grad_ref[lax.rem(row - mine + blocks, blocks)]
-        products = grads.astype(jnp.float32) * full_ref[row]
-        totals = total_ref[row]
-        query_sum = jnp.zeros((span_rows, lanes), jnp.float32)
+    def one_pair(pair, carry):
+        wide = pl.multiple_of(pair * (3 * lanes), lanes)
+        own_lanes = pl.ds(pl.multiple_of(pair * lanes, lanes), lanes)
+        part = [pl.ds(pl.multiple_of(wide + which * lanes, lanes), lanes) for which in range(3)]
+        key_sum[...] = jnp.zeros_like(key_sum)
+        value_sum[...] = jnp.zeros_like(value_sum)
+        plane[...] = jnp.zeros_like(plane)
+        for row in range(blocks):
+            queries = qkv_ref[place(row), :, part[0]]
+            grads = grad_ref[lax.rem(row - mine + blocks, blocks), :, own_lanes]
+            products = grads.astype(jnp.float32) * full_ref[row, :, own_lanes]
+            totals = total_ref[row, :, own_lanes]
+            query_sum = jnp.zeros((span_rows, lanes), jnp.float32)
+            for half in range(halves):
+                own = lane // head_size == half
+                one = jnp.where(own, 1.0, 0.0).astype(jnp.bfloat16)
+                head_q = queries * jnp.where(own, scale, 0.0).astype(jnp.bfloat16)
+                head_g = grads * one
+                delta = jnp.sum(jnp.where(own, products, 0.0), axis=1, keepdims=True)
+                total = totals[:, half : half + 1]
+                for column in range(row + 1):
+                    at = (blocks - 1 - row + column) * span_rows
+                    keys = qkv_ref[place(column), :, part[1]]
+                    logits = dot_nt(head_q, keys)
+                    bias = bias_ref[pair * halves + half, :, at : at + span_rows]
+                    logits = logits + bias + masks[column]
+                    weights = jnp.exp(logits - total)
+                    weight_grads = dot_nt(head_g, qkv_ref[place(column), :, part[2]])
+                    score_grads = weights * (weight_grads - delta)
+                    plane[half, :, at : at + span_rows] += score_grads
+                    low_weights = weights.astype(jnp.bfloat16)
+                    low_grads = score_grads.astype(jnp.bfloat16)
+                    query_sum = query_sum + dot_nn(low_grads, keys * one)
+                    key_sum[column] += dot_tn(low_grads, head_q)
+                    value_sum[column] += dot_tn(low_weights, head_g)
+            ring_ref[place(row), :, part[0]] = (query_sum * scale).astype(jnp.bfloat16)
+        for row in range(blocks):
+            ring_ref[place(row), :, part[1]] = key_sum[row].astype(jnp.bfloat16)
+            ring_ref[place(row), :, part[2]] = value_sum[row].astype(jnp.bfloat16)
         for half in range(halves):
-            own = lane // head_size == half
-            one = jnp.where(own, 1.0, 0.0).astype(jnp.bfloat16)
-            head_q = queries * jnp.where(own, scale, 0.0).astype(jnp.bfloat16)
-            head_g = grads * one
-            delta = jnp.sum(jnp.where(own, products, 0.0), axis=1, keepdims=True)
-            total = totals[:, half : half + 1]
-            for column in range(row + 1):
-                at = (blocks - 1 - row + column) * span_rows
-                keys = k_ref[0, place(column)]
-                logits = dot_nt(head_q, keys)
-                logits = logits + bias_ref[half, :, at : at + span_rows] + masks[column]
-                weights = jnp.exp(logits - total)
-                weight_grads = dot_nt(head_g, v_ref[0, place(column)])
-                score_grads = weights * (weight_grads - delta)
-                plane[half, :, at : at + span_rows] += score_grads
-                low_weights = weights.astype(jnp.bfloat16)
-                low_grads = score_grads.astype(jnp.bfloat16)
-                query_sum = query_sum + dot_nn(low_grads, keys * one)
-                key_sum[column] += dot_tn(low_grads, head_q)
-                value_sum[column] += dot_tn(low_weights, head_g)
-        result = (query_sum * scale).astype(jnp.bfloat16)
-        ring_ref[place(row), :, :lanes] = result
-    for row in range(blocks):
-        result = key_sum[row].astype(jnp.bfloat16)
-        ring_ref[place(row), :, lanes : 2 * lanes] = result
-        result = value_sum[row].astype(jnp.bfloat16)
-        ring_ref[place(row), :, 2 * lanes :] = result
-    for half in range(halves):
-        full = jnp.concatenate(
-            [plane[half], jnp.zeros((span_rows, span_rows), jnp.float32)], axis=1
-        )
-        summed = jnp.sum(shear(full, True), axis=0, keepdims=True)
-        line_ref[half] = pltpu.roll(summed, span_rows - 1, 1)
-
-
-def attend_backward(meta, slot, qkv, bias, grads, full, totals, scale, head_size):
-    _, blocks, span_rows, width = qkv.shape
-    pairs = width // (3 * 128)
-    per_pair = bias.shape[0] // pairs
-    lanes = bias.shape[2] + span_rows
-
-    def part(which):
-        return pl.BlockSpec((1, blocks, span_rows, 128), lambda p: (slot, 0, 0, 3 * p + which))
-
-    plain = pl.BlockSpec((blocks, span_rows, 128), lambda p: (0, 0, p))
-    wide = pl.BlockSpec((blocks, span_rows, 384), lambda p: (0, 0, p))
-    return pl.pallas_call(
-        functools.partial(backward_kernel, scale, head_size),
-        grid=(pairs,),
-        in_specs=[
-            pl.BlockSpec(memory_space=pltpu.SMEM),
-            part(0),
-            part(1),
-            part(2),
-            pl.BlockSpec((per_pair,) + bias.shape[1:], lambda p: (p, 0, 0)),
-            plain,
-            plain,
-            plain,
-        ],
-        out_specs=[wide, pl.BlockSpec((per_pair, 1, lanes), lambda p: (p, 0, 0))],
-        out_shape=[
-            jax.ShapeDtypeStruct(qkv.shape[1:], jnp.bfloat16),
-            jax.ShapeDtypeStruct((bias.shape[0], 1, lanes), jnp.float32),
-        ],
-        scratch_shapes=[
-            pltpu.VMEM((blocks, span_rows, 128), jnp.float32),
-            pltpu.VMEM((blocks, span_rows, 128), jnp.float32),
-            pltpu.VMEM((per_pair,) + bias.shape[1:], jnp.float32),
-        ],
-        cost_estimate=cost(20e9, 12e6),
-        compiler_params=compiler_params(),
-        name="attend_backward",
-    )(meta, qkv, qkv, qkv, bias, grads, full, totals)
-
-
-def own_rows(meta_ref, span_rows):
-    position = meta_ref[0] * span_rows + lax.broadcasted_iota(jnp.int32, (span_rows, 1), 0)
-    return jnp.where(position < meta_ref[1], 1.0, 0.0)
+            full = jnp.concatenate(
+                [plane[half], jnp.zeros((span_rows, span_rows), jnp.float32)], axis=1
+            )
+            summed = jnp.sum(shear(full, True), axis=0, keepdims=True)
+            line_ref[pair * halves + half] = pltpu.roll(summed, span_rows - 1, 1)
+        if after_pair is not None:
+            after_pair(pair)
+        return carry
+
+    lax.fori_loop(0, width // (3 * lanes), one_pair, 0)
+
+
+def backward_work(blocks, span_rows, head_size):
+    return [
+        pltpu.VMEM((blocks, span_rows, 128), jnp.float32),
+        pltpu.VMEM((blocks, span_rows, 128), jnp.float32),
+        pltpu.VMEM((128 // head_size, span_rows, blocks * span_rows), jnp.float32),
+    ]
+
+
+def greet(*others):
+    barrier = pltpu.get_barrier_semaphore()
+    for other in others:
+        pl.semaphore_signal(
+            barrier, inc=1, device_id=other, device_id_type=pl.DeviceIdType.MESH
+        )
+    pl.semaphore_wait(barrier, len(others))
+
+
+def push(source, target, send_sem, recv_sem, other):
+    return pltpu.make_async_remote_copy(
+        src_ref=source,
+        dst_ref=target,
+        send_sem=send_sem,
+        recv_sem=recv_sem,
+        device_id=other,
+        device_id_type=pl.DeviceIdType.MESH,
+    )
+
+
+def ring_others(mine, count):
+    return [{"cp": lax.rem(mine + j, count)} for j in range(1, count)]
+
+
+def deliveries(source, target, sems, mine, count):
+    return [
+        push(
+            source.at[j],
+            target.at[j],
+            sems.at[0, j],
+            sems.at[1, j],
+            {"cp": lax.rem(mine + (count - j), count)},
+        )
+        for j in range(1, count)
+    ]
+
+
+def remote_params(number):
+    return pltpu.CompilerParams(
+        vmem_limit_bytes=vmem_bytes, collective_id=number, has_side_effects=True
+    )
+
+
+def own_rows(block, length, span_rows):
+    position = block * span_rows + lax.broadcasted_iota(jnp.int32, (span_rows, 1), 0)
+    return jnp.where(position < length, 1.0, 0.0)
 
 
 def router_of(rows, router_w, experts):
@@ -686,16 +708,16 @@
             at = pl.multiple_of((group * count + owner) * 128, 128)
             attended_ref[:, pl.ds(at, 128)] = part[:, group * 128 : (group + 1) * 128]
     projected = dot_nn(attended_ref[...], weight_ref[...])
-    hidden = input_ref[...].astype(jnp.float32) + own_rows(meta_ref, projected.shape[0]) * projected
+    hidden = input_ref[...].astype(jnp.float32) + own_rows(meta_ref[0], meta_ref[1], projected.shape[0]) * projected
     hidden_ref[...] = hidden
     normed_ref[...] = (hidden * root_scale(hidden) * gain_ref[...]).astype(jnp.bfloat16)
 
 
-def project_rows(meta, inputs, gain, w_attn, parts):
+def project_rows(meta, inputs, gain, w_attn, parts, waits=()):
     span_rows, model_width = inputs.shape
     whole = pl.BlockSpec(memory_space=pltpu.VMEM)
     return pl.pallas_call(
-        project_kernel,
+        held(project_kernel, 4 + len(parts), len(waits)),
         grid=(1,),
         in_specs=[
             pl.BlockSpec(memory_space=pltpu.SMEM),
@@ -703,7 +725,8 @@
             whole,
             pl.BlockSpec((model_width, model_width), lambda i: (0, 3)),
         ]
-        + [whole] * len(parts),
+        + [whole] * len(parts)
+        + anywhere(waits),
         out_specs=[whole] * 3,
         out_shape=[
             jax.ShapeDtypeStruct((span_rows, model_width), jnp.bfloat16),
@@ -713,32 +736,17 @@
         cost_estimate=cost(2e9, 6e6),
         compiler_params=compiler_params(),
         name="project_rows",
-    )(meta, inputs, gain, w_attn, *parts)
-
-
-def hidden_kernel(
-    experts,
-    meta_ref,
-    own_ref,
-    first_ref,
-    last_ref,
-    grad_ref,
-    hidden_ref,
-    normed_ref,
-    gain_ref,
-    router_ref,
-    weight_ref,
-    *refs,
+    )(meta, inputs, gain, w_attn, *parts, *waits)
+
+
+def hidden_body(
+    experts, mine, length, own, first, last, grad_ref, hidden_ref, normed_ref, gain_ref, router_ref, weight_ref,
+    hidden_grad_ref, proj_ref, router_grad_ref, gain_grad_ref, leaving_ref, attended,
 ):
-    hidden_grad_ref, proj_ref, router_grad_ref, gain_grad_ref = refs[:4]
-    leaving, attended = refs[4:-1], refs[-1]
-    count = len(leaving)
+    count = leaving_ref.shape[0]
     span_rows, model_width = hidden_ref.shape
-    back = (
-        own_ref[...].astype(jnp.float32)
-        + first_ref[...].astype(jnp.float32)
-        + last_ref[...].astype(jnp.float32)
-    )
+    back = own[...].astype(jnp.float32) + first[...].astype(jnp.float32)
+    back = back + last[...].astype(jnp.float32)
     normed = normed_ref[...]
     probs = router_of(normed, router_ref[...], experts)
     shares = back[:, model_width:]
@@ -753,80 +761,408 @@
         grads, hidden, scale_rows, gain_ref[...]
     )
     hidden_grad_ref[...] = hidden_grads
-    proj = (own_rows(meta_ref, span_rows) * hidden_grads).astype(jnp.bfloat16)
+    proj = (own_rows(mine, length, span_rows) * hidden_grads).astype(jnp.bfloat16)
     proj_ref[...] = proj
     attended[...] = dot_nt(proj, weight_ref[...]).astype(jnp.bfloat16)
-    for j, part in enumerate(leaving):
-        owner = lax.rem(meta_ref[0] + (count - j), count)
-        for group in range(part.shape[1] // 128):
+    for j in range(count):
+        owner = lax.rem(mine + (count - j), count)
+        for group in range(leaving_ref.shape[2] // 128):
             at = pl.multiple_of((group * count + owner) * 128, 128)
-            part[:, group * 128 : (group + 1) * 128] = attended[:, pl.ds(at, 128)]
-
-
-def hidden_back(meta, own, first, last, grads, hidden, normed, gain, router, w_attn, experts, count):
-    span_rows, model_width = hidden.shape
+            leaving_ref[j, :, group * 128 : (group + 1) * 128] = attended[:, pl.ds(at, 128)]
+
+
+def hidden_kernel(
+    experts, scale, head_size, slots, length_ref, gain_ref, router_ref, weight_ref, qkv_ref, bias_ref, full_ref, total_ref, *refs
+):
+    per_slot = [refs[6 * s : 6 * s + 6] for s in range(slots)]
+    refs = refs[6 * slots :]
+    outs = [refs[4 * s : 4 * s + 4] for s in range(slots)]
+    ring_ref, line_ref, rest_ref, leaving, arriving, attended, sems = refs[4 * slots : 4 * slots + 7]
+    work = refs[4 * slots + 7 :]
+    count = qkv_ref.shape[1]
+    mine = lax.axis_index("cp")
+    greet(*ring_others(mine, count))
+    copies = []
+    for s in range(slots):
+        hidden_body(
+            experts, mine, length_ref[s], *per_slot[s], gain_ref, router_ref, weight_ref,
+            *outs[s], leaving.at[s], attended,
+        )
+        target = arriving if s == 0 else rest_ref.at[s - 1]
+        copies.append(deliveries(leaving.at[s], target, sems.at[s], mine, count))
+        for copy in copies[s]:
+            copy.start()
+        target[0] = leaving[s, 0]
+    for copy in copies[0]:
+        copy.wait()
+    backward_body(
+        mine, length_ref[0], scale, head_size, qkv_ref.at[0], bias_ref, arriving, full_ref, total_ref,
+        ring_ref, line_ref, work,
+    )
+    for copy in (copy for some in copies[1:] for copy in some):
+        copy.wait()
+
+
+def hidden_back(
+    lengths, back_rows, grads, hidden, normed, gain, router, w_attn, experts, qkvs, bias, full, total, scale, head_size, waits=()
+):
+    slots, count, span_rows, own_width = qkvs.shape
+    model_width = hidden[0].shape[1]
+    heads = bias.shape[0]
     whole = pl.BlockSpec(memory_space=pltpu.VMEM)
     f32, bf16 = jnp.float32, jnp.bfloat16
-    return pl.pallas_call(
-        functools.partial(hidden_kernel, experts),
+    each = []
+    for s in range(slots):
+        each += [*back_rows[s], grads[s], hidden[s], normed[s]]
+    own_shape = (count, span_rows, own_width // 3)
+    got = pl.pallas_call(
+        held(
+            functools.partial(hidden_kernel, experts, scale, head_size, slots),
+            8 + len(each),
+            len(waits),
+        ),
         grid=(1,),
-        in_specs=[pl.BlockSpec(memory_space=pltpu.SMEM)]
-        + [whole] * 8
-        + [pl.BlockSpec((model_width, model_width), lambda i: (0, 3))],
-        out_specs=[whole] * (4 + count),
+        in_specs=[
+            pl.BlockSpec(memory_space=pltpu.SMEM),
+            whole,
+            whole,
+            pl.BlockSpec((model_width, model_width), lambda i: (0, 3)),
+            pl.BlockSpec((1,) + qkvs.shape[1:], lambda i: (0, 0, 0, 0)),
+        ]
+        + [whole] * (3 + len(each))
+        + anywhere(waits),
+        out_specs=[whole] * (4 * slots + 3),
         out_shape=[
             jax.ShapeDtypeStruct((span_rows, model_width), f32),
             jax.ShapeDtypeStruct((span_rows, model_width), bf16),
             jax.ShapeDtypeStruct((model_width, router.shape[1]), f32),
             jax.ShapeDtypeStruct((1, model_width), f32),
         ]
-        + [jax.ShapeDtypeStruct((span_rows, model_width // count), bf16)] * count,
-        scratch_shapes=[pltpu.VMEM((span_rows, model_width), bf16)],
-        cost_estimate=cost(3e9, 8e6),
-        compiler_params=compiler_params(),
+        * slots
+        + [
+            jax.ShapeDtypeStruct(qkvs.shape[1:], bf16),
+            jax.ShapeDtypeStruct((heads, 1, bias.shape[2] + span_rows), f32),
+            jax.ShapeDtypeStruct((slots - 1,) + own_shape, bf16),
+        ],
+        scratch_shapes=[
+            pltpu.VMEM((slots,) + own_shape, bf16),
+            pltpu.VMEM(own_shape, bf16),
+            pltpu.VMEM((span_rows, model_width), bf16),
+            pltpu.SemaphoreType.DMA((slots, 2, count)),
+        ]
+        + backward_work(count, span_rows, head_size),
+        cost_estimate=cost(20e9, 20e6),
+        compiler_params=remote_params(1),
         name="hidden_back",
-    )(meta, own, first, last, grads, hidden, normed, gain, router, w_attn)
-
-
-def token_kernel(meta_ref, input_ref, hidden_ref, gain_ref, weight_ref, *refs):
-    parts, out_ref = refs[:-1], refs[-1]
-    count = len(parts)
+    )(lengths, gain, router, w_attn, qkvs, bias, full, total, *each, *waits)
+    return [got[4 * s : 4 * s + 4] for s in range(slots)], got[4 * slots :]
+
+
+def near_others(dp, ep):
+    core, across = lax.rem(dp, 2), dp // 2
+    return (
+        {"dp": across * 2 + (1 - core)},
+        {"dp": (1 - across) * 2 + core},
+        {"ep": 1 - ep},
+    )
+
+
+def second_kernel(
+    scale, head_size, slots, length_ref, former_ref, normed_ref, qkv_ref, bias_ref, grad_ref, full_ref, total_ref,
+    *refs,
+):
+    attended, proj, refs = refs[:slots], refs[slots : 2 * slots], refs[2 * slots :]
+    ring_ref, line_ref, arrived_ref, weight_ref, rows_ref = refs[:5]
+    sums, low, got_core, got_x, got_y, leaving, coming, sems, near_sems, last_sems = refs[5:15]
+    work = refs[15:]
+    count = qkv_ref.shape[1]
+    mine = lax.axis_index("cp")
+    dp, ep = lax.axis_index("dp"), lax.axis_index("ep")
+    core, across = lax.rem(dp, 2), dp // 2
+    others = near_others(dp, ep)
+    greet(*ring_others(mine, count), *others)
+    copies = deliveries(former_ref, arrived_ref, sems, mine, count)
+    for copy in copies:
+        copy.start()
+    arrived_ref[0] = former_ref[0]
+    height = sums.shape[0] // 2
+    sizes = (height, height // 2, height // 4)
+    bits = (core, across, ep)
+    landing = (got_core, got_x, got_y)
+    total = None
+    for s in range(slots):
+        term = dot_tn(attended[s][...], proj[s][...])
+        total = term if total is None else total + term
+    sums[...] = total
+
+    def low_part(stage):
+        return low.at[stage, pl.ds(0, sizes[stage])]
+
+    def stage_copy(stage):
+        return push(
+            low_part(stage), landing[stage], near_sems.at[0, stage], near_sems.at[1, stage], others[stage]
+        )
+
+    def start_of(stage):
+        start = 0
+        for former in range(stage):
+            start = start + bits[former] * sizes[former]
+        return start
+
+    def begin(stage):
+        at = start_of(stage) + (1 - bits[stage]) * sizes[stage]
+        away = sums[pl.ds(pl.multiple_of(at, 128), sizes[stage]), :]
+        low[stage, : sizes[stage]] = away.astype(jnp.bfloat16)
+        stage_copy(stage).start()
+
+    def finish(stage):
+        stage_copy(stage).wait()
+        at = pl.ds(pl.multiple_of(start_of(stage + 1), 128), sizes[stage])
+        sums[at, :] = sums[at, :] + landing[stage][...].astype(jnp.float32)
+
+    def after_pair(pair):
+        for stage in range(2):
+
+            @pl.when(pair == stage)
+            def _():
+                finish(stage)
+                begin(stage + 1)
+
+    begin(0)
+    backward_body(
+        mine, length_ref[1], scale, head_size, qkv_ref.at[0], bias_ref, grad_ref.at[0], full_ref, total_ref,
+        ring_ref, line_ref, work, after_pair,
+    )
+    finish(2)
+    at = pl.ds(pl.multiple_of(start_of(3), 128), sizes[2])
+    groups = leaving.shape[2] // 128
+    for j in range(count):
+        owner = lax.rem(mine + (count - j), count)
+        for group in range(groups):
+            lanes = pl.ds(pl.multiple_of((group * count + owner) * 128, 128), 128)
+            part = sums[at, lanes]
+            leaving[j, :, group * 128 : (group + 1) * 128] = part.astype(jnp.bfloat16)
+            if j == 0:
+                rows_ref[:, group * 128 : (group + 1) * 128] = part
+    last = deliveries(leaving, coming, last_sems, mine, count)
+    for copy in last:
+        copy.start()
+    total = None
+    for j in range(count):
+        term = dot_tn(normed_ref[0, j], former_ref[j])
+        total = term if total is None else total + term
+    weight_ref[...] = total
+    for copy in last:
+        copy.wait()
+    for j in range(1, count):
+        rows_ref[...] = rows_ref[...] + coming[j].astype(jnp.float32)
+    for copy in copies:
+        copy.wait()
+
+
+def second_back(
+    lengths, former, normed_all, qkvs, bias, grads, full, total, attended, proj, scale, head_size, waits=()
+):
+    slots, count, span_rows, own_width = qkvs.shape
+    model_width = normed_all.shape[3]
+    whole = pl.BlockSpec(memory_space=pltpu.VMEM)
+    slot = lambda a, s: pl.BlockSpec((1,) + a.shape[1:], lambda i: (s,) + (0,) * (len(a.shape) - 1))
+    f32, bf16 = jnp.float32, jnp.bfloat16
+    rows_shape = (model_width // 8, own_width // 3)
+    return pl.pallas_call(
+        held(
+            functools.partial(second_kernel, scale, head_size, slots), 8 + 2 * slots, len(waits)
+        ),
+        grid=(1,),
+        in_specs=[
+            pl.BlockSpec(memory_space=pltpu.SMEM),
+            whole,
+            slot(normed_all, 0),
+            slot(qkvs, 1),
+            whole,
+            whole,
+            whole,
+            whole,
+        ]
+        + [whole] * (2 * slots)
+        + anywhere(waits),
+        out_specs=[whole] * 5,
+        out_shape=[
+            jax.ShapeDtypeStruct(qkvs.shape[1:], bf16),
+            jax.ShapeDtypeStruct((bias.shape[0], 1, bias.shape[2] + span_rows), f32),
+            jax.ShapeDtypeStruct(qkvs.shape[1:], bf16),
+            jax.ShapeDtypeStruct((model_width, own_width), f32),
+            jax.ShapeDtypeStruct(rows_shape, f32),
+        ],
+        scratch_shapes=[
+            pltpu.VMEM((model_width, model_width), f32),
+            pltpu.VMEM((3, model_width // 2, model_width), bf16),
+            pltpu.VMEM((model_width // 2, model_width), bf16),
+            pltpu.VMEM((model_width // 4, model_width), bf16),
+            pltpu.VMEM((model_width // 8, model_width), bf16),
+            pltpu.VMEM((count,) + rows_shape, bf16),
+            pltpu.VMEM((count,) + rows_shape, bf16),
+            pltpu.SemaphoreType.DMA((2, count)),
+            pltpu.SemaphoreType.DMA((2, 3)),
+            pltpu.SemaphoreType.DMA((2, count)),
+        ]
+        + backward_work(count, span_rows, head_size),
+        cost_estimate=cost(20e9, 20e6),
+        compiler_params=remote_params(2),
+        name="second_back",
+    )(lengths, former, normed_all, qkvs, bias, grads, full, total, *attended, *proj, *waits)
+
+
+def token_body(mine, input_ref, hidden_ref, gain_ref, weight_ref, parts_ref, own_ref, out_ref):
+    count = parts_ref.shape[0]
     model_width = input_ref.shape[1]
     total = None
-    for j, part in enumerate(parts):
-        owner = lax.rem(meta_ref[0] + j, count)
+    for j in range(count):
+        owner = lax.rem(mine + j, count)
         pieces = []
-        for group in range(part.shape[1] // 384):
+        for group in range(parts_ref.shape[2] // 384):
             for which in range(3):
                 at = which * model_width + (group * count + owner) * 128
                 pieces.append(weight_ref[:, pl.ds(pl.multiple_of(at, 128), 128)])
-        term = dot_nt(part[...], jnp.concatenate(pieces, axis=1))
+        part = own_ref[j] if j == 0 else parts_ref[j]
+        term = dot_nt(part, jnp.concatenate(pieces, axis=1))
         total = term if total is None else total + term
     inputs = input_ref[...].astype(jnp.float32)
     back = norm_back(total, inputs, root_scale(inputs), gain_ref[...])
     out_ref[...] = (hidden_ref[...] + back).astype(jnp.bfloat16)
 
 
-def token_grads(meta, inputs, hidden_grads, gain, w_attn, parts):
-    span_rows, model_width = inputs.shape
+def final_kernel(
+    slots, ring_ref, normed_ref, former_ref, own_w_ref, arrived_ref, blocks_ref, small_ref, gain_ref, weight_ref, *refs
+):
+    inputs, hiddens, refs = refs[:slots], refs[slots : 2 * slots], refs[2 * slots :]
+    outs, refs = refs[:slots], refs[slots:]
+    small_out, attn_out = refs[:2]
+    coming, here, sum_blocks, low_blocks, small_now, small_in, sems, near_sems, small_sems = refs[2:11]
+    got_core, got_x, got_y = refs[11:]
+    count = ring_ref.shape[0]
+    mine = lax.axis_index("cp")
+    dp, ep = lax.axis_index("dp"), lax.axis_index("ep")
+    core, across = lax.rem(dp, 2), dp // 2
+    core_other, x_other, y_other = near_others(dp, ep)
+    greet(*ring_others(mine, count), core_other, x_other, y_other)
+    copies = deliveries(ring_ref, coming, sems, mine, count)
+    for copy in copies:
+        copy.start()
+
+    total = former_ref[...]
+    for j in range(count):
+        total = total + dot_tn(normed_ref[0, j], ring_ref[j])
+    ones = jnp.ones((8, total.shape[1]), jnp.float32)
+    first_gain = lax.dot_general(
+        ones,
+        total * own_w_ref[...].astype(jnp.float32),
+        (((1,), (1,)), ((), ())),
+        precision=lax.Precision.HIGHEST,
+        preferred_element_type=jnp.float32,
+    )
+    row = lax.broadcasted_iota(jnp.int32, small_ref.shape, 0)
+    small_now[0] = jnp.where(row == 6, first_gain / gain_ref[...], small_ref[...])
+    groups = total.shape[1] // 384
+    for group in range(groups):
+        for which in range(3):
+            at = (group * 3 + which) * 128
+            part = total[:, at : at + 128]
+            sum_blocks[which % 2, which // 2, group] = part
+            low_blocks[which % 2, which // 2, group] = part.astype(jnp.bfloat16)
+        height = blocks_ref.shape[0]
+        here_rows = pl.ds(pl.multiple_of((core * 4 + across * 2 + ep) * height, 128), height)
+        part = blocks_ref[:, group * 128 : (group + 1) * 128]
+        sum_blocks[1, 1, group] = jnp.zeros_like(sum_blocks[1, 1, group])
+        low_blocks[1, 1, group] = jnp.zeros_like(low_blocks[1, 1, group])
+        sum_blocks[1, 1, group, here_rows] = part
+        low_blocks[1, 1, group, here_rows] = part.astype(jnp.bfloat16)
+    first = push(low_blocks.at[1 - core], got_core, near_sems.at[0, 0], near_sems.at[1, 0], core_other)
+    first.start()
+
+    stages = [core_other, x_other, y_other]
+    step = 1
+    while step < count:
+        flip = mine + step - 2 * step * lax.rem(mine // step, 2)
+        stages.append({"cp": flip})
+        step *= 2
+
+    def small_push(at):
+        return push(small_now.at[at], small_in.at[at], small_sems.at[0, at], small_sems.at[1, at], stages[at])
+
+    small_push(0).start()
+    token_body(mine, inputs[0], hiddens[0], gain_ref, weight_ref, arrived_ref, arrived_ref, outs[0])
+    first.wait()
+    here[...] = sum_blocks[core] + got_core[...].astype(jnp.float32)
+    low_blocks[0, 0] = here[1 - across].astype(jnp.bfloat16)
+    second = push(low_blocks.at[0, 0], got_x, near_sems.at[0, 1], near_sems.at[1, 1], x_other)
+    second.start()
+    for at in range(len(stages)):
+        small_push(at).wait()
+        now = small_now[at] + small_in[at]
+        if at + 1 < len(stages):
+            small_now[at + 1] = now
+            small_push(at + 1).start()
+        else:
+            small_out[...] = now
+        if at == 1:
+            second.wait()
+            sum_blocks[0, 0] = here[across] + got_x[...].astype(jnp.float32)
+            low_blocks[0, 1, 0] = sum_blocks[0, 0, 1 - ep].astype(jnp.bfloat16)
+            third = push(low_blocks.at[0, 1, 0], got_y, near_sems.at[0, 2], near_sems.at[1, 2], y_other)
+            third.start()
+    third.wait()
+    attn_out[...] = sum_blocks[0, 0, ep] + got_y[...].astype(jnp.float32)
+    for copy in copies:
+        copy.wait()
+    token_body(mine, inputs[1], hiddens[1], gain_ref, weight_ref, coming, ring_ref, outs[1])
+
+
+def final_back(ring, normed_all, former, own_w, arrived, blocks, small, gain, w_attn, inputs, hiddens):
+    count, span_rows, own_width = ring.shape
+    slots = len(inputs)
+    model_width = inputs[0].shape[1]
+    groups = blocks.shape[1] // 128
     whole = pl.BlockSpec(memory_space=pltpu.VMEM)
+    f32, bf16 = jnp.float32, jnp.bfloat16
+    stages = 3 + (count - 1).bit_length()
+    tile = (model_width, 128)
     return pl.pallas_call(
-        token_kernel,
+        functools.partial(final_kernel, slots),
         grid=(1,),
         in_specs=[
-            pl.BlockSpec(memory_space=pltpu.SMEM),
+            whole,
+            pl.BlockSpec((1,) + normed_all.shape[1:], lambda i: (1, 0, 0, 0)),
+            whole,
+            whole,
+            whole,
             whole,
             whole,
             whole,
             pl.BlockSpec((model_width, 3 * model_width), lambda i: (0, 0)),
         ]
-        + [whole] * len(parts),
-        out_specs=whole,
-        out_shape=jax.ShapeDtypeStruct((span_rows, model_width), jnp.bfloat16),
-        cost_estimate=cost(4e9, 8e6),
-        compiler_params=compiler_params(),
-        name="token_grads",
-    )(meta, inputs, hidden_grads, gain, w_attn, *parts)
+        + [whole] * (2 * slots),
+        out_specs=[whole] * (slots + 2),
+        out_shape=[jax.ShapeDtypeStruct((span_rows, model_width), bf16)] * slots
+        + [jax.ShapeDtypeStruct(small.shape, f32), jax.ShapeDtypeStruct(tile, f32)],
+        scratch_shapes=[
+            pltpu.VMEM(ring.shape, bf16),
+            pltpu.VMEM((2, groups) + tile, f32),
+            pltpu.VMEM((2, 2, groups) + tile, f32),
+            pltpu.VMEM((2, 2, groups) + tile, bf16),
+            pltpu.VMEM((stages,) + small.shape, f32),
+            pltpu.VMEM((stages,) + small.shape, f32),
+            pltpu.SemaphoreType.DMA((2, count)),
+            pltpu.SemaphoreType.DMA((2, 3)),
+            pltpu.SemaphoreType.DMA((2, stages)),
+            pltpu.VMEM((2, groups) + tile, bf16),
+            pltpu.VMEM((groups,) + tile, bf16),
+            pltpu.VMEM(tile, bf16),
+        ],
+        cost_estimate=cost(20e9, 20e6),
+        compiler_params=remote_params(3),
+        name="final_back",
+    )(ring, normed_all, former, own_w, arrived, blocks, small, gain, w_attn, *inputs, *hiddens)
 
 
 gelu_inner = 0.7978845608028654
@@ -854,32 +1190,35 @@
             out_ref[source, expert] = picked.astype(jnp.bfloat16)
 
 
-def pick_rows(base, targets, blocks, experts, capacity):
+def pick_rows(base, targets, blocks, experts, capacity, waits=()):
     flat = [part for parts in blocks for part in parts]
     width = flat[0].shape[1]
     whole = pl.BlockSpec(memory_space=pltpu.VMEM)
     return pl.pallas_call(
-        pick_kernel,
-        in_specs=[pl.BlockSpec(memory_space=pltpu.SMEM)] + [whole] * (1 + len(flat)),
+        held(pick_kernel, 2 + len(flat), len(waits)),
+        in_specs=[pl.BlockSpec(memory_space=pltpu.SMEM)]
+        + [whole] * (1 + len(flat))
+        + anywhere(waits),
         out_specs=whole,
         out_shape=jax.ShapeDtypeStruct((len(blocks), experts, capacity, width), jnp.bfloat16),
         cost_estimate=cost(1.6e9 * len(blocks), 3e6 * len(blocks)),
         compiler_params=compiler_params(),
         name="pick_rows",
-    )(base, targets, *flat)
-
-
-def place_kernel(base_ref, target_ref, mine_ref, theirs_ref, *out_refs):
-    sources, experts, capacity, _ = mine_ref.shape
+    )(base, targets, *flat, *waits)
+
+
+def place_kernel(experts, base_ref, target_ref, *refs):
+    pairs = [refs[2 * e : 2 * e + 2] for e in range(experts)]
+    out_refs = refs[2 * experts :]
+    sources, capacity, _ = pairs[0][0].shape
     parts = len(out_refs) // sources
     span = out_refs[0].shape[0]
     for source in range(sources):
         both = [
-            (
-                mine_ref[source, expert].astype(jnp.float32)
-                + theirs_ref[source, expert].astype(jnp.float32)
-            ).astype(jnp.bfloat16)
-            for expert in range(experts)
+            (mine[source].astype(jnp.float32) + theirs[source].astype(jnp.float32)).astype(
+                jnp.bfloat16
+            )
+            for mine, theirs in pairs
         ]
         for at in range(parts):
             total = None
@@ -895,42 +1234,49 @@
             out_refs[source * parts + at][...] = total.astype(jnp.bfloat16)
 
 
-def place_rows(base, targets, mine, theirs, parts):
-    sources, experts, capacity, width = mine.shape
+def place_rows(base, targets, pairs, parts, waits=()):
+    sources, capacity, width = pairs[0][0].shape
     span = targets.shape[1] // parts
     whole = pl.BlockSpec(memory_space=pltpu.VMEM)
+    flat = [part for pair in pairs for part in pair]
     return pl.pallas_call(
-        place_kernel,
-        in_specs=[pl.BlockSpec(memory_space=pltpu.SMEM), whole, whole, whole],
+        held(functools.partial(place_kernel, len(pairs)), 2 + len(flat), len(waits)),
+        in_specs=[pl.BlockSpec(memory_space=pltpu.SMEM)]
+        + [whole] * (1 + len(flat))
+        + anywhere(waits),
         out_specs=[whole] * (sources * parts),
         out_shape=[jax.ShapeDtypeStruct((span, width), jnp.bfloat16)] * (sources * parts),
         cost_estimate=cost(1.6e9 * sources, 4e6 * sources),
         compiler_params=compiler_params(),
         name="place_rows",
-    )(base, targets, mine, theirs)
+    )(base, targets, *flat, *waits)
 
 
 def expert_kernel(
     experts,
     own_units,
     kept_count,
+    ends,
     first_ref,
     window_ref,
-    rows_mine,
-    rows_theirs,
-    grads_mine,
-    grads_theirs,
-    router_ref,
-    gate_ref,
-    up_ref,
-    down_ref,
     *refs,
 ):
-    back_mine, back_theirs, out_mine, out_theirs = refs[kept_count : kept_count + 4]
-    kept_rows, kept_grads, kept_gate, kept_up, kept_inner = refs[kept_count + 4 :]
-    capacity, model_width = rows_mine.shape[2:]
-    rows = jnp.concatenate([rows_mine[0, 0], rows_theirs[0, 0]], axis=0)
-    grads = jnp.concatenate([grads_mine[0, 0], grads_theirs[0, 0]], axis=0)
+    given, refs = refs[: 4 * len(ends)], refs[4 * len(ends) :]
+    router_ref, gate_ref, up_ref, down_ref = refs[:4]
+    refs = refs[4 + kept_count :]
+    back_mine, back_theirs, out_mine, out_theirs = refs[:4]
+    kept_rows, kept_grads, kept_gate, kept_up, kept_inner = refs[4:]
+    capacity, model_width = given[0].shape[2:]
+    source = pl.program_id(1)
+
+    def chosen(which):
+        value = given[which][0, 0]
+        for at in range(1, len(ends)):
+            value = jnp.where(source < ends[at - 1], value, given[4 * at + which][0, 0])
+        return value
+
+    rows = jnp.concatenate([chosen(0), chosen(1)], axis=0)
+    grads = jnp.concatenate([chosen(2), chosen(3)], axis=0)
     kept_rows[0, 0] = rows
     kept_grads[0, 0] = grads
     lane = lax.broadcasted_iota(jnp.int32, (1, router_ref.shape[1]), 1)
@@ -967,48 +1313,60 @@
         out_ref[0, 0] = out[part]
 
 
-def run_experts(
-    first, window, mine, theirs, grads_mine, grads_theirs, router, weights, kept, at, total, experts, units
-):
-    sources, exp_dev, capacity, model_width = mine.shape
+def run_experts(first, window, given, router, weights, kept, at, total, experts, units, chosen):
+    low, high = chosen
+    _, exp_dev, capacity, model_width = given[0][0].shape
+    sizes = [group[0].shape[0] for group in given]
+    ends = [sum(sizes[: i + 1]) for i in range(len(sizes))]
+    sources = ends[-1]
     wide_units = aligned_units(units)
     tile = 2 * capacity
-    rows = pl.BlockSpec((1, 1, capacity, model_width), lambda e, k, f, w: (k, e, 0, 0))
-    wide = pl.BlockSpec((1, 1, capacity, model_width + 128), lambda e, k, f, w: (k, e, 0, 0))
+
+    def rows_of(i):
+        start, size = ends[i] - sizes[i], sizes[i]
+        return pl.BlockSpec(
+            (1, 1, capacity, model_width),
+            lambda e, k, f, w: (jnp.clip(k - start, 0, size - 1), low + e, 0, 0),
+        )
+
+    out = lambda width: pl.BlockSpec((1, 1, capacity, width), lambda e, k, f, w: (e, k, 0, 0))
+    wide, rows = out(model_width + 128), out(model_width)
     weight = pl.BlockSpec(
         (pl.Element(1), pl.Element(model_width), pl.Element(wide_units)),
-        lambda e, k, f, w: (e, 0, pl.multiple_of(w[0], 128)),
-    )
-    keep = lambda width: pl.BlockSpec((1, 1, tile, width), lambda e, k, f, w: (e, at + k, 0, 0))
+        lambda e, k, f, w: (low + e, 0, pl.multiple_of(w[0], 128)),
+    )
+    keep = lambda width: pl.BlockSpec(
+        (1, 1, tile, width), lambda e, k, f, w: (low + e, at + k, 0, 0)
+    )
     keep_widths = (model_width, model_width, wide_units, wide_units, wide_units)
     kept = list(kept)
-    back_shape = jax.ShapeDtypeStruct((sources, exp_dev, capacity, model_width + 128), jnp.bfloat16)
-    out_shape = jax.ShapeDtypeStruct((sources, exp_dev, capacity, model_width), jnp.bfloat16)
+    flat = [part for group in given for part in group]
+    out_of = lambda width: jax.ShapeDtypeStruct(
+        (high - low, sources, capacity, width), jnp.bfloat16
+    )
+    back_shape, out_shape = out_of(model_width + 128), out_of(model_width)
     got = pl.pallas_call(
-        functools.partial(expert_kernel, experts, units, len(kept)),
+        functools.partial(expert_kernel, experts, units, len(kept), tuple(ends)),
         grid_spec=pltpu.PrefetchScalarGridSpec(
             num_scalar_prefetch=2,
-            grid=(exp_dev, sources),
-            in_specs=[
-                rows,
-                rows,
-                rows,
-                rows,
+            grid=(high - low, sources),
+            in_specs=[rows_of(i) for i in range(len(given)) for _ in range(4)]
+            + [
                 pl.BlockSpec(router.shape, lambda e, k, f, w: (0, 0)),
                 weight,
                 weight,
                 weight,
             ]
-            + [pl.BlockSpec(memory_space=pl.ANY)] * len(kept),
+            + anywhere(kept),
             out_specs=[wide, wide, rows, rows] + [keep(width) for width in keep_widths],
         ),
         out_shape=[back_shape, back_shape, out_shape, out_shape]
         + [jax.ShapeDtypeStruct((exp_dev, total, tile, w), jnp.bfloat16) for w in keep_widths],
-        input_output_aliases={10 + i: 4 + i for i in range(len(kept))},
+        input_output_aliases={6 + len(flat) + i: 4 + i for i in range(len(kept))},
         cost_estimate=cost(20e9 * sources, 8e6 * sources),
         compiler_params=compiler_params(),
         name="expert_rows",
-    )(first, window, mine, theirs, grads_mine, grads_theirs, router, *weights, *kept)
+    )(first + low, window, *flat, router, *weights, *kept)
     return got[:4], got[4:]
 
 
@@ -1036,22 +1394,24 @@
             weight_ref[at] = got.astype(jnp.bfloat16)
 
 
-def weight_grads(window, kept, expert, pieces, units):
+def weight_grads(window, kept, expert, pieces, units, waits=()):
     _, tiles, tile, model_width = kept[0].shape
     wide_units = kept[2].shape[3]
     block = lambda a: pl.BlockSpec((1, 1) + a.shape[2:], lambda i: (expert, i, 0, 0))
     shape = (pieces, 3, units // pieces, model_width)
     return pl.pallas_call(
-        weight_kernel,
+        held(weight_kernel, 1 + len(kept), len(waits)),
         grid=(tiles,),
-        in_specs=[pl.BlockSpec(memory_space=pltpu.SMEM)] + [block(a) for a in kept],
+        in_specs=[pl.BlockSpec(memory_space=pltpu.SMEM)]
+        + [block(a) for a in kept]
+        + anywhere(waits),
         out_specs=pl.BlockSpec(shape, lambda i: (0, 0, 0, 0)),
         out_shape=jax.ShapeDtypeStruct(shape, jnp.bfloat16),
         scratch_shapes=[pltpu.VMEM((3, wide_units, model_width), jnp.float32)],
         cost_estimate=cost(20e9, 20e6),
         compiler_params=compiler_params(),
         name="weight_grads",
-    )(window, *kept)
+    )(window, *kept, *waits)
 
 
 def send(values, axis, pairs):
@@ -1150,9 +1510,11 @@
         (target_rows[low:high], target_columns[low:high]) for low, high in group_at
     ]
 
-    def pick_group(at, blocks):
+    def pick_group(at, blocks, waits=()):
         low, high = group_at[at]
-        mine = pick_rows(base, target_groups[at][0], blocks[low:high], exp_dev, capacity)
+        mine = pick_rows(
+            base, target_groups[at][0], blocks[low:high], exp_dev, capacity, waits
+        )
         return mine, send(mine, "dp", over_core)
 
     low_out = [cotangent[:, s] for s in each]
@@ -1179,11 +1541,17 @@
         fulls.append(full)
         totals.append(total)
         returned.append(deliver(low))
-    grad_blocks = after(grad_blocks, fulls)
     grad_groups = [pick_group(at, grad_blocks) for at in range(len(group_at))]
     attended, hidden, normed_second = [], [], []
     for s in each:
-        got = project_rows(metas[s], low_in[s], gain_second, w_attn, returned[s])
+        got = project_rows(
+            metas[s],
+            low_in[s],
+            gain_second,
+            w_attn,
+            returned[s],
+            [group[0] for group in grad_groups],
+        )
         attended.append(got[0])
         hidden.append(got[1])
         normed_second.append(got[2])
@@ -1191,137 +1559,132 @@
     first = (my_ep * exp_dev).astype(jnp.int32).reshape(1)
     row_blocks = plane_gather(normed_second)
 
-    def experts_of(at, picked, kept):
-        low, high = group_at[at]
-        results, kept = run_experts(
+    def experts_of(at, picked, kept, chosen):
+        given = [(*picked[i], *grad_groups[at + i]) for i in range(len(picked))]
+        return run_experts(
             first,
             window,
-            *picked,
-            *grad_groups[at],
+            given,
             router_wide,
             (w_gate, w_up, w_down),
             kept,
-            low,
+            group_at[at][0],
             sources,
             experts,
             units,
-        )
-        return results[:2], results[2:], kept
-
-    def placed(at, pair):
-        return place_rows(base, target_groups[at][1], *pair, slots)
-
-    def over_cores(pair):
-        return pair[0], send(pair[1], "dp", over_core)
-
+            chosen,
+        )
+
+    def over_cores(mine, theirs):
+        return mine, send(theirs, "dp", over_core)
+
+    def expert_pairs(mine, theirs):
+        mine, theirs = over_cores(mine, theirs)
+        return [(mine[e], theirs[e]) for e in range(mine.shape[0])]
+
+    own_columns = target_columns[: group_at[0][1]]
+    rest_columns = target_columns[group_at[0][1] :]
     picked_own = pick_group(0, row_blocks)
-    back_own, out_own, kept = experts_of(0, picked_own, ())
-    row_blocks = after(row_blocks, kept)
-    picked_near = pick_group(1, row_blocks)
-    picked_far = pick_group(2, row_blocks)
-    place_own = placed(0, over_cores(back_own))
-    picked_near = after(picked_near, picked_far[0], place_own)
-    back_near, out_near, kept = experts_of(1, picked_near, kept)
-    back_far, out_far, kept = experts_of(2, picked_far, kept)
-    pair_near = over_cores(back_near)
-    pair_far = over_cores(back_far)
-    place_near = placed(1, after(pair_near, kept))
-    weight_part = weight_grads(window, after(kept, place_near), 0, n_cp, units)
-    place_far = placed(2, after(pair_far, weight_part))
-    weight_sums = []
+    own, kept = experts_of(0, [picked_own], (), (0, exp_dev))
+    picked_rest = [pick_group(1, row_blocks, kept[:1]), pick_group(2, row_blocks, kept[:1])]
+    place_own = place_rows(
+        base, own_columns, expert_pairs(own[0], own[1]), slots, [part[0] for part in picked_rest]
+    )
+    back_pairs, out_pairs, weight_sums = [], [], []
+    weight_part = None
     for e in range(exp_dev):
-        if e:
-            weight_part = weight_grads(window, after(kept, place_far, weight_part), e, n_cp, units)
-        part = after(weight_part, weight_sums)
-        weight_sums.append(lax.psum_scatter(part, "cp", scatter_dimension=0, tiled=False))
-
-    def plane_sum(own, near, far, hold=None):
-        (over, up), across = (near[:2], near[2:]), far
+        rest, kept = experts_of(1, picked_rest, kept, (e, e + 1))
+        back_pairs += expert_pairs(rest[0], rest[1])
+        out_pairs += expert_pairs(rest[2], rest[3])
+        if e + 1 < exp_dev:
+            weight_part = weight_grads(window, kept, e, n_cp, units)
+            weight_sums.append(
+                lax.psum_scatter(weight_part, "cp", scatter_dimension=0, tiled=False)
+            )
+            kept = after(kept, weight_part)
+    place_rest = place_rows(base, rest_columns, back_pairs, slots)
+    weight_part = weight_grads(window, kept, exp_dev - 1, n_cp, units, place_rest[:1])
+    weight_sums.append(lax.psum_scatter(weight_part, "cp", scatter_dimension=0, tiled=False))
+    out_own = place_rows(
+        base, own_columns, expert_pairs(own[2], own[3]), slots, [weight_part]
+    )
+    out_rest = place_rows(base, rest_columns, out_pairs, slots, [weight_part])
+
+    def plane_sum(own, rest):
+        over, up, across = (rest[i * slots : (i + 1) * slots] for i in range(3))
         got_first = send(over[0], "dp", over_x)
         got_second = send(up[1], "ep", over_y)
         far_first = send(across[0], "dp", over_x).astype(f32)
         far_second = send(across[1], "ep", over_y).astype(f32)
-        if hold is not None:
-            far_first, far_second = after((far_first, far_second), hold)
         next_first = (up[0].astype(f32) + far_first).astype(bf16)
         next_second = (over[1].astype(f32) + far_second).astype(bf16)
         last_first = send(next_first, "ep", over_y)
         last_second = send(next_second, "dp", over_x)
         return [(own[0], got_first, last_first), (own[1], got_second, last_second)]
 
-    back_rows = plane_sum(place_own, place_near, place_far, weight_part)
-    hidden_grads, proj_grads, leaving, router_parts, gain_parts = [], [], [], [], []
-    for s in each:
-        got = hidden_back(
-            metas[s],
-            *back_rows[s],
-            low_out[s],
-            hidden[s],
-            normed_second[s],
-            gain_second,
-            router_wide,
-            w_attn,
-            experts,
-            n_cp,
-        )
-        hidden_grads.append(got[0])
-        proj_grads.append(got[1])
-        router_parts.append(got[2])
-        gain_parts.append(got[3])
-        leaving.append(deliver(got[4:]))
-    router_grad = sum(router_parts)[:, :experts]
-    gain_second_grad = sum(gain_parts)[0]
-    out_grad = sum(dot_tn(attended[s], proj_grads[s]) for s in each)
-
-    out_grad = out_grad.astype(bf16).reshape(model_width, n_ep, n_cp, 128).transpose(2, 1, 0, 3)
-    out_grad = after(out_grad, weight_sums)
-    out_grad = lax.psum_scatter(out_grad, "cp", scatter_dimension=0, tiled=False)
-    arriving = []
-    line_grads, qkv_grad = 0.0, 0.0
-    for s in each:
-        grads = jnp.stack(leaving[s])
-        ringed, line = attend_backward(
-            metas[s], s, qkvs, bias, grads, fulls[s], totals[s], scale, head_size
-        )
-        line_grads = line_grads + line[:, 0]
-        qkv_grad = qkv_grad + dot_tn(
-            normed_all[s].reshape(seq_len, model_width), ringed.reshape(seq_len, own_width)
-        )
-        arriving.append(deliver(ringed))
-
-    gain_first_grad = jnp.sum(qkv_grad * w_own.astype(f32), axis=1) / norm1_gain
-    attn_term = qkv_grad.reshape(model_width, groups, 3, 128).transpose(2, 1, 0, 3)
-    attn_term = jnp.concatenate(
-        [attn_term.reshape(3 * groups, model_width, 128).astype(bf16), out_grad], axis=0
-    )
-    attn_sum = lax.psum_scatter(attn_term, ("dp", "ep"), scatter_dimension=0, tiled=False)
-    distance_grads = line_grads[:, :seq_len][:, ::-1]
+    back_rows = plane_sum(place_own, place_rest)
+    got, (ringed, line_first, grads_rest) = hidden_back(
+        lengths,
+        back_rows,
+        low_out,
+        hidden,
+        normed_second,
+        gain_second,
+        router_wide,
+        w_attn,
+        experts,
+        qkvs,
+        bias,
+        fulls[0],
+        totals[0],
+        scale,
+        head_size,
+        [out_own[0], out_rest[0]],
+    )
+    hidden_grads, proj_grads, router_parts, gain_parts = zip(*got)
+    router_grad = sum(router_parts)[:, :experts].T
+    ring_second, line_second, arrived, weight_first, out_grad = second_back(
+        lengths,
+        ringed,
+        normed_all,
+        qkvs,
+        bias,
+        grads_rest,
+        fulls[1],
+        totals[1],
+        attended,
+        proj_grads,
+        scale,
+        head_size,
+        weight_sums[:1],
+    )
+    distance_grads = (line_first + line_second)[:, 0, :seq_len][:, ::-1]
     table_grad = jnp.dot(distance_grads, bucket_hot, precision=exact)
     table_grad = jnp.einsum("hg,hb->gb", head_hot, table_grad, precision=exact)
-    small = [router_grad.T, table_grad, gain_first_grad, gain_second_grad]
-    total = jnp.concatenate([part.reshape(-1, 128) for part in small], axis=0)
-    for axis, pairs in (("dp", over_core), ("dp", over_x), ("ep", over_y)):
-        total = total + send(total, axis, pairs)
-    step = 1
-    while step < n_cp:
-        total = total + send(total, "cp", [(i, i ^ step) for i in range(n_cp)])
-        step *= 2
-    total = total.reshape(-1)
-    cuts = [0]
-    for part in small:
-        cuts.append(cuts[-1] + part.size)
-    router_sum, table_sum, gain_first_sum, gain_second_sum = (
-        total[cuts[i] : cuts[i + 1]].reshape(part.shape) for i, part in enumerate(small)
-    )
-
-    out_pairs = after([out_own, out_near, out_far], hidden_grads)
-    out_rows = plane_sum(*(placed(at, over_cores(pair)) for at, pair in enumerate(out_pairs)))
+    table_row = jnp.pad(table_grad.reshape(1, -1), ((0, 0), (0, model_width - table_grad.size)))
+    small = jnp.concatenate(
+        [router_grad, sum(gain_parts), table_row, jnp.zeros((2, model_width), f32)], axis=0
+    )
+    *tokens_grad, small_sum, attn_sum = final_back(
+        ring_second,
+        normed_all,
+        weight_first,
+        w_own,
+        arrived,
+        out_grad,
+        small,
+        gain_first,
+        w_attn,
+        low_in,
+        hidden_grads,
+    )
+    router_sum, gain_second_sum = small_sum[:experts], small_sum[experts]
+    table_sum = small_sum[experts + 1, : table_grad.size].reshape(table_grad.shape)
+    gain_first_sum = small_sum[experts + 2]
+
+    out_rows = plane_sum(out_own, out_rest)
     mixed = [
         (hidden[s] + sum(part.astype(f32) for part in out_rows[s])).astype(bf16) for s in each
-    ]
-    tokens_grad = [
-        token_grads(metas[s], low_in[s], hidden_grads[s], gain_first, w_attn, arriving[s])
-        for s in each
     ]
     weight_sum = jnp.stack(weight_sums)
     gate_sum, up_sum, down_sum = (
@@ -1330,7 +1693,7 @@
     return (
         jnp.stack(mixed, axis=1),
         jnp.stack(tokens_grad, axis=1),
-        attn_sum.astype(f32),
+        attn_sum,
         table_sum,
         gain_first_sum,
         gain_second_sum,

time: 715 us -> 636 us (0.89)
  the two profiles are of different devices: /device:TPU:18 before, /device:TPU:0 now
where the time goes in v3:
time: 636 us; the launch traced here: 632 us
  Pallas kernels  427 us (67%)
  waiting for transfers between devices  87.6 us (14%)
  local copies, waits for them, and re-layouts  47.8 us (8%)
  starting transfers between devices  41.1 us (6%)
  between operations  15.1 us (2%)
  other arithmetic  12.5 us (2%)
    ppermute x48, waiting for transfers between devices, send(): return lax.ppermute(values, axis, pairs)  87.5 us
    pallas_call x3, Pallas kernels, run_experts(): pl.pallas_call(functools.partial(expert_kernel, experts, units, len(kept)...  82.1 us
    pallas_call x1, Pallas kernels, gather_project(): pl.pallas_call(gather_kernel, in_specs=[whole] * 3, out_specs=[whole] * 3...  77.9 us
    pallas_call x1, Pallas kernels, hidden_back(): pl.pallas_call(held(functools.partial(hidden_kernel, experts, scale, head...  53.4 us
    pallas_call x1, Pallas kernels, second_back(): pl.pallas_call(held(functools.partial(second_kernel, scale, head_size, sl...  48.4 us
    pallas_call x1, Pallas kernels, final_back(): pl.pallas_call(functools.partial(final_kernel, slots), grid=(1,), in_spec...  47.9 us
    pallas_call x2, Pallas kernels, weight_grads(): pl.pallas_call(held(weight_kernel, 1 + len(kept), len(waits)), grid=(tile...  42.7 us
    ppermute x48, starting transfers between devices, send(): return lax.ppermute(values, axis, pairs)  41 us
  transfers between devices with their start and end apart: 50, of which 15 were waited for; matrix products, arithmetic and copies ran while one was open for 8% of the time, Pallas kernels for 60%

profile of v3, /device:TPU:0, one launch (start us, length us, event | category | flops | bytes accessed | tf_op | source)
XLA Modules:
  0.0 632.2 jit_solution(4455239579002179909)
XLA Ops:
  8.0 3.0 collective-permute-start.5
  11.0 1.5 collective-permute-start.3
  12.5 3.3 fusion.15
  20.9 1.7 fusion.16
  29.4 1.5 fusion.2.normed_ref
  30.9 77.9 %gather_project.1 = (bf16[2,4,256,1024]{3,2,1,0:T(8,128)(2,1)}, bf16[2,4,256,768]{3,2,1,0:T(8,128)(2,1)}, f32[4,256,1024]{2,1,0:T(8,128)}) custom-call(bf16[2,256,1024]{2,1,0:T(8,128)(2,1)} %fusion.2.normed_ref, bf16[1024,768]{1,0:T(8,128)(2,1)} %copy-done.15, f32[4,1,1280]{2,1,0:T(1,128)} %broadcast_in_dim.13.line_ref), custom_call_target="tpu_custom_call" | custom-call | flops 3000000000 | bytes 1000000 | tf_op jit(solution)/shard_map/gather_project/pallas_call | solution.py:468
  108.8 1.9 pad_add_fusion.5
  110.7 9.9 %attend_forward.2 = (bf16[4,256,256]{2,1,0:T(8,128)(2,1)}, f32[4,256,256]{2,1,0:T(8,128)}, f32[4,256,256]{2,1,0:T(8,128)}) custom-call(s32[2]{0:T(128)} %get-tuple-element.241.meta_ref.refs_0_, bf16[2,4,256,768]{3,2,1,0:T(8,128)(2,1)} %get-tuple-element.100.q_ref.k_ref.v_ref.refs_4_.refs_3_, ...), custom_call_target="tpu_custom_call" | custom-call | flops 400000000 | bytes 400000 | tf_op jit(solution)/shard_map/attend_forward/pallas_call | solution.py:550
  120.6 1.8 slice_bitcast_fusion.15
  122.3 1.6 collective-permute-start.2
  123.9 1.5 collective-permute-start.6
  125.5 1.5 collective-permute-start.4
  126.9 9.7 %attend_forward.3 = (bf16[4,256,256]{2,1,0:T(8,128)(2,1)}, f32[4,256,256]{2,1,0:T(8,128)}, f32[4,256,256]{2,1,0:T(8,128)}) custom-call(s32[2]{0:T(128)} %get-tuple-element.242.meta_ref.refs_0_, bf16[2,4,256,768]{3,2,1,0:T(8,128)(2,1)} %get-tuple-element.100.q_ref.k_ref.v_ref.refs_4_.refs_3_, ...), custom_call_target="tpu_custom_call" | custom-call | flops 400000000 | bytes 400000 | tf_op jit(solution)/shard_map/attend_forward/pallas_call | solution.py:550
  138.6 3.1 pick_rows.6.refs_8_.refs_2_
  141.7 1.5 collective-permute-start.9
  143.2 1.5 collective-permute-start.8
  147.2 4.3 collective-permute-done.1.refs_6_
  152.7 4.1 collective-permute-done.9.refs_4_
  156.8 2.3 collective-permute-start
  159.1 4.4 collective-permute-done.13.refs_2_
  164.7 2.3 collective-permute-start.15
  167.8 4.5 pick_rows.7.refs_9_.refs_2_
  172.4 3.1 pick_rows.8.refs_10_.refs_6_
  176.2 3.9 project_rows.2
  180.8 3.9 project_rows.3
  184.7 3.3 pick_rows.9.refs_0_
  188.7 1.5 collective-permute-start.21
  192.9 1.7 concatenate.31.refs_4_.refs_8_.refs_2_
  195.3 22.6 %expert_rows.3 = (bf16[2,1,320,1152]{3,2,1,0:T(8,128)(2,1)}, bf16[2,1,320,1152]{3,2,1,0:T(8,128)(2,1)}, bf16[2,1,320,1024]{3,2,1,0:T(8,128)(2,1)}, bf16[2,1,320,...) custom-call(s32[1]{0:T(128)} %bitcast.23.first_ref, ...), custom_call_target="tpu_custom_call" | custom-call | flops 1000000000 | bytes 400000 | tf_op jit(solution)/shard_map/expert_rows/pallas_call | solution.py:1348
  217.9 4.7 pick_rows.10.refs_0_.refs_6_
  223.8 1.6 collective-permute-start.28
  225.3 11.8 %collective-permute-done.27.refs_2_ = bf16[256,1024]{1,0:T(8,128)(2,1)S(1)} collective-permute-done((bf16[256,1024]{1,0:T(8,128)(2,1)}, bf16[256,1024]{1,0:T(8,128)(2,1)S(1)}, u32[]{:S(2)}, u32[]{:S(2)}) %collective-permute-start.27) | collective-permute-done | bytes 524320 | tf_op jit(solution)/shard_map/ppermute | solution.py:1418
  237.9 3.1 pick_rows.11.refs_4_.refs_7_
  241.1 3.4 collective-permute-done.29.refs_5_
  244.5 29.3 %expert_rows.4 = (bf16[1,3,320,1152]{3,2,1,0:T(8,128)(2,1)}, bf16[1,3,320,1152]{3,2,1,0:T(8,128)(2,1)}, bf16[1,3,320,1024]{3,2,1,0:T(8,128)(2,1)}, bf16[1,3,320,...) custom-call(s32[1]{0:T(128)} %bitcast.23.first_ref, ...), custom_call_target="tpu_custom_call", output_to_operand_aliasing={{4}: (14, {}), {5}: (15, {}), {6}: (16, {}), {7}: (17, {}),... | custom-call | flops 3000000000 | bytes 1200000 | tf_op jit(solution)/shard_map/expert_rows/pallas_call | solution.py:1348
  273.8 21.2 %weight_grads.2 = bf16[4,3,176,1024]{3,2,1,0:T(8,128)(2,1)} custom-call(s32[2]{0:T(128)} %pad_add_fusion.6.window_ref.refs_0_, bf16[2,4,640,1024]{3,2,1,0:T(8,128)(2,1)} %get-tuple-element.115.refs_1_.refs_12_, bf16[2,4,640,1024]{3,2,1,0:T(8,128)(2,1)} %get-tuple-element.116.refs_2_.refs_13_, bf16[2,4,640,768]{3,2,1,0:T(8,128)(2,1)} %get-tuple-element.117.refs_3_.refs_14_, ...), custom_call_target="tpu_custom_call" | custom-call | flops 1000000000 | bytes 1000000 | tf_op jit(solution)/shard_map/weight_grads/pallas_call | solution.py:1402
  295.2 30.2 %expert_rows.5 = (bf16[1,3,320,1152]{3,2,1,0:T(8,128)(2,1)}, bf16[1,3,320,1152]{3,2,1,0:T(8,128)(2,1)}, bf16[1,3,320,1024]{3,2,1,0:T(8,128)(2,1)}, bf16[1,3,320,...) custom-call(s32[1]{0:T(128)S(6)} %add.161.first_ref, ...), custom_call_target="tpu_custom_call", output_to_operand_aliasing={{4}: (14, {}), {5}: (15, {}), {6}: (16, {}), {7}: (17, {}),... | custom-call | flops 3000000000 | bytes 1200000 | tf_op jit(solution)/shard_map/expert_rows/pallas_call | solution.py:1348
  326.9 3.1 collective-permute-done.32
  330.1 1.4 copy-done.14
  331.4 8.9 %place_rows.4 = (bf16[256,1152]{1,0:T(8,128)(2,1)}, bf16[256,1152]{1,0:T(8,128)(2,1)}, bf16[256,1152]{1,0:T(8,128)(2,1)}, bf16[256,1152]{1,0:T(8,128)(2,1)}, bf1...) custom-call(s32[1]{0:T(128)} %bitcast.9.refs_0_, s32[3,512,2]{2,1,0:T(8,128)} %slice.147.refs_1_, ...), custom_call_target="tpu_custom_call" | custom-call | flops 240000000 | bytes 600000 | tf_op jit(solution)/shard_map/place_rows/pallas_call | solution.py:1242
  340.3 21.5 %weight_grads.3.refs_6_ = bf16[4,3,176,1024]{3,2,1,0:T(8,128)(2,1)} custom-call(s32[2]{0:T(128)} %pad_add_fusion.6.window_ref.refs_0_, bf16[2,4,640,1024]{3,2,1,0:T(8,128)(2,1)} %get-tuple-element.120.refs_1_, bf16[2,4,640,1024]{3,2,1,0:T(8,128)(2,1)} %get-tuple-element.121.refs_2_, bf16[2,4,640,768]{3,2,1,0:T(8,128)(2,1)} %get-tuple-element.122.refs_3_, ...), custom_call_target="tpu_custom_call" | custom-call | flops 1000000000 | bytes 1000000 | tf_op jit(solution)/shard_map/weight_grads/pallas_call | solution.py:1402
  363.7 2.5 slice_bitcast_fusion.9
  367.4 3.4 collective-permute-done.20
  372.0 1.3 copy-done.17
  374.0 8.0 %place_rows.6 = (bf16[256,1024]{1,0:T(8,128)(2,1)}, bf16[256,1024]{1,0:T(8,128)(2,1)}, bf16[256,1024]{1,0:T(8,128)(2,1)}, bf16[256,1024]{1,0:T(8,128)(2,1)}, bf1...) custom-call(s32[1]{0:T(128)} %bitcast.9.refs_0_, s32[3,512,2]{2,1,0:T(8,128)} %slice.147.refs_1_, ...), custom_call_target="tpu_custom_call" | custom-call | flops 240000000 | bytes 600000 | tf_op jit(solution)/shard_map/place_rows/pallas_call | solution.py:1242
  381.9 1.5 collective-permute-start.36
  385.9 4.3 place_rows.7
  390.3 1.5 collective-permute-start.42
  393.0 4.0 place_rows.5
  397.0 1.3 collective-permute-start.35
  399.7 9.9 %collective-permute-done.43 = bf16[256,1152]{1,0:T(8,128)(2,1)S(1)} collective-permute-done((bf16[256,1152]{1,0:T(8,128)(2,1)}, bf16[256,1152]{1,0:T(8,128)(2,1)S(1)}, u32[]{:S(2)}, u32[]{:S(2)}) %collective-permute-start.43) | collective-permute-done | bytes 589856 | tf_op jit(solution)/shard_map/ppermute | solution.py:1418
  410.4 11.8 %collective-permute-done.46 = bf16[256,1152]{1,0:T(8,128)(2,1)S(1)} collective-permute-done((bf16[256,1152]{1,0:T(8,128)(2,1)S(1)}, bf16[256,1152]{1,0:T(8,128)(2,1)S(1)}, u32[]{:S(2)}, u32[]{:S(2)}) %collective-permute-start.46) | collective-permute-done | bytes 589856 | tf_op jit(solution)/shard_map/ppermute | solution.py:1418
  423.8 9.6 %collective-permute-done.35 = bf16[256,1024]{1,0:T(8,128)(2,1)S(1)} collective-permute-done((bf16[256,1024]{1,0:T(8,128)(2,1)S(1)}, bf16[256,1024]{1,0:T(8,128)(2,1)S(1)}, u32[]{:S(2)}, u32[]{:S(2)}) %collective-permute-start.35) | collective-permute-done | bytes 524320 | tf_op jit(solution)/shard_map/ppermute | solution.py:1418
  434.1 9.9 %collective-permute-done.40 = bf16[256,1024]{1,0:T(8,128)(2,1)S(1)} collective-permute-done((bf16[256,1024]{1,0:T(8,128)(2,1)S(1)}, bf16[256,1024]{1,0:T(8,128)(2,1)S(1)}, u32[]{:S(2)}, u32[]{:S(2)}) %collective-permute-start.40) | collective-permute-done | bytes 524320 | tf_op jit(solution)/shard_map/ppermute | solution.py:1418
  444.0 1.5 collective-permute-start.47
  446.4 2.0 copy.85
  448.4 9.4 %collective-permute-done.44.refs_10_ = bf16[256,1152]{1,0:T(8,128)(2,1)S(1)} collective-permute-done((bf16[256,1152]{1,0:T(8,128)(2,1)S(1)}, bf16[256,1152]{1,0:T(8,128)(2,1)S(1)}, u32[]{:S(2)}, u32[]{:S(2)}) %collective-permute-start.44) | collective-permute-done | bytes 589856 | tf_op jit(solution)/shard_map/ppermute | solution.py:1418
  459.8 53.4 %hidden_back.1 = (f32[256,1024]{1,0:T(8,128)}, bf16[256,1024]{1,0:T(8,128)(2,1)}, f32[1024,128]{1,0:T(8,128)}, f32[1,1024]{1,0:T(1,128)}, f32[256,1024]{1,0:T(8,...) custom-call(s32[2]{0:T(128)} %refs_0_.3, ...), custom_call_target="tpu_custom_call" | custom-call | flops 1000000000 | bytes 1000000 | tf_op jit(solution)/shard_map/hidden_back/pallas_call | solution.py:818
  515.8 48.4 %second_back.1 = (bf16[4,256,768]{2,1,0:T(8,128)(2,1)}, f32[4,1,1280]{2,1,0:T(1,128)}, bf16[4,256,768]{2,1,0:T(8,128)(2,1)}, f32[1024,768]{1,0:T(8,128)}, f32[128,256]{1,0:T(8,128)}) custom-call(s32[2]{0:T(128)} %refs_0_.3, bf16[4,256,768]{2,1,0:T(8,128)(2,1)} %get-tuple-element.153.refs_1_, bf16[2,4,256,1024]{3,2,1,0:T(8,128)(2,1)} %get-tuple-element.154.refs_2_.normed_ref, ...), custom_call_target="tpu_custom_call" | custom-call | flops 1000000000 | bytes 1000000 | tf_op jit(solution)/shard_map/second_back/pallas_call | solution.py:972
  567.4 47.9 %final_back.1 = (bf16[256,1024]{1,0:T(8,128)(2,1)}, bf16[256,1024]{1,0:T(8,128)(2,1)}, f32[8,1024]{1,0:T(8,128)}, f32[1024,128]{1,0:T(8,128)}) custom-call(bf16[4,256,768]{2,1,0:T(8,128)(2,1)} %get-tuple-element.162.ring_ref, bf16[2,4,256,1024]{3,2,1,0:T(8,128)(2,1)} %get-tuple-element.154.refs_2_.normed_ref, f32[1024,768]{1,0:T(8,128)} %get-tuple-element.163.former_ref, ...), custom_call_target="tpu_custom_call" | custom-call | flops 1000000000 | bytes 1000000 | tf_op jit(solution)/shard_map/final_back/pallas_call | solution.py:1130
  615.3 1.4 pad_maximum_fusion.2
  616.7 2.0 copy.86
  620.8 1.3 constant_dynamic-update-slice_fusion
  622.1 2.2 convert_bitcast_fusion
  (257 shorter events, 53.6 us)
Async XLA Ops:
  7.2 508.6 %reduce-scatter.3.cloned.1.call-start = ((), (), s32[]{:S(2)}) async-start(), calls=%async_computation.2 | async-start | bytes 5406720 | tf_op jit(solution)/shard_map/reduce_scatter | solution.py:1602
  8.0 116.0 %collective-permute-start.5 = (s32[2,256]{1,0:T(2,128)S(1)}, s32[2,256]{1,0:T(2,128)S(1)}, u32[]{:S(2)}, u32[]{:S(2)}) collective-permute-start(s32[2,256]{1,0:T(2,128)S(1)} %get-tuple-element.237), channel_id=1, source_target_pairs={{0,4},{4,0},{1,5},{5,1},{2,6},{6,2},{3,7},{7,3},{8,12},{12,8},{9,1... | collective-permute-start | bytes 6152 | tf_op jit(solution)/shard_map/ppermute | solution.py:1418
  11.0 114.5 %collective-permute-start.3 = (s32[2,256]{1,0:T(2,128)S(1)}, s32[2,256]{1,0:T(2,128)S(1)}, u32[]{:S(2)}, u32[]{:S(2)}) collective-permute-start(s32[2,256]{1,0:T(2,128)S(1)} %get-tuple-element.237), channel_id=1, source_target_pairs={{0,16},{8,24},{16,0},{24,8},{1,17},{9,25},{17,1},{25,9},{2,18},{10... | collective-permute-start | bytes 6152 | tf_op jit(solution)/shard_map/ppermute | solution.py:1418
  16.7 128.6 %collective-permute-start.7 = (bf16[256,1024]{1,0:T(8,128)(2,1)}, bf16[256,1024]{1,0:T(8,128)(2,1)S(1)}, u32[]{:S(2)}, u32[]{:S(2)}) collective-permute-start(bf16[256,1024]{1,0:T(8,128)(2,1)} %bitcast.115.refs_2_.refs_11_), channel_id=1, source_target_pairs={{0,16},{8,24},{16,0},{24,8},{1,17},{9,25},{17,1},{25,9},{2,18},{10... | collective-permute-start | bytes 1572872 | tf_op jit(solution)/shard_map/ppermute | solution.py:1418
  18.3 127.5 %collective-permute-start.10 = (bf16[256,1024]{1,0:T(8,128)(2,1)}, bf16[256,1024]{1,0:T(8,128)(2,1)}, u32[]{:S(2)}, u32[]{:S(2)}) collective-permute-start(bf16[256,1024]{1,0:T(8,128)(2,1)} %bitcast.114.refs_3_.refs_17_), channel_id=1, source_target_pairs={{0,4},{4,0},{1,5},{5,1},{2,6},{6,2},{3,7},{7,3},{8,12},{12,8},{9,1... | collective-permute-start | bytes 1572872 | tf_op jit(solution)/shard_map/ppermute | solution.py:1418
  122.3 22.4 %collective-permute-start.2 = (bf16[256,256]{1,0:T(8,128)(2,1)S(1)}, bf16[256,256]{1,0:T(8,128)(2,1)S(1)}, u32[]{:S(2)}, u32[]{:S(2)}) collective-permute-start(bf16[256,256]{1,0:T(8,128)(2,1)S(1)} %get-tuple-element.227), channel_id=1, source_target_pairs={{0,1},{1,2},{2,3},{3,0},{4,5},{5,6},{6,7},{7,4},{8,9},{9,10},{10,1... | collective-permute-start | bytes 393224 | tf_op jit(solution)/shard_map/ppermute | solution.py:1418
  123.9 13.6 %collective-permute-start.6 = (s32[2,256]{1,0:T(2,128)S(1)}, s32[2,256]{1,0:T(2,128)S(1)}, u32[]{:S(2)}, u32[]{:S(2)}) collective-permute-start(s32[2,256]{1,0:T(2,128)S(1)} %get-tuple-element.238), channel_id=1, source_target_pairs={{0,4},{4,0},{1,5},{5,1},{2,6},{6,2},{3,7},{7,3},{8,12},{12,8},{9,1... | collective-permute-start | bytes 6152 | tf_op jit(solution)/shard_map/ppermute | solution.py:1418
  125.5 12.6 %collective-permute-start.4 = (s32[2,256]{1,0:T(2,128)S(1)}, s32[2,256]{1,0:T(2,128)S(1)}, u32[]{:S(2)}, u32[]{:S(2)}) collective-permute-start(s32[2,256]{1,0:T(2,128)S(1)} %get-tuple-element.238), channel_id=1, source_target_pairs={{0,16},{8,24},{16,0},{24,8},{1,17},{9,25},{17,1},{25,9},{2,18},{10... | collective-permute-start | bytes 6152 | tf_op jit(solution)/shard_map/ppermute | solution.py:1418
  137.5 4.2 collective-permute-start.11
  138.0 5.2 collective-permute-start.12
  141.7 15.1 %collective-permute-start.9 = (bf16[256,1024]{1,0:T(8,128)(2,1)}, bf16[256,1024]{1,0:T(8,128)(2,1)S(1)}, u32[]{:S(2)}, u32[]{:S(2)}) collective-permute-start(bf16[256,1024]{1,0:T(8,128)(2,1)} %bitcast.115.refs_2_.refs_11_), channel_id=1, source_target_pairs={{0,4},{4,0},{1,5},{5,1},{2,6},{6,2},{3,7},{7,3},{8,12},{12,8},{9,1... | collective-permute-start | bytes 1572872 | tf_op jit(solution)/shard_map/ppermute | solution.py:1418
  143.2 15.8 %collective-permute-start.8 = (bf16[256,1024]{1,0:T(8,128)(2,1)}, bf16[256,1024]{1,0:T(8,128)(2,1)S(1)}, u32[]{:S(2)}, u32[]{:S(2)}) collective-permute-start(bf16[256,1024]{1,0:T(8,128)(2,1)} %bitcast.114.refs_3_.refs_17_), channel_id=1, source_target_pairs={{0,16},{8,24},{16,0},{24,8},{1,17},{9,25},{17,1},{25,9},{2,18},{10... | collective-permute-start | bytes 1572872 | tf_op jit(solution)/shard_map/ppermute | solution.py:1418
  144.7 27.7 %copy-start.37 = (bf16[256,256]{1,0:T(8,128)(2,1)}, bf16[256,256]{1,0:T(8,128)(2,1)S(1)}, u32[]{:S(2)}) copy-start(bf16[256,256]{1,0:T(8,128)(2,1)S(1)} %collective-permute-done.2.refs_7_) | copy-start | bytes 393220
  144.7 6.8 %collective-permute-start.1 = (bf16[256,256]{1,0:T(8,128)(2,1)S(1)}, bf16[256,256]{1,0:T(8,128)(2,1)S(1)}, u32[]{:S(2)}, u32[]{:S(2)}) collective-permute-start(bf16[256,256]{1,0:T(8,128)(2,1)S(1)} %get-tuple-element.228), channel_id=1, source_target_pairs={{0,2},{1,3},{2,0},{3,1},{4,6},{5,7},{6,4},{7,5},{8,10},{9,11},{10,... | collective-permute-start | bytes 393224 | tf_op jit(solution)/shard_map/ppermute | solution.py:1418
  145.3 22.5 %copy-start.27 = (bf16[256,1024]{1,0:T(8,128)(2,1)}, bf16[256,1024]{1,0:T(8,128)(2,1)S(1)}, u32[]{:S(2)}) copy-start(bf16[256,1024]{1,0:T(8,128)(2,1)S(1)} %collective-permute-done.7.refs_2_) | copy-start | bytes 1572868
  145.3 18.2 %collective-permute-start.13 = (bf16[256,1024]{1,0:T(8,128)(2,1)S(1)}, bf16[256,1024]{1,0:T(8,128)(2,1)}, u32[]{:S(2)}, u32[]{:S(2)}) collective-permute-start(bf16[256,1024]{1,0:T(8,128)(2,1)S(1)} %collective-permute-done.7.refs_2_), channel_id=1, source_target_pairs={{0,4},{4,0},{1,5},{5,1},{2,6},{6,2},{3,7},{7,3},{8,12},{12,8},{9,1... | collective-permute-start | bytes 1572872 | tf_op jit(solution)/shard_map/ppermute | solution.py:1418
  145.8 18.9 %collective-permute-start.14 = (bf16[256,1024]{1,0:T(8,128)(2,1)}, bf16[256,1024]{1,0:T(8,128)(2,1)}, u32[]{:S(2)}, u32[]{:S(2)}) collective-permute-start(bf16[256,1024]{1,0:T(8,128)(2,1)} %collective-permute-done.10.refs_5_), channel_id=1, source_target_pairs={{0,16},{8,24},{16,0},{24,8},{1,17},{9,25},{17,1},{25,9},{2,18},{10... | collective-permute-start | bytes 1572872 | tf_op jit(solution)/shard_map/ppermute | solution.py:1418
  151.5 20.9 %copy-start.38 = (bf16[256,256]{1,0:T(8,128)(2,1)}, bf16[256,256]{1,0:T(8,128)(2,1)S(1)}, u32[]{:S(2)}) copy-start(bf16[256,256]{1,0:T(8,128)(2,1)S(1)} %collective-permute-done.1.refs_6_) | copy-start | bytes 393220
  151.5 40.0 %collective-permute-start.19 = (bf16[1,2,320,1024]{3,2,1,0:T(8,128)(2,1)}, bf16[1,2,320,1024]{3,2,1,0:T(8,128)(2,1)}, u32[]{:S(2)}, u32[]{:S(2)}) collective-permute-start(bf16[1,2,320,1024]{3,2,1,0:T(8,128)(2,1)} %pick_rows.6.refs_8_.refs_2_), channel_id=1, source_target_pairs={{0,8},{8,0},{16,24},{24,16},{1,9},{9,1},{17,25},{25,17},{2,10},{10... | collective-permute-start | bytes 3932168 | tf_op jit(solution)/shard_map/ppermute | solution.py:1418
  156.8 18.8 %collective-permute-start = (bf16[256,256]{1,0:T(8,128)(2,1)S(1)}, bf16[256,256]{1,0:T(8,128)(2,1)S(1)}, u32[]{:S(2)}, u32[]{:S(2)}) collective-permute-start(bf16[256,256]{1,0:T(8,128)(2,1)S(1)} %get-tuple-element.229), channel_id=1, source_target_pairs={{0,3},{1,0},{2,1},{3,2},{4,7},{5,4},{6,5},{7,6},{8,11},{9,8},{10,9... | collective-permute-start | bytes 393224 | tf_op jit(solution)/shard_map/ppermute | solution.py:1418
  159.0 21.0 %collective-permute-start.17 = (bf16[256,256]{1,0:T(8,128)(2,1)}, bf16[256,256]{1,0:T(8,128)(2,1)S(1)}, u32[]{:S(2)}, u32[]{:S(2)}) collective-permute-start(bf16[256,256]{1,0:T(8,128)(2,1)} %get-tuple-element.231), channel_id=1, source_target_pairs={{0,1},{1,2},{2,3},{3,0},{4,5},{5,6},{6,7},{7,4},{8,9},{9,10},{10,1... | collective-permute-start | bytes 393224 | tf_op jit(solution)/shard_map/ppermute | solution.py:1418
  163.5 16.6 %collective-permute-start.16 = (bf16[256,256]{1,0:T(8,128)(2,1)}, bf16[256,256]{1,0:T(8,128)(2,1)S(1)}, u32[]{:S(2)}, u32[]{:S(2)}) collective-permute-start(bf16[256,256]{1,0:T(8,128)(2,1)} %get-tuple-element.232), channel_id=1, source_target_pairs={{0,2},{1,3},{2,0},{3,1},{4,6},{5,7},{6,4},{7,5},{8,10},{9,11},{10,... | collective-permute-start | bytes 393224 | tf_op jit(solution)/shard_map/ppermute | solution.py:1418
  164.7 15.4 %collective-permute-start.15 = (bf16[256,256]{1,0:T(8,128)(2,1)}, bf16[256,256]{1,0:T(8,128)(2,1)S(1)}, u32[]{:S(2)}, u32[]{:S(2)}) collective-permute-start(bf16[256,256]{1,0:T(8,128)(2,1)} %get-tuple-element.233), channel_id=1, source_target_pairs={{0,3},{1,0},{2,1},{3,2},{4,7},{5,4},{6,5},{7,6},{8,11},{9,8},{10,9... | collective-permute-start | bytes 393224 | tf_op jit(solution)/shard_map/ppermute | solution.py:1418
  188.0 7.3 %collective-permute-start.18 = (bf16[1,2,320,1024]{3,2,1,0:T(8,128)(2,1)}, bf16[1,2,320,1024]{3,2,1,0:T(8,128)(2,1)}, u32[]{:S(2)}, u32[]{:S(2)}) collective-permute-start(bf16[1,2,320,1024]{3,2,1,0:T(8,128)(2,1)} %pick_rows.9.refs_0_), channel_id=1, source_target_pairs={{0,8},{8,0},{16,24},{24,16},{1,9},{9,1},{17,25},{25,17},{2,10},{10... | collective-permute-start | bytes 3932168 | tf_op jit(solution)/shard_map/ppermute | solution.py:1418
  188.0 29.9 %collective-permute-start.23 = (bf16[256,1024]{1,0:T(8,128)(2,1)}, bf16[256,1024]{1,0:T(8,128)(2,1)}, u32[]{:S(2)}, u32[]{:S(2)}) collective-permute-start(bf16[256,1024]{1,0:T(8,128)(2,1)} %get-tuple-element.98.refs_2_.refs_13_), channel_id=1, source_target_pairs={{0,4},{4,0},{1,5},{5,1},{2,6},{6,2},{3,7},{7,3},{8,12},{12,8},{9,1... | collective-permute-start | bytes 1572872 | tf_op jit(solution)/shard_map/ppermute | solution.py:1418
  188.7 29.2 %collective-permute-start.21 = (bf16[256,1024]{1,0:T(8,128)(2,1)}, bf16[256,1024]{1,0:T(8,128)(2,1)}, u32[]{:S(2)}, u32[]{:S(2)}) collective-permute-start(bf16[256,1024]{1,0:T(8,128)(2,1)} %get-tuple-element.98.refs_2_.refs_13_), channel_id=1, source_target_pairs={{0,16},{8,24},{16,0},{24,8},{1,17},{9,25},{17,1},{25,9},{2,18},{10... | collective-permute-start | bytes 1572872 | tf_op jit(solution)/shard_map/ppermute | solution.py:1418
  190.2 27.7 %collective-permute-start.24 = (bf16[256,1024]{1,0:T(8,128)(2,1)}, bf16[256,1024]{1,0:T(8,128)(2,1)}, u32[]{:S(2)}, u32[]{:S(2)}) collective-permute-start(bf16[256,1024]{1,0:T(8,128)(2,1)} %get-tuple-element.102.refs_3_.refs_19_), channel_id=1, source_target_pairs={{0,4},{4,0},{1,5},{5,1},{2,6},{6,2},{3,7},{7,3},{8,12},{12,8},{9,1... | collective-permute-start | bytes 1572872 | tf_op jit(solution)/shard_map/ppermute | solution.py:1418
  191.5 26.4 %collective-permute-start.22 = (bf16[256,1024]{1,0:T(8,128)(2,1)}, bf16[256,1024]{1,0:T(8,128)(2,1)}, u32[]{:S(2)}, u32[]{:S(2)}) collective-permute-start(bf16[256,1024]{1,0:T(8,128)(2,1)} %get-tuple-element.102.refs_3_.refs_19_), channel_id=1, source_target_pairs={{0,16},{8,24},{16,0},{24,8},{1,17},{9,25},{17,1},{25,9},{2,18},{10... | collective-permute-start | bytes 1572872 | tf_op jit(solution)/shard_map/ppermute | solution.py:1418
  195.3 45.8 %collective-permute-start.26 = (bf16[2,2,320,1024]{3,2,1,0:T(8,128)(2,1)S(1)}, bf16[2,2,320,1024]{3,2,1,0:T(8,128)(2,1)S(1)}, u32[]{:S(2)}, u32[]{:S(2)}) collective-permute-start(bf16[2,2,320,1024]{3,2,1,0:T(8,128)(2,1)S(1)} %copy-done.2), channel_id=1, source_target_pairs={{0,8},{8,0},{16,24},{24,16},{1,9},{9,1},{17,25},{25,17},{2,10},{10... | collective-permute-start | bytes 7864328 | tf_op jit(solution)/shard_map/ppermute | solution.py:1418
  222.6 21.9 %collective-permute-start.25 = (bf16[2,2,320,1024]{3,2,1,0:T(8,128)(2,1)}, bf16[2,2,320,1024]{3,2,1,0:T(8,128)(2,1)}, u32[]{:S(2)}, u32[]{:S(2)}) collective-permute-start(bf16[2,2,320,1024]{3,2,1,0:T(8,128)(2,1)} %pick_rows.10.refs_0_.refs_6_), channel_id=1, source_target_pairs={{0,8},{8,0},{16,24},{24,16},{1,9},{9,1},{17,25},{25,17},{2,10},{10... | collective-permute-start | bytes 7864328 | tf_op jit(solution)/shard_map/ppermute | solution.py:1418
  223.0 14.1 %collective-permute-start.27 = (bf16[256,1024]{1,0:T(8,128)(2,1)}, bf16[256,1024]{1,0:T(8,128)(2,1)S(1)}, u32[]{:S(2)}, u32[]{:S(2)}) collective-permute-start(bf16[256,1024]{1,0:T(8,128)(2,1)} %collective-permute-done.21.refs_2_), channel_id=1, source_target_pairs={{0,4},{4,0},{1,5},{5,1},{2,6},{6,2},{3,7},{7,3},{8,12},{12,8},{9,1... | collective-permute-start | bytes 1572872 | tf_op jit(solution)/shard_map/ppermute | solution.py:1418
  223.8 13.9 %collective-permute-start.28 = (bf16[256,1024]{1,0:T(8,128)(2,1)}, bf16[256,1024]{1,0:T(8,128)(2,1)}, u32[]{:S(2)}, u32[]{:S(2)}) collective-permute-start(bf16[256,1024]{1,0:T(8,128)(2,1)} %collective-permute-done.24.refs_5_), channel_id=1, source_target_pairs={{0,16},{8,24},{16,0},{24,8},{1,17},{9,25},{17,1},{25,9},{2,18},{10... | collective-permute-start | bytes 1572872 | tf_op jit(solution)/shard_map/ppermute | solution.py:1418
  225.3 15.7 %collective-permute-start.30 = (bf16[1,2,320,1024]{3,2,1,0:T(8,128)(2,1)S(1)}, bf16[1,2,320,1024]{3,2,1,0:T(8,128)(2,1)}, u32[]{:S(2)}, u32[]{:S(2)}) collective-permute-start(bf16[1,2,320,1024]{3,2,1,0:T(8,128)(2,1)S(1)} %copy-done.3), channel_id=1, source_target_pairs={{0,8},{8,0},{16,24},{24,16},{1,9},{9,1},{17,25},{25,17},{2,10},{10... | collective-permute-start | bytes 3932168 | tf_op jit(solution)/shard_map/ppermute | solution.py:1418
  241.1 3.4 collective-permute-start.29
  295.0 325.8 %reduce-scatter.5.cloned.1.call-start = ((), (), s32[]{:S(2)}) async-start(), calls=%async_computation.3 | async-start | bytes 5406720 | tf_op jit(solution)/shard_map/reduce_scatter | solution.py:1607
  295.0 30.9 %copy-start.12 = (s32[2,512]{0,1:T(8,128)S(1)}, s32[2,512]{0,1:T(8,128)}, u32[]{:S(2)}) copy-start(s32[2,512]{0,1:T(8,128)} %copy-done.11) | copy-start | bytes 12292
  295.0 31.9 %collective-permute-start.31 = (bf16[1,3,320,1152]{3,2,1,0:T(8,128)(2,1)}, bf16[1,3,320,1152]{3,2,1,0:T(8,128)(2,1)S(1)}, u32[]{:S(2)}, u32[]{:S(2)}) collective-permute-start(bf16[1,3,320,1152]{3,2,1,0:T(8,128)(2,1)} %get-tuple-element.126), channel_id=1, source_target_pairs={{0,8},{8,0},{16,24},{24,16},{1,9},{9,1},{17,25},{25,17},{2,10},{10... | collective-permute-start | bytes 6635528 | tf_op jit(solution)/shard_map/ppermute | solution.py:1418
  325.4 4.6 collective-permute-start.32
  361.9 10.1 %collective-permute-start.33 = (bf16[1,3,320,1024]{3,2,1,0:T(8,128)(2,1)}, bf16[1,3,320,1024]{3,2,1,0:T(8,128)(2,1)S(1)}, u32[]{:S(2)}, u32[]{:S(2)}) collective-permute-start(bf16[1,3,320,1024]{3,2,1,0:T(8,128)(2,1)} %get-tuple-element.132), channel_id=1, source_target_pairs={{0,8},{8,0},{16,24},{24,16},{1,9},{9,1},{17,25},{25,17},{2,10},{10... | collective-permute-start | bytes 5898248 | tf_op jit(solution)/shard_map/ppermute | solution.py:1418
  362.3 9.7 %collective-permute-start.34 = (bf16[1,3,320,1024]{3,2,1,0:T(8,128)(2,1)}, bf16[1,3,320,1024]{3,2,1,0:T(8,128)(2,1)S(1)}, u32[]{:S(2)}, u32[]{:S(2)}) collective-permute-start(bf16[1,3,320,1024]{3,2,1,0:T(8,128)(2,1)} %get-tuple-element.134), channel_id=1, source_target_pairs={{0,8},{8,0},{16,24},{24,16},{1,9},{9,1},{17,25},{25,17},{2,10},{10... | collective-permute-start | bytes 5898248 | tf_op jit(solution)/shard_map/ppermute | solution.py:1418
  362.4 8.4 %collective-permute-start.20 = (bf16[2,1,320,1024]{3,2,1,0:T(8,128)(2,1)}, bf16[2,1,320,1024]{3,2,1,0:T(8,128)(2,1)S(1)}, u32[]{:S(2)}, u32[]{:S(2)}) collective-permute-start(bf16[2,1,320,1024]{3,2,1,0:T(8,128)(2,1)} %get-tuple-element.104), channel_id=1, source_target_pairs={{0,8},{8,0},{16,24},{24,16},{1,9},{9,1},{17,25},{25,17},{2,10},{10... | collective-permute-start | bytes 3932168 | tf_op jit(solution)/shard_map/ppermute | solution.py:1418
  362.8 21.9 %collective-permute-start.41 = (bf16[2,1,320,1152]{3,2,1,0:T(8,128)(2,1)}, bf16[2,1,320,1152]{3,2,1,0:T(8,128)(2,1)S(1)}, u32[]{:S(2)}, u32[]{:S(2)}) collective-permute-start(bf16[2,1,320,1152]{3,2,1,0:T(8,128)(2,1)} %get-tuple-element.145), channel_id=1, source_target_pairs={{0,8},{8,0},{16,24},{24,16},{1,9},{9,1},{17,25},{25,17},{2,10},{10... | collective-permute-start | bytes 4423688 | tf_op jit(solution)/shard_map/ppermute | solution.py:1418
  381.9 15.1 %collective-permute-start.36 = (bf16[256,1024]{1,0:T(8,128)(2,1)}, bf16[256,1024]{1,0:T(8,128)(2,1)S(1)}, u32[]{:S(2)}, u32[]{:S(2)}) collective-permute-start(bf16[256,1024]{1,0:T(8,128)(2,1)} %get-tuple-element.137), channel_id=1, source_target_pairs={{0,16},{8,24},{16,0},{24,8},{1,17},{9,25},{17,1},{25,9},{2,18},{10... | collective-permute-start | bytes 1572872 | tf_op jit(solution)/shard_map/ppermute | solution.py:1418
  383.4 15.2 %collective-permute-start.39 = (bf16[256,1024]{1,0:T(8,128)(2,1)}, bf16[256,1024]{1,0:T(8,128)(2,1)S(1)}, u32[]{:S(2)}, u32[]{:S(2)}) collective-permute-start(bf16[256,1024]{1,0:T(8,128)(2,1)} %get-tuple-element.142), channel_id=1, source_target_pairs={{0,4},{4,0},{1,5},{5,1},{2,6},{6,2},{3,7},{7,3},{8,12},{12,8},{9,1... | collective-permute-start | bytes 1572872 | tf_op jit(solution)/shard_map/ppermute | solution.py:1418
  384.2 25.3 %collective-permute-start.43 = (bf16[256,1152]{1,0:T(8,128)(2,1)}, bf16[256,1152]{1,0:T(8,128)(2,1)S(1)}, u32[]{:S(2)}, u32[]{:S(2)}) collective-permute-start(bf16[256,1152]{1,0:T(8,128)(2,1)} %get-tuple-element.148), channel_id=1, source_target_pairs={{0,16},{8,24},{16,0},{24,8},{1,17},{9,25},{17,1},{25,9},{2,18},{10... | collective-permute-start | bytes 1769480 | tf_op jit(solution)/shard_map/ppermute | solution.py:1418
  390.3 58.2 %collective-permute-start.42 = (bf16[256,1152]{1,0:T(8,128)(2,1)S(1)}, bf16[256,1152]{1,0:T(8,128)(2,1)S(1)}, u32[]{:S(2)}, u32[]{:S(2)}) collective-permute-start(bf16[256,1152]{1,0:T(8,128)(2,1)S(1)} %copy-done.26), channel_id=1, source_target_pairs={{0,16},{8,24},{16,0},{24,8},{1,17},{9,25},{17,1},{25,9},{2,18},{10... | collective-permute-start | bytes 1769480 | tf_op jit(solution)/shard_map/ppermute | solution.py:1418
  391.8 31.2 %collective-permute-start.38 = (bf16[256,1024]{1,0:T(8,128)(2,1)}, bf16[256,1024]{1,0:T(8,128)(2,1)S(1)}, u32[]{:S(2)}, u32[]{:S(2)}) collective-permute-start(bf16[256,1024]{1,0:T(8,128)(2,1)} %get-tuple-element.140), channel_id=1, source_target_pairs={{0,4},{4,0},{1,5},{5,1},{2,6},{6,2},{3,7},{7,3},{8,12},{12,8},{9,1... | collective-permute-start | bytes 1572872 | tf_op jit(solution)/shard_map/ppermute | solution.py:1418
  397.0 13.2 %copy-start.25 = (bf16[256,1152]{1,0:T(8,128)(2,1)S(1)}, bf16[256,1152]{1,0:T(8,128)(2,1)}, u32[]{:S(2)}) copy-start(bf16[256,1152]{1,0:T(8,128)(2,1)} %get-tuple-element.147) | copy-start | bytes 1769476
  397.0 36.3 %collective-permute-start.35 = (bf16[256,1024]{1,0:T(8,128)(2,1)S(1)}, bf16[256,1024]{1,0:T(8,128)(2,1)S(1)}, u32[]{:S(2)}, u32[]{:S(2)}) collective-permute-start(bf16[256,1024]{1,0:T(8,128)(2,1)S(1)} %copy-done.28), channel_id=1, source_target_pairs={{0,16},{8,24},{16,0},{24,8},{1,17},{9,25},{17,1},{25,9},{2,18},{10... | collective-permute-start | bytes 1572872 | tf_op jit(solution)/shard_map/ppermute | solution.py:1418
  398.5 24.3 %copy-start.24 = (bf16[256,1152]{1,0:T(8,128)(2,1)S(1)}, bf16[256,1152]{1,0:T(8,128)(2,1)}, u32[]{:S(2)}) copy-start(bf16[256,1152]{1,0:T(8,128)(2,1)} %get-tuple-element.151) | copy-start | bytes 1769476
  398.6 23.7 %collective-permute-start.46 = (bf16[256,1152]{1,0:T(8,128)(2,1)S(1)}, bf16[256,1152]{1,0:T(8,128)(2,1)S(1)}, u32[]{:S(2)}, u32[]{:S(2)}) collective-permute-start(bf16[256,1152]{1,0:T(8,128)(2,1)S(1)} %copy-done.53), channel_id=1, source_target_pairs={{0,4},{4,0},{1,5},{5,1},{2,6},{6,2},{3,7},{7,3},{8,12},{12,8},{9,1... | collective-permute-start | bytes 1769480 | tf_op jit(solution)/shard_map/ppermute | solution.py:1418
  399.6 23.4 %copy-start.52 = (bf16[256,1152]{1,0:T(8,128)(2,1)S(1)}, bf16[256,1152]{1,0:T(8,128)(2,1)}, u32[]{:S(2)}) copy-start(bf16[256,1152]{1,0:T(8,128)(2,1)} %get-tuple-element.150) | copy-start | bytes 1769476
  399.6 45.9 %copy-start.9 = (f32[256,1024]{1,0:T(8,128)S(1)}, f32[256,1024]{1,0:T(8,128)}, u32[]{:S(2)}) copy-start(f32[256,1024]{1,0:T(8,128)} %get-tuple-element.138.refs_18_) | copy-start | bytes 3145732
  399.6 45.9 %copy-start.36 = (bf16[256,1024]{1,0:T(8,128)(2,1)S(1)}, bf16[256,1024]{1,0:T(8,128)(2,1)}, u32[]{:S(2)}) copy-start(bf16[256,1024]{1,0:T(8,128)(2,1)} %get-tuple-element.139) | copy-start | bytes 1572868
  409.5 36.4 %collective-permute-start.37 = (bf16[256,1024]{1,0:T(8,128)(2,1)S(1)}, bf16[256,1024]{1,0:T(8,128)(2,1)S(1)}, u32[]{:S(2)}, u32[]{:S(2)}) collective-permute-start(bf16[256,1024]{1,0:T(8,128)(2,1)S(1)} %add_convert_fusion.5), channel_id=1, source_target_pairs={{0,4},{4,0},{1,5},{5,1},{2,6},{6,2},{3,7},{7,3},{8,12},{12,8},{9,1... | collective-permute-start | bytes 1572872 | tf_op jit(solution)/shard_map/ppermute | solution.py:1418
  422.2 21.8 %collective-permute-start.40 = (bf16[256,1024]{1,0:T(8,128)(2,1)S(1)}, bf16[256,1024]{1,0:T(8,128)(2,1)S(1)}, u32[]{:S(2)}, u32[]{:S(2)}) collective-permute-start(bf16[256,1024]{1,0:T(8,128)(2,1)S(1)} %add_convert_fusion.3), channel_id=1, source_target_pairs={{0,16},{8,24},{16,0},{24,8},{1,17},{9,25},{17,1},{25,9},{2,18},{10... | collective-permute-start | bytes 1572872 | tf_op jit(solution)/shard_map/ppermute | solution.py:1418
  423.0 22.9 %copy-start.8 = (f32[256,1024]{1,0:T(8,128)S(1)}, f32[256,1024]{1,0:T(8,128)}, u32[]{:S(2)}) copy-start(f32[256,1024]{1,0:T(8,128)} %get-tuple-element.97.refs_12_) | copy-start | bytes 3145732
  423.0 22.9 %copy-start.16 = (bf16[256,1024]{1,0:T(8,128)(2,1)S(1)}, bf16[256,1024]{1,0:T(8,128)(2,1)}, u32[]{:S(2)}) copy-start(bf16[256,1024]{1,0:T(8,128)(2,1)} %get-tuple-element.130.refs_20_) | copy-start | bytes 1572868
  423.0 25.4 %collective-permute-start.45 = (bf16[256,1152]{1,0:T(8,128)(2,1)S(1)}, bf16[256,1152]{1,0:T(8,128)(2,1)S(1)}, u32[]{:S(2)}, u32[]{:S(2)}) collective-permute-start(bf16[256,1152]{1,0:T(8,128)(2,1)S(1)} %copy-done.52), channel_id=1, source_target_pairs={{0,4},{4,0},{1,5},{5,1},{2,6},{6,2},{3,7},{7,3},{8,12},{12,8},{9,1... | collective-permute-start | bytes 1769480 | tf_op jit(solution)/shard_map/ppermute | solution.py:1418
  433.4 24.5 %collective-permute-start.44 = (bf16[256,1152]{1,0:T(8,128)(2,1)S(1)}, bf16[256,1152]{1,0:T(8,128)(2,1)S(1)}, u32[]{:S(2)}, u32[]{:S(2)}) collective-permute-start(bf16[256,1152]{1,0:T(8,128)(2,1)S(1)} %add_convert_fusion.1), channel_id=1, source_target_pairs={{0,4},{4,0},{1,5},{5,1},{2,6},{6,2},{3,7},{7,3},{8,12},{12,8},{9,1... | collective-permute-start | bytes 1769480 | tf_op jit(solution)/shard_map/ppermute | solution.py:1418
  444.0 14.9 %collective-permute-start.47 = (bf16[256,1152]{1,0:T(8,128)(2,1)S(1)}, bf16[256,1152]{1,0:T(8,128)(2,1)S(1)}, u32[]{:S(2)}, u32[]{:S(2)}) collective-permute-start(bf16[256,1152]{1,0:T(8,128)(2,1)S(1)} %add_convert_fusion), channel_id=1, source_target_pairs={{0,16},{8,24},{16,0},{24,8},{1,17},{9,25},{17,1},{25,9},{2,18},{10... | collective-permute-start | bytes 1769480 | tf_op jit(solution)/shard_map/ppermute | solution.py:1418
  515.8 48.5 %copy-start.45 = (f32[4,1,1280]{2,1,0:T(1,128)S(1)}, f32[4,1,1280]{2,1,0:T(1,128)}, u32[]{:S(2)}) copy-start(f32[4,1,1280]{2,1,0:T(1,128)} %get-tuple-element.170) | copy-start | bytes 61444
  515.8 50.2 %copy-start.49 = (s32[1024]{0:T(1024)S(1)}, s32[1024]{0:T(1024)}, u32[]{:S(2)}) copy-start(s32[1024]{0:T(1024)} %param.18) | copy-start | bytes 12292
  515.8 50.5 %copy-start.55 = (s32[4]{0:T(128)S(1)}, s32[4]{0:T(128)}, u32[]{:S(2)}) copy-start(s32[4]{0:T(128)} %copy-done.54) | copy-start | bytes 52
  (42 other events, 197.2 us)
Sparse Core Ops, SparseCore 0:
  295.1 77.4 reduce-scatter.2
  374.9 79.3 reduce-scatter.4
